TPU v7x, 32 devices: a whole 2x2x4 slice. The times are simulated.
32 devices in a mesh: tok: 4 (over y, x), tp: 8 (over z, core).
Axes of the slice: x: 2, y: 2, z: 4, core: 2. Of those that a mesh axis runs over, the one named last changes fastest.
Arguments:
- source: bfloat16 [1024, 8192], P('tp', 'tok'), may hold values from -6 to 6
- row_token: int32 [1024], replicated, may hold values from 0 to 1023, each once
- seg_ids: int32 [4, 256], P('tok'), may hold values from 0 to 3, never falling along the last dimension, each value on 1 to 128 neighbouring positions
- stitch_weight: bfloat16 [8192, 8192], P('tok', 'tp'), may hold values from -0.0625 to 0.0625
- norm_gain: float32 [8192], replicated, may hold values from 0.5 to 1.5
- q_weight: bfloat16 [8192, 8192], P(None, 'tp'), may hold values from -2 to 2
- kv_weight: bfloat16 [8192, 2048], P(None, 'tp'), may hold values from -2 to 2
- o_weight: bfloat16 [8192, 8192], P('tp'), may hold values from -0.0625 to 0.0625
- out_grad: bfloat16 [1024, 8192], P('tok', 'tp'), may hold values from -6 to 6
Outputs:
- layer_out: bfloat16 [1024, 8192], P('tok', 'tp')
- stitch_grad: float32 [8192, 8192], P('tok', 'tp')
Inputs may be any that keep to these rules, and one draw needn't show every extreme that they name: `row_token`: each token index appears exactly once. `seg_ids`: within a pack the ids never fall; a document holds 1 to 128 tokens.
All inputs are finite; a program needn't handle non-finite values.
Results may differ from a plain program's by a relative error of at most 0.024.
Values may be sent and summed in bfloat16 or wider, within the bound.
No kernel may reach another device: no remote copies, remote signals or barrier semaphores. Data moves between devices by JAX's collectives and lax.ppermute only.
A program may use at most 128 MiB of HBM per device.

v0:
```python
import math

import jax
import jax.numpy as jnp
from jax import lax
from jax.sharding import PartitionSpec as P

HD = 128


epsilon = 1e-05


def swapped(value, axis, distance):
    mask = 2**distance
    pairs = [(source, source ^ mask) for source in range(lax.axis_size(axis))]
    return lax.ppermute(value, axis, pairs)


def frequencies():
    exponent = jnp.arange(0, HD, 2).astype(jnp.float32) / HD
    plain_rate = 500000.0 ** (-exponent)
    wavelength = 2.0 * math.pi / plain_rate
    smoothing = (8192.0 / wavelength - 1.0) / 3.0
    blended = (1.0 - smoothing) * plain_rate / 8.0 + smoothing * plain_rate
    return jnp.where(
        wavelength < 2048.0, plain_rate, jnp.where(wavelength > 8192.0, plain_rate / 8.0, blended)
    )


def rotate(vector_in, cosine_table, sine_table):
    half_size = vector_in.shape[-1] // 2
    first_half = vector_in[..., :half_size]
    second = vector_in[..., half_size:]
    return jnp.concatenate(
        [
            first_half * cosine_table - second * sine_table,
            second * cosine_table + first_half * sine_table,
        ],
        axis=-1,
    )


def unrotate(vector_in, cosine_table, sine_table):
    half_size = vector_in.shape[-1] // 2
    first_half = vector_in[..., :half_size]
    second = vector_in[..., half_size:]
    return jnp.concatenate(
        [
            first_half * cosine_table + second * sine_table,
            second * cosine_table - first_half * sine_table,
        ],
        axis=-1,
    )


def body(
    source, row_token, seg_ids, stitch_weight, norm_gain, q_weight, kv_weight, o_weight, out_grad
):
    tp_rank = lax.axis_index("tp")
    pack_len = seg_ids.shape[1]
    score_scale = 1.0 / math.sqrt(HD)
    gathered = lax.all_gather(source, "tp", axis=0, tiled=True)
    every_row_stack = gathered.shape[0]
    placing = (
        jnp.zeros((every_row_stack,), jnp.int32)
        .at[row_token]
        .set(jnp.arange(every_row_stack, dtype=jnp.int32))
    )
    column_block = jnp.take(gathered, placing, axis=0)
    token_rows = lax.all_to_all(column_block, "tok", split_axis=0, concat_axis=1, tiled=True)
    features = token_rows
    hidden_cols = jnp.dot(
        features,
        lax.all_gather(stitch_weight, "tok", axis=0, tiled=True),
        preferred_element_type=jnp.float32,
    )
    hidden_bf = hidden_cols.astype(jnp.bfloat16)
    hidden_all = lax.all_gather(hidden_bf, "tp", axis=1, tiled=True)
    hidden_f = hidden_all.astype(jnp.float32)
    inv_rms = lax.rsqrt(jnp.mean(hidden_f * hidden_f, axis=1, keepdims=True) + epsilon)
    normed = (hidden_f * inv_rms * norm_gain).astype(jnp.bfloat16)
    seg_row = seg_ids[0]
    earlier = jnp.sum((seg_row[None, :] < seg_row[:, None]).astype(jnp.int32), axis=1)
    index_row = jnp.arange(pack_len, dtype=jnp.int32)
    angles = (index_row - earlier).astype(jnp.float32)[:, None] * frequencies()[None, :]
    cosines = jnp.cos(angles)[:, None, :]
    sine_table = jnp.sin(angles)[:, None, :]
    allowed = (
        (seg_row[:, None] == seg_row[None, :]) & (index_row[None, :] <= index_row[:, None])
    ).astype(jnp.int32)
    local_heads = q_weight.shape[1] // HD
    kv_cols = kv_weight.shape[1]
    paired = kv_cols == HD
    kv_local = 1 if paired else kv_cols // (2 * HD)
    repeat = local_heads // kv_local
    queries = rotate(
        jnp.dot(normed, q_weight, preferred_element_type=jnp.float32).reshape(
            pack_len, local_heads, HD
        ),
        cosines,
        sine_table,
    ).astype(jnp.bfloat16)
    projected = jnp.dot(normed, kv_weight, preferred_element_type=jnp.float32)
    is_key = tp_rank % 2 == 0
    if paired:
        own_part = jnp.where(
            is_key, rotate(projected, cosines[:, 0], sine_table[:, 0]), projected
        ).astype(jnp.bfloat16)
        partner = swapped(own_part, "tp", 0)
        per_head_keys = jnp.where(is_key, own_part, partner)[:, None, :]
        per_head_values = jnp.where(is_key, partner, own_part)[:, None, :]
    else:
        halves = projected.reshape(pack_len, kv_local, 2, HD)
        per_head_keys = rotate(halves[:, :, 0], cosines, sine_table).astype(jnp.bfloat16)
        per_head_values = halves[:, :, 1].astype(jnp.bfloat16)
    per_head_queries = queries.reshape(pack_len, kv_local, repeat, HD)
    scores = (
        jnp.einsum(
            "nkej,wkj->kenw", per_head_queries, per_head_keys, preferred_element_type=jnp.float32
        )
        * score_scale
    )
    scores = jnp.where(allowed != 0, scores, -1e30)
    row_max = jnp.max(scores, axis=-1, keepdims=True)
    exponents = jnp.exp(scores - row_max)
    attention = exponents / jnp.sum(exponents, axis=-1, keepdims=True)
    attention_half_precision = attention.astype(jnp.bfloat16)
    context = jnp.einsum(
        "cnfo,och->fcnh",
        attention_half_precision,
        per_head_values,
        preferred_element_type=jnp.float32,
    ).astype(jnp.bfloat16)
    context = context.reshape(pack_len, local_heads * HD)
    attended = lax.psum_scatter(
        jnp.dot(context, o_weight, preferred_element_type=jnp.float32).astype(jnp.bfloat16),
        "tp",
        scatter_dimension=1,
        tiled=True,
    ).astype(jnp.float32)
    layer_out = (hidden_bf.astype(jnp.float32) + attended).astype(jnp.bfloat16)
    gradient_every_row = lax.all_gather(out_grad, "tp", axis=1, tiled=True)
    grad_context = jnp.dot(
        gradient_every_row, o_weight.T, preferred_element_type=jnp.float32
    ).astype(jnp.bfloat16)
    context_gradient = grad_context.reshape(pack_len, kv_local, repeat, HD)
    grad_probs = jnp.einsum(
        "nkej,wkj->kenw", context_gradient, per_head_values, preferred_element_type=jnp.float32
    )
    centered = grad_probs - jnp.sum(grad_probs * attention, axis=-1, keepdims=True)
    score_gradient = (attention * centered * score_scale).astype(jnp.bfloat16)
    query_grad = jnp.einsum(
        "cnfo,och->fcnh", score_gradient, per_head_keys, preferred_element_type=jnp.float32
    )
    grad_queries = unrotate(
        query_grad.reshape(pack_len, local_heads, HD), cosines, sine_table
    ).astype(jnp.bfloat16)
    key_part = jnp.einsum(
        "bwlf,lbwj->fbj", score_gradient, per_head_queries, preferred_element_type=jnp.float32
    )
    value_part = jnp.einsum(
        "bwlf,lbwj->fbj",
        attention_half_precision,
        context_gradient,
        preferred_element_type=jnp.float32,
    )
    if paired:
        outgoing = jnp.where(is_key, value_part, key_part)[:, 0]
        incoming = swapped(outgoing.astype(jnp.bfloat16), "tp", 0).astype(outgoing.dtype)
        own_sum = jnp.where(is_key, key_part, value_part)[:, 0] + incoming
        grad_pairs = jnp.where(
            is_key, unrotate(own_sum, cosines[:, 0], sine_table[:, 0]), own_sum
        ).astype(jnp.bfloat16)
    else:
        grad_keys = unrotate(key_part, cosines, sine_table).astype(jnp.bfloat16)
        grad_pairs = jnp.stack([grad_keys, value_part.astype(jnp.bfloat16)], axis=2).reshape(
            pack_len, kv_cols
        )
    grad_normed = jnp.dot(
        grad_queries.reshape(pack_len, local_heads * HD),
        q_weight.T,
        preferred_element_type=jnp.float32,
    )
    grad_normed = grad_normed + jnp.dot(grad_pairs, kv_weight.T, preferred_element_type=jnp.float32)
    weighted = norm_gain * grad_normed
    cubed = inv_rms * inv_rms * inv_rms
    norm_term = inv_rms * weighted - hidden_f * cubed * jnp.mean(
        weighted * hidden_f, axis=1, keepdims=True
    )
    grad_sum = lax.psum_scatter(
        norm_term.astype(jnp.bfloat16), "tp", scatter_dimension=1, tiled=True
    ).astype(jnp.float32)
    grad_hidden = (out_grad.astype(jnp.float32) + grad_sum).astype(jnp.bfloat16)
    features = token_rows
    stitch_grad = lax.psum_scatter(
        lax.dot_general(
            features, grad_hidden, (((0,), (0,)), ((), ())), preferred_element_type=jnp.float32
        ).astype(jnp.bfloat16),
        "tok",
        scatter_dimension=0,
        tiled=True,
    ).astype(jnp.float32)
    return (layer_out, stitch_grad)


def solution(mesh):
    placed = (
        P("tp", "tok"),
        P(),
        P("tok", None),
        P("tok", "tp"),
        P(),
        P(None, "tp"),
        P(None, "tp"),
        P("tp", None),
        P("tok", "tp"),
    )
    return jax.shard_map(
        body,
        mesh=mesh,
        in_specs=placed,
        out_specs=(P("tok", "tp"), P("tok", "tp")),
        check_vma=False,
    )
```

profile of v0, /device:TPU:0, one launch (start us, length us, event | category | flops | bytes accessed | tf_op | source)
XLA Modules:
  0.0 686.0 jit_solution(14851816572652181340)
XLA Ops:
  8.0 0.7 all-gather.7.cloned.1.call-update
  9.5 4.3 scatter_custom_fusion
  13.8 45.7 %all-gather.5.cloned.1.call-done = bf16[1024,2048]{1,0:T(8,128)(2,1)} async-done(((bf16[128,2048]{1,0:T(8,128)(2,1)}), bf16[1024,2048]{1,0:T(8,128)(2,1)}) %all-gather.5.cloned.1.call-update) | async-done | bytes 4194320 | tf_op jit(solution)/shard_map/all_gather | solution.py:63
  59.5 11.5 %gather_fusion = bf16[1024,2048]{1,0:T(8,128)(2,1)} fusion(bf16[1024,2048]{1,0:T(8,128)(2,1)} %all-gather.5.cloned.1.call-done, s32[1024]{0:T(1024)S(1)} %fusion.47), kind=kCustom, calls=%fused_computation | custom fusion | bytes 8392704 | tf_op jit(solution)/shard_map/jit(_take)/gather | solution.py:70
  71.0 6.7 copy.26
  77.7 2.6 broadcast_select_fusion
  80.3 84.4 %all_to_all.16 = bf16[4,256,2048]{1,2,0:T(8,128)(2,1)} all-to-all(bf16[4,256,2048]{1,2,0:T(8,128)(2,1)S(1)} %broadcast_select_fusion), channel_id=1, replica_groups=mesh['tok'=4,'tp'=8] {'tok'}, dimensions={0} | all-to-all | bytes 8388608 | tf_op jit(solution)/shard_map/all_to_all | solution.py:71
  164.7 97.7 %all-gather.7.cloned.1.call-done = bf16[8192,1024]{1,0:T(8,128)(2,1)} async-done(((bf16[2048,1024]{1,0:T(8,128)(2,1)}), bf16[8192,1024]{1,0:T(8,128)(2,1)}) %all-gather.7.cloned.1.call-update) | async-done | bytes 16777232 | tf_op jit(solution)/shard_map/all_gather | solution.py:75
  262.4 12.4 %convolution_convert_fusion.4 = bf16[256,1024]{1,0:T(8,128)(2,1)} fusion(bf16[256,8192]{0,1:T(8,128)(2,1)} %bitcast.116, bf16[8192,1024]{1,0:T(8,128)(2,1)} %all-gather.7.cloned.1.call-done), kind=kOutput, calls=%fused_computation.32 | convolution fusion | flops 4295229440 | bytes 21495808 | tf_op jit(solution)/shard_map/dot_general | solution.py:73
  275.6 0.7 convert_compare_fusion
  276.8 34.4 %all-gather.11.cloned.1.call-done = bf16[256,8192]{1,0:T(8,128)(2,1)} async-done(((bf16[256,1024]{1,0:T(8,128)(2,1)}), bf16[256,8192]{1,0:T(8,128)(2,1)}) %all-gather.11.cloned.1.call-update) | async-done | bytes 4194320 | tf_op jit(solution)/shard_map/all_gather | solution.py:143
  311.2 11.6 %convolution_convert_fusion.3 = bf16[256,1024]{1,0:T(8,128)(2,1)S(1)} fusion(bf16[256,8192]{1,0:T(8,128)(2,1)} %all-gather.11.cloned.1.call-done, bf16[1024,8192]{1,0:T(8,128)(2,1)} %param.16), kind=kOutput, calls=%fused_computation.31 | convolution fusion | flops 4295229440 | bytes 21495808 | tf_op jit(solution)/shard_map/dot_general | solution.py:144
  322.9 36.3 %all-gather.9.cloned.1.call-done = bf16[256,8192]{1,0:T(8,128)(2,1)} async-done(((bf16[256,1024]{1,0:T(8,128)(2,1)}), bf16[256,8192]{1,0:T(8,128)(2,1)}) %all-gather.9.cloned.1.call-update) | async-done | bytes 4194320 | tf_op jit(solution)/shard_map/all_gather | solution.py:79
  359.2 3.3 fusion.1
  362.6 8.4 %convolution_bitcast_fusion = f32[32,8,8,128]{3,1,2,0:T(8,128)S(1)} fusion(bf16[8192,1024]{1,0:T(8,128)(2,1)} %param.14, bf16[256,8192]{1,0:T(8,128)(2,1)S(1)} %copy-done, f32[8192]{0:T(1024)S(1)} %copy-done.8, f32[256]{0:T(256)S(1)} %get-tuple-element.17), kind=kOutput, calls=%fused_computation.28 | convolution fusion | flops 4303355904 | bytes 22053888 | tf_op jit(solution)/shard_map/dot_general | solution.py:98
  371.6 1.6 copy-done.3
  373.2 2.2 fusion.15
  376.8 1.0 copy.60
  378.8 1.5 fusion.54
  381.2 0.7 fusion.19
  384.1 19.3 %fusion.55 = f32[256,8192]{1,0:T(8,128)} fusion(bf16[256,1024]{0,1:T(8,128)(2,1)S(1)} %bitcast.121, bf16[8192,1024]{1,0:T(8,128)(2,1)} %param.14), kind=kOutput, calls=%fused_computation.100 | convolution fusion | flops 4294967296 | bytes 25690112 | tf_op jit(solution)/shard_map/dot_general | solution.py:180
  403.4 1.0 copy.53
  405.7 7.9 %fusion.7 = (f32[256]{0:T(256)S(1)}, f32[256,8192]{1,0:T(8,128)S(1)}) fusion(bf16[256,8192]{1,0:T(8,128)(2,1)} %all-gather.9.cloned.1.call-done, f32[256,8192]{1,0:T(8,128)} %fusion.55, bf16[256,256]{0,1:T(8,128)(2,1)S(1)} %bitcast.124, bf16[8192,256]{1,0:T(8,128)(2,1)} %param.15, f32[8192]{0:T(1024)S(1)} %copy-done.9), kind=kOutput, calls=%fused_computation.16 | convolution fusion | flops 1084227328 | bytes 25330688 | tf_op jit(solution)/shard_map/dot_general | solution.py:185
  413.7 3.6 fusion.6
  417.4 0.9 copy-done.7
  418.6 12.5 %convolution_convert_fusion.1 = bf16[256,8192]{1,0:T(8,128)(2,1)} fusion(bf16[256,1024]{0,1:T(8,128)(2,1)S(1)} %bitcast.122, bf16[1024,8192]{1,0:T(8,128)(2,1)} %param.16), kind=kOutput, calls=%fused_computation.9 | convolution fusion | flops 4297064448 | bytes 21495808 | tf_op jit(solution)/shard_map/dot_general | solution.py:137
  431.4 34.8 %reduce-scatter.6.cloned.1.call-done = bf16[256,1024]{1,0:T(8,128)(2,1)} async-done(((bf16[256,8192]{1,0:T(8,128)(2,1)}), bf16[256,1024]{1,0:T(8,128)(2,1)}) %reduce-scatter.6.cloned.1.call-update) | async-done | bytes 524304 | tf_op jit(solution)/shard_map/reduce_scatter | solution.py:191
  466.2 12.6 %convolution_convert_fusion = bf16[8192,1024]{1,0:T(8,128)(2,1)} fusion(bf16[256,8192]{0,1:T(8,128)(2,1)} %bitcast.117, bf16[256,1024]{1,0:T(8,128)(2,1)} %reduce-scatter.6.cloned.1.call-done, bf16[256,1024]{1,0:T(8,128)(2,1)S(1)} %copy-done.4), kind=kOutput, calls=%fused_computation.2 | convolution fusion | flops 4304404480 | bytes 22020096 | tf_op jit(solution)/shard_map/dot_general | solution.py:197
  478.9 38.3 %reduce-scatter.4.cloned.1.call-done = bf16[256,1024]{1,0:T(8,128)(2,1)} async-done(((bf16[256,8192]{1,0:T(8,128)(2,1)}), bf16[256,1024]{1,0:T(8,128)(2,1)}) %reduce-scatter.4.cloned.1.call-update) | async-done | bytes 524304 | tf_op jit(solution)/shard_map/reduce_scatter | solution.py:136
  517.1 2.0 add_convert_fusion.2
  519.2 153.1 %reduce-scatter.8.cloned.1.call-done = bf16[2048,1024]{1,0:T(8,128)(2,1)} async-done(((bf16[8192,1024]{1,0:T(8,128)(2,1)}), bf16[2048,1024]{1,0:T(8,128)(2,1)}) %reduce-scatter.8.cloned.1.call-update) | async-done | bytes 4194320 | tf_op jit(solution)/shard_map/reduce_scatter | solution.py:196
  672.2 6.6 convert_element_type.148
  (64 shorter events, 11.0 us)
Async XLA Ops:
  7.2 2.3 copy-start.11
  7.2 52.3 %all-gather.5.cloned.1.call-start = ((), (), s32[]{:S(2)}) async-start(), calls=%async_computation.4 | async-start | bytes 4718592 | tf_op jit(solution)/shard_map/all_gather | solution.py:63
  7.9 254.5 %all-gather.7.cloned.1.call-start = ((), (), s32[]{:S(2)}) async-start(), calls=%async_computation.5 | async-start | bytes 20971520 | tf_op jit(solution)/shard_map/all_gather | solution.py:75
  8.7 302.6 %all-gather.11.cloned.1.call-start = ((), (), s32[]{:S(2)}) async-start(), calls=%async_computation.8 | async-start | bytes 4718592 | tf_op jit(solution)/shard_map/all_gather | solution.py:143
  9.4 349.8 %all-gather.9.cloned.1.call-start = ((), (), s32[]{:S(2)}) async-start(), calls=%async_computation.6 | async-start | bytes 4718592 | tf_op jit(solution)/shard_map/all_gather | solution.py:79
  262.4 13.0 %copy-start.10 = (s32[1,256]{1,0:T(1,128)S(1)}, s32[1,256]{1,0:T(1,128)}, u32[]{:S(2)}) copy-start(s32[1,256]{1,0:T(1,128)} %param.11) | copy-start | bytes 3076
  274.8 191.4 %reduce-scatter.6.cloned.1.call-start = ((), (), s32[]{:S(2)}) async-start(), calls=%async_computation.9 | async-start | bytes 4718592 | tf_op jit(solution)/shard_map/reduce_scatter | solution.py:191
  322.8 39.6 %copy-start.8 = (f32[8192]{0:T(1024)S(1)}, f32[8192]{0:T(1024)}, u32[]{:S(2)}) copy-start(f32[8192]{0:T(1024)} %param.13) | copy-start | bytes 98308
  359.2 3.4 copy-start
  371.1 2.2 copy-start.3
  375.4 0.7 copy-start.5
  378.4 2.3 copy-start.6
  403.4 2.4 copy-start.9
  405.7 8.0 %copy-start.1 = (bf16[256,8192]{1,0:T(8,128)(2,1)S(1)}, bf16[256,8192]{1,0:T(8,128)(2,1)}, u32[]{:S(2)}) copy-start(bf16[256,8192]{1,0:T(8,128)(2,1)} %all-gather.9.cloned.1.call-done) | copy-start | bytes 12582916
  417.3 0.9 copy-start.7
  417.4 99.8 %reduce-scatter.4.cloned.1.call-start = ((), (), s32[]{:S(2)}) async-start(), calls=%async_computation.7 | async-start | bytes 4718592 | tf_op jit(solution)/shard_map/reduce_scatter | solution.py:136
  431.1 35.2 %copy-start.4 = (bf16[256,1024]{1,0:T(8,128)(2,1)S(1)}, bf16[256,1024]{1,0:T(8,128)(2,1)}, u32[]{:S(2)}) copy-start(bf16[256,1024]{1,0:T(8,128)(2,1)} %param.17) | copy-start | bytes 1572868
  431.1 241.1 %reduce-scatter.8.cloned.1.call-start = ((), (), s32[]{:S(2)}) async-start(), calls=%async_computation.10 | async-start | bytes 20971520 | tf_op jit(solution)/shard_map/reduce_scatter | solution.py:196
  478.8 38.3 %copy-start.2 = (bf16[256,1024]{1,0:T(8,128)(2,1)S(1)}, bf16[256,1024]{1,0:T(8,128)(2,1)}, u32[]{:S(2)}) copy-start(bf16[256,1024]{1,0:T(8,128)(2,1)} %convolution_convert_fusion.4) | copy-start | bytes 1572868
Sparse Core Ops, SparseCore 0:
  9.6 49.8 all-gather.4
  61.3 201.0 all-gather.6
  264.0 47.1 all-gather.10
  313.3 45.8 all-gather.8
  417.5 48.7 reduce-scatter.5
  469.0 48.1 reduce-scatter.3
  520.2 151.9 reduce-scatter.7
where the time goes:
time: 692 us; the launch traced here: 686 us
  waiting for transfers between devices  442 us (64%)
  matrix products  91 us (13%)
  blocking collectives  84.4 us (12%)
  local copies, waits for them, and re-layouts  29.6 us (4%)
  other arithmetic  22.9 us (3%)
  between operations  14.7 us (2%)
    reduce_scatter x1, waiting for transfers between devices, body(): lax.psum_scatter(lax.dot_general(features, grad_hidden, (((0,), (0,)), ((...  153 us
    all_gather x1, waiting for transfers between devices, body(): lax.all_gather(stitch_weight, 'tok', axis=0, tiled=True)  97.7 us
    all_to_all x1, blocking collectives, body(): lax.all_to_all(column_block, 'tok', split_axis=0, concat_axis=1, tiled=True)  84.4 us
    all_gather x1, waiting for transfers between devices, body(): gathered = lax.all_gather(source, 'tp', axis=0, tiled=True)  45.7 us
    reduce_scatter x1, waiting for transfers between devices, body(): lax.psum_scatter(jnp.dot(context, o_weight, preferred_element_type=jnp.fl...  38.3 us
    all_gather x1, waiting for transfers between devices, body(): hidden_all = lax.all_gather(hidden_bf, 'tp', axis=1, tiled=True)  36.3 us
    reduce_scatter x1, waiting for transfers between devices, body(): lax.psum_scatter(norm_term.astype(jnp.bfloat16), 'tp', scatter_dimension=...  34.8 us
    all_gather x1, waiting for transfers between devices, body(): gradient_every_row = lax.all_gather(out_grad, 'tp', axis=1, tiled=True)  34.4 us
  transfers between devices with their start and end apart: 7, of which 7 were waited for; matrix products, arithmetic and copies ran while one was open for 11% of the time, Pallas kernels for 0%

commit v1 on v0

v1 whole, which is shorter than its diff:
```python
import math

import jax
import jax.numpy as jnp
from jax import lax
from jax.sharding import PartitionSpec as P

HD = 128


epsilon = 1e-05


def swapped(value, axis, mask):
    pairs = [(source, source ^ mask) for source in range(lax.axis_size(axis))]
    return lax.ppermute(value, axis, pairs)


def summed(value, axis):
    mask = 1
    while mask < lax.axis_size(axis):
        value = value + swapped(value, axis, mask)
        mask *= 2
    return value


def frequencies():
    exponent = jnp.arange(0, HD, 2).astype(jnp.float32) / HD
    plain_rate = 500000.0 ** (-exponent)
    wavelength = 2.0 * math.pi / plain_rate
    smoothing = (8192.0 / wavelength - 1.0) / 3.0
    blended = (1.0 - smoothing) * plain_rate / 8.0 + smoothing * plain_rate
    return jnp.where(
        wavelength < 2048.0, plain_rate, jnp.where(wavelength > 8192.0, plain_rate / 8.0, blended)
    )


def rotate(vector_in, cosine_table, sine_table):
    half_size = vector_in.shape[-1] // 2
    first_half = vector_in[..., :half_size]
    second = vector_in[..., half_size:]
    return jnp.concatenate(
        [
            first_half * cosine_table - second * sine_table,
            second * cosine_table + first_half * sine_table,
        ],
        axis=-1,
    )


def unrotate(vector_in, cosine_table, sine_table):
    return rotate(vector_in, cosine_table, -sine_table)


def body(
    source, row_token, seg_ids, stitch_weight, norm_gain, q_weight, kv_weight, o_weight, out_grad
):
    tok_rank = lax.axis_index("tok")
    tp_rank = lax.axis_index("tp")
    packs = lax.axis_size("tok")
    pack_len = seg_ids.shape[1]
    width = q_weight.shape[0]
    own_cols = stitch_weight.shape[1]
    score_scale = 1.0 / math.sqrt(HD)
    own_gain = lax.dynamic_slice_in_dim(norm_gain, tp_rank * own_cols, own_cols)

    gathered = lax.all_gather(source, "tp", axis=0, tiled=True)
    partial = jnp.dot(gathered, stitch_weight, preferred_element_type=jnp.float32).astype(
        jnp.bfloat16
    )
    within = jnp.arange(pack_len, dtype=jnp.int32)
    hidden = None
    for distance in range(packs):
        pack = tok_rank ^ distance
        rows = (row_token[None, :] == (pack * pack_len + within)[:, None]).astype(jnp.bfloat16)
        placed = jnp.dot(rows, partial, preferred_element_type=jnp.float32)
        if distance:
            placed = swapped(placed.astype(jnp.bfloat16), "tok", distance).astype(jnp.float32)
        hidden = placed if hidden is None else hidden + placed
    hidden_bf = hidden.astype(jnp.bfloat16)
    hidden_f = hidden_bf.astype(jnp.float32)
    square_sum = summed(jnp.sum(hidden_f * hidden_f, axis=1), "tp")
    inv_rms = lax.rsqrt(square_sum / width + epsilon)[:, None]
    gained = lax.all_gather((hidden_f * own_gain).astype(jnp.bfloat16), "tp", axis=1, tiled=True)

    order = (row_token[:, None] == jnp.arange(row_token.shape[0], dtype=jnp.int32)[None, :]).astype(
        jnp.bfloat16
    )
    tokens_last = lax.dot_general(
        gathered, order, (((0,), (0,)), ((), ())), preferred_element_type=jnp.float32
    ).astype(jnp.bfloat16)

    seg_row = seg_ids[0]
    earlier = jnp.sum((seg_row[None, :] < seg_row[:, None]).astype(jnp.int32), axis=1)
    angles = (within - earlier).astype(jnp.float32)[:, None] * frequencies()[None, :]
    cosines = jnp.cos(angles)[:, None, :]
    sine_table = jnp.sin(angles)[:, None, :]
    allowed = (seg_row[:, None] == seg_row[None, :]) & (within[None, :] <= within[:, None])
    local_heads = q_weight.shape[1] // HD
    kv_cols = kv_weight.shape[1]
    paired = kv_cols == HD
    kv_local = 1 if paired else kv_cols // (2 * HD)
    repeat = local_heads // kv_local
    query_pre = (
        jnp.dot(gained, q_weight, preferred_element_type=jnp.float32) * inv_rms
    ).reshape(pack_len, local_heads, HD)
    queries = rotate(query_pre, cosines, sine_table).astype(jnp.bfloat16)
    projected = jnp.dot(gained, kv_weight, preferred_element_type=jnp.float32) * inv_rms
    is_key = tp_rank % 2 == 0
    if paired:
        own_part = jnp.where(
            is_key, rotate(projected, cosines[:, 0], sine_table[:, 0]), projected
        ).astype(jnp.bfloat16)
        partner = swapped(own_part, "tp", 1)
        per_head_keys = jnp.where(is_key, own_part, partner)[:, None, :]
        per_head_values = jnp.where(is_key, partner, own_part)[:, None, :]
    else:
        halves = projected.reshape(pack_len, kv_local, 2, HD)
        per_head_keys = rotate(halves[:, :, 0], cosines, sine_table).astype(jnp.bfloat16)
        per_head_values = halves[:, :, 1].astype(jnp.bfloat16)
    per_head_queries = queries.reshape(pack_len, kv_local, repeat, HD)
    scores = (
        jnp.einsum(
            "nkej,wkj->kenw", per_head_queries, per_head_keys, preferred_element_type=jnp.float32
        )
        * score_scale
    )
    scores = jnp.where(allowed, scores, -1e30)
    row_max = jnp.max(scores, axis=-1, keepdims=True)
    exponents = jnp.exp(scores - row_max)
    attention = exponents / jnp.sum(exponents, axis=-1, keepdims=True)
    attention_half_precision = attention.astype(jnp.bfloat16)
    context = jnp.einsum(
        "cnfo,och->fcnh",
        attention_half_precision,
        per_head_values,
        preferred_element_type=jnp.float32,
    ).astype(jnp.bfloat16)
    context = context.reshape(pack_len, local_heads * HD)
    attended = lax.psum_scatter(
        jnp.dot(context, o_weight, preferred_element_type=jnp.float32).astype(jnp.bfloat16),
        "tp",
        scatter_dimension=1,
        tiled=True,
    ).astype(jnp.float32)
    layer_out = (hidden_f + attended).astype(jnp.bfloat16)

    every_grad = lax.all_gather(out_grad, "tp", axis=1, tiled=True)
    grad_context = lax.dot_general(
        every_grad, o_weight, (((1,), (1,)), ((), ())), preferred_element_type=jnp.float32
    ).astype(jnp.bfloat16)
    context_gradient = grad_context.reshape(pack_len, kv_local, repeat, HD)
    grad_probs = jnp.einsum(
        "nkej,wkj->kenw", context_gradient, per_head_values, preferred_element_type=jnp.float32
    )
    centered = grad_probs - jnp.sum(grad_probs * attention, axis=-1, keepdims=True)
    score_gradient = (attention * centered * score_scale).astype(jnp.bfloat16)
    query_grad = jnp.einsum(
        "cnfo,och->fcnh", score_gradient, per_head_keys, preferred_element_type=jnp.float32
    )
    grad_queries = unrotate(
        query_grad.reshape(pack_len, local_heads, HD), cosines, sine_table
    ).astype(jnp.bfloat16)
    key_part = jnp.einsum(
        "bwlf,lbwj->fbj", score_gradient, per_head_queries, preferred_element_type=jnp.float32
    )
    value_part = jnp.einsum(
        "bwlf,lbwj->fbj",
        attention_half_precision,
        context_gradient,
        preferred_element_type=jnp.float32,
    )
    if paired:
        outgoing = jnp.where(is_key, value_part, key_part)[:, 0]
        incoming = swapped(outgoing.astype(jnp.bfloat16), "tp", 1).astype(outgoing.dtype)
        own_sum = jnp.where(is_key, key_part, value_part)[:, 0] + incoming
        grad_pairs = jnp.where(
            is_key, unrotate(own_sum, cosines[:, 0], sine_table[:, 0]), own_sum
        ).astype(jnp.bfloat16)
    else:
        grad_keys = unrotate(key_part, cosines, sine_table).astype(jnp.bfloat16)
        grad_pairs = jnp.stack([grad_keys, value_part.astype(jnp.bfloat16)], axis=2).reshape(
            pack_len, kv_cols
        )
    aligned = jnp.sum(grad_queries.astype(jnp.float32) * query_pre, axis=(1, 2)) + jnp.sum(
        grad_pairs.astype(jnp.float32) * projected, axis=1
    )
    aligned = summed(aligned, "tp")[:, None]
    grad_normed = lax.dot_general(
        grad_queries.reshape(pack_len, local_heads * HD),
        q_weight,
        (((1,), (1,)), ((), ())),
        preferred_element_type=jnp.float32,
    ) + lax.dot_general(
        grad_pairs, kv_weight, (((1,), (1,)), ((), ())), preferred_element_type=jnp.float32
    )
    grad_sum = lax.psum_scatter(
        grad_normed.astype(jnp.bfloat16), "tp", scatter_dimension=1, tiled=True
    ).astype(jnp.float32)
    grad_hidden = (
        out_grad.astype(jnp.float32)
        + inv_rms * own_gain * grad_sum
        - hidden_f * (inv_rms * inv_rms * aligned / width)
    ).astype(jnp.bfloat16)
    every_pack = lax.all_gather(grad_hidden, "tok", axis=0, tiled=True)
    stitch_grad = jnp.dot(tokens_last, every_pack, preferred_element_type=jnp.float32)
    return (layer_out, stitch_grad)


def solution(mesh):
    placed = (
        P("tp", "tok"),
        P(),
        P("tok", None),
        P("tok", "tp"),
        P(),
        P(None, "tp"),
        P(None, "tp"),
        P("tp", None),
        P("tok", "tp"),
    )
    return jax.shard_map(
        body,
        mesh=mesh,
        in_specs=placed,
        out_specs=(P("tok", "tp"), P("tok", "tp")),
        check_vma=False,
    )
```

time: 692 us -> 340 us (0.49)
  waiting for transfers between devices: 442 us -> 210 us
  blocking collectives: 84.4 us -> 0 us
  local copies, waits for them, and re-layouts: 29.6 us -> 9 us
  other arithmetic: 22.9 us -> 7.88 us
    reduce_scatter x2 -> x1, waiting for transfers between devices: 188 us -> 50.3 us  [body(): lax.psum_scatter(grad_normed.astype(jnp.bfloat16), 'tp', scatter_dimensio...]
    all_gather x3, waiting for transfers between devices: 168 us -> 70.9 us  [the longest x1 36.5 us: body(): lax.all_gather((hidden_f * own_gain).astype(jnp.bfloat16), 'tp', axis=1,...]
    all_to_all x1 -> x0, blocking collectives: 84.4 us -> none  [body(): lax.all_to_all(column_block, 'tok', split_axis=0, concat_axis=1, tiled=True)]
    reduce_scatter x1, waiting for transfers between devices: 38.3 us -> 1.71 us  [body(): lax.psum_scatter(jnp.dot(context, o_weight, preferred_element_type=jnp.fl...]
    ppermute x0 -> x9, waiting for transfers between devices: none -> 34.4 us  [swapped(): return lax.ppermute(value, axis, pairs)]
    gather x2 -> x0, local copies, waits for them, and re-layouts: 18.2 us -> none  [body(): column_block = jnp.take(gathered, placing, axis=0)]
    convert_element_type x4 -> x2, other arithmetic: 12.3 us -> 2.76 us  [the longest x1 2.75 us: body(): grad_hidden = (out_grad.astype(jnp.float32) + inv_rms * own_gain * grad_s...]
    dot_general x7 -> x11, matrix products: 74.4 us -> 81.1 us  [the longest x1 19.3 us: body(): lax.dot_general(grad_queries.reshape(pack_len, local_heads * HD), q_weigh...]
  transfers between devices with their start and end apart: 7 -> 15, of which waited for: 7 -> 12; matrix products, arithmetic and copies ran while one was open for 11% -> 19% of each run, Pallas kernels for 0% -> 0%
where the time goes in v1:
time: 340 us
  waiting for transfers between devices  210 us (62%)
  matrix products  92.5 us (27%)
  between operations  14.6 us (4%)
  local copies, waits for them, and re-layouts  9 us (3%)
  other arithmetic  7.88 us (2%)
  starting transfers between devices  6.08 us (2%)
    all_gather x1, waiting for transfers between devices, body(): gathered = lax.all_gather(source, 'tp', axis=0, tiled=True)  50.7 us
    reduce_scatter x1, waiting for transfers between devices, body(): lax.psum_scatter(grad_normed.astype(jnp.bfloat16), 'tp', scatter_dimensio...  50.3 us
    all_gather x1, waiting for transfers between devices, body(): lax.all_gather((hidden_f * own_gain).astype(jnp.bfloat16), 'tp', axis=1,...  36.5 us
    ppermute x9, waiting for transfers between devices, swapped(): return lax.ppermute(value, axis, pairs)  34.4 us
    all_gather x1, waiting for transfers between devices, body(): every_pack = lax.all_gather(grad_hidden, 'tok', axis=0, tiled=True)  33.6 us
    dot_general x1, matrix products, body(): lax.dot_general(grad_queries.reshape(pack_len, local_heads * HD), q_weigh...  19.3 us
    dot_general x1, matrix products, body(): jnp.dot(tokens_last, every_pack, preferred_element_type=jnp.float32)  13.6 us
    dot_general x1, matrix products, body(): lax.dot_general(every_grad, o_weight, (((1,), (1,)), ((), ())), preferred...  11.6 us
  transfers between devices with their start and end apart: 15, of which 12 were waited for; matrix products, arithmetic and copies ran while one was open for 19% of the time, Pallas kernels for 0%

profile of v1, /device:TPU:0, one launch (start us, length us, event | category | flops | bytes accessed | tf_op | source)
XLA Modules:
  0.0 339.6 jit_solution(1355695698567680489)
XLA Ops:
  8.8 50.7 %all-gather.5.cloned.1.call-done = bf16[1024,2048]{1,0:T(8,128)(2,1)} async-done(((bf16[128,2048]{1,0:T(8,128)(2,1)}), bf16[1024,2048]{1,0:T(8,128)(2,1)}) %all-gather.5.cloned.1.call-update) | async-done | bytes 4194320 | tf_op jit(solution)/shard_map/all_gather | solution.py:67
  59.5 7.9 %convolution_convert_fusion.1 = bf16[1024,1024]{1,0:T(8,128)(2,1)S(1)} fusion(bf16[1024,2048]{1,0:T(8,128)(2,1)} %all-gather.5.cloned.1.call-done, bf16[2048,1024]{1,0:T(8,128)(2,1)} %param.12), kind=kOutput, calls=%fused_computation.16 | convolution fusion | flops 4296015872 | bytes 10485760 | tf_op jit(solution)/shard_map/dot_general | solution.py:68
  69.8 1.5 collective-permute-start
  71.3 1.5 collective-permute-start.1
  74.0 10.6 %collective-permute-done = bf16[256,1024]{1,0:T(8,128)(2,1)S(1)} collective-permute-done((bf16[256,1024]{1,0:T(8,128)(2,1)S(1)}, bf16[256,1024]{1,0:T(8,128)(2,1)S(1)}, u32[]{:S(2)}, u32[]{:S(2)}) %collective-permute-start) | collective-permute-done | bytes 524320 | tf_op jit(solution)/shard_map/ppermute | solution.py:16
  84.6 11.8 %collective-permute-done.1 = bf16[256,1024]{1,0:T(8,128)(2,1)S(1)} collective-permute-done((bf16[256,1024]{1,0:T(8,128)(2,1)S(1)}, bf16[256,1024]{1,0:T(8,128)(2,1)S(1)}, u32[]{:S(2)}, u32[]{:S(2)}) %collective-permute-start.1) | collective-permute-done | bytes 524320 | tf_op jit(solution)/shard_map/ppermute | solution.py:16
  96.4 3.5 %fusion.14 = (f32[256]{0:T(256)S(1)}, bf16[256,1024]{1,0:T(8,128)(2,1)}, bf16[256,1024]{1,0:T(8,128)(2,1)}) fusion(f32[1024]{0:T(1024)S(1)} %dynamic_slice.3, bf16[256,1024]{1,0:T(8,128)(2,1)S(1)} %collective-permute-done.2, bf16[256,1024]{1,0:T(8,128)(2,1)S(1)} %collective-permute-done.1, bf16[256,1024]{1,0:T(8,128)(2,1)S(1)} %collective-permute-done, ...), kind=kOutput, calls=%fused_computation.35 | convolution fusion | flops 540278528 | bytes 4728832 | tf_op jit(solution)/shard_map/dot_general | solution.py:76
  100.4 1.2 fusion.63
  101.7 3.6 %collective-permute-done.4 = f32[256]{0:T(256)S(1)} collective-permute-done((f32[256]{0:T(256)S(1)}, f32[256]{0:T(256)S(1)}, u32[]{:S(2)}, u32[]{:S(2)}) %collective-permute-start.4) | collective-permute-done | bytes 1056 | tf_op jit(solution)/shard_map/ppermute | solution.py:16
  105.3 0.9 collective-permute-start.5
  106.2 0.8 all-gather.9.cloned.1.call-done
  107.0 11.6 %convolution_convert_fusion.6 = bf16[256,1024]{1,0:T(8,128)(2,1)S(1)} fusion(bf16[256,8192]{1,0:T(8,128)(2,1)} %all-gather.9.cloned.1.call-done, bf16[1024,8192]{1,0:T(8,128)(2,1)} %param.16), kind=kOutput, calls=%fused_computation.29 | convolution fusion | flops 4295229440 | bytes 21495808 | tf_op jit(solution)/shard_map/dot_general | solution.py:149
  118.6 36.5 %all-gather.7.cloned.1.call-done = bf16[256,8192]{1,0:T(8,128)(2,1)} async-done(((bf16[256,1024]{1,0:T(8,128)(2,1)}), bf16[256,8192]{1,0:T(8,128)(2,1)}) %all-gather.7.cloned.1.call-update) | async-done | bytes 4194320 | tf_op jit(solution)/shard_map/all_gather | solution.py:84
  155.1 5.2 %broadcast_multiply_fusion = f32[256,256]{0,1:T(8,128)S(1)} fusion(f32[256]{0:T(256)S(1)} %add_rsqrt_fusion, bf16[256,8192]{1,0:T(8,128)(2,1)} %all-gather.7.cloned.1.call-done, bf16[8192,256]{1,0:T(8,128)(2,1)} %param.15), kind=kOutput, calls=%fused_computation.95 | convolution fusion | flops 1073807360 | bytes 8651776 | tf_op jit(solution)/shard_map/dot_general | solution.py:108
  161.0 9.6 %convolution_multiply_fusion = f32[256,1024]{1,0:T(8,128)S(1)} fusion(bf16[256,8192]{1,0:T(8,128)(2,1)} %all-gather.7.cloned.1.call-done, bf16[8192,1024]{1,0:T(8,128)(2,1)} %param.14, f32[256]{0:T(256)S(1)} %add_rsqrt_fusion), kind=kOutput, calls=%fused_computation.23 | convolution fusion | flops 4295229440 | bytes 22021120 | tf_op jit(solution)/shard_map/dot_general | solution.py:105
  174.6 1.2 slice-done.2
  175.8 1.2 slice-done.3
  177.1 6.4 %convolution_convert_fusion = bf16[256,8192]{1,0:T(8,128)(2,1)} fusion(bf16[256,1024]{0,1:T(8,128)(2,1)S(1)} %bitcast.134, bf16[1024,8192]{1,0:T(8,128)(2,1)S(1)} %bitcast.127), kind=kOutput, calls=%fused_computation.1 | convolution fusion | flops 4297064448 | bytes 21495808 | tf_op jit(solution)/shard_map/dot_general | solution.py:141
  183.6 1.9 copy.50
  185.5 1.8 copy.37
  187.3 2.2 fusion.12
  192.0 19.3 %fusion.26 = f32[256,8192]{1,0:T(8,128)} fusion(bf16[8192,1024]{1,0:T(8,128)(2,1)} %param.14, bf16[256,8,64]{2,0,1:T(8,128)(2,1)S(1)} %get-tuple-element.7, bf16[256,8,64]{2,0,1:T(8,128)(2,1)S(1)} %get-tuple-element.6), kind=kOutput, calls=%fused_computation.52 | convolution fusion | flops 4296015872 | bytes 25690112 | tf_op jit(solution)/shard_map/dot_general | solution.py:189
  211.3 8.1 %fusion = bf16[256,8192]{1,0:T(8,128)(2,1)} fusion(f32[256,8192]{1,0:T(8,128)} %fusion.26, bf16[256,256]{0,1:T(8,128)(2,1)S(1)} %bitcast.135, bf16[8192,256]{1,0:T(8,128)(2,1)} %param.15), kind=kOutput, calls=%fused_computation.2 | convolution fusion | flops 1077936128 | bytes 16908288 | tf_op jit(solution)/shard_map/dot_general | solution.py:194
  219.5 1.1 copy-done.1
  221.4 0.9 collective-permute-done.6
  222.3 3.8 %collective-permute-done.7 = f32[256]{0:T(256)S(1)} collective-permute-done((f32[256]{0:T(256)S(1)}, f32[256]{0:T(256)S(1)}, u32[]{:S(2)}, u32[]{:S(2)}) %collective-permute-start.7) | collective-permute-done | bytes 1056 | tf_op jit(solution)/shard_map/ppermute | solution.py:16
  226.8 3.9 %collective-permute-done.8 = f32[256]{0:T(256)S(1)} collective-permute-done((f32[256]{0:T(256)S(1)}, f32[256]{0:T(256)S(1)}, u32[]{:S(2)}, u32[]{:S(2)}) %collective-permute-start.8) | collective-permute-done | bytes 1056 | tf_op jit(solution)/shard_map/ppermute | solution.py:16
  230.7 1.7 reduce-scatter.3.cloned.1.call-done
  232.4 50.3 %reduce-scatter.5.cloned.1.call-done = bf16[256,1024]{1,0:T(8,128)(2,1)} async-done(((bf16[256,8192]{1,0:T(8,128)(2,1)}), bf16[256,1024]{1,0:T(8,128)(2,1)}) %reduce-scatter.5.cloned.1.call-update) | async-done | bytes 524304 | tf_op jit(solution)/shard_map/reduce_scatter | solution.py:197
  282.8 2.8 fusion.17
  285.6 33.6 %all-gather.11.cloned.1.call-done = bf16[1024,1024]{1,0:T(8,128)(2,1)} async-done(((bf16[256,1024]{1,0:T(8,128)(2,1)}), bf16[1024,1024]{1,0:T(8,128)(2,1)}) %all-gather.11.cloned.1.call-update) | async-done | bytes 2097168 | tf_op jit(solution)/shard_map/all_gather | solution.py:205
  319.2 13.6 %fusion.1 = f32[2048,1024]{1,0:T(8,128)} fusion(bf16[1024,1024]{1,0:T(8,128)(2,1)} %all-gather.11.cloned.1.call-done, bf16[1024,2048]{1,0:T(8,128)(2,1)} %all-gather.5.cloned.1.call-done, s32[1024]{0:T(1024)S(1)} %copy-done.11), kind=kOutput, calls=%fused_computation.3 | convolution fusion | flops 8593080320 | bytes 14684160 | tf_op jit(solution)/shard_map/dot_general | solution.py:206
  (91 shorter events, 14.3 us)
Async XLA Ops:
  7.2 52.3 %all-gather.5.cloned.1.call-start = ((), (), s32[]{:S(2)}) async-start(), calls=%async_computation.2 | async-start | bytes 4718592 | tf_op jit(solution)/shard_map/all_gather | solution.py:67
  7.9 99.1 %all-gather.9.cloned.1.call-start = ((), (), s32[]{:S(2)}) async-start(), calls=%async_computation.5 | async-start | bytes 4718592 | tf_op jit(solution)/shard_map/all_gather | solution.py:148
  8.6 146.4 %all-gather.7.cloned.1.call-start = ((), (), s32[]{:S(2)}) async-start(), calls=%async_computation.3 | async-start | bytes 4718592 | tf_op jit(solution)/shard_map/all_gather | solution.py:84
  8.7 58.7 %copy-start.10 = (s32[1024]{0:T(1024)S(1)}, s32[1024]{0:T(1024)}, u32[]{:S(2)}) copy-start(s32[1024]{0:T(1024)} %param.10) | copy-start | bytes 12292
  67.4 2.3 copy-start.12
  69.0 31.2 %copy-start.9 = (s32[1,256]{1,0:T(1,128)S(1)}, s32[1,256]{1,0:T(1,128)}, u32[]{:S(2)}) copy-start(s32[1,256]{1,0:T(1,128)} %param.11) | copy-start | bytes 3076
  69.8 14.8 %collective-permute-start = (bf16[256,1024]{1,0:T(8,128)(2,1)S(1)}, bf16[256,1024]{1,0:T(8,128)(2,1)S(1)}, u32[]{:S(2)}, u32[]{:S(2)}) collective-permute-start(bf16[256,1024]{1,0:T(8,128)(2,1)S(1)} %convolution_convert_fusion.5), channel_id=1, source_target_pairs={{0,8},{8,0},{16,24},{24,16},{1,9},{9,1},{17,25},{25,17},{2,10},{10... | collective-permute-start | bytes 1572872 | tf_op jit(solution)/shard_map/ppermute | solution.py:16
  71.3 25.0 %collective-permute-start.1 = (bf16[256,1024]{1,0:T(8,128)(2,1)S(1)}, bf16[256,1024]{1,0:T(8,128)(2,1)S(1)}, u32[]{:S(2)}, u32[]{:S(2)}) collective-permute-start(bf16[256,1024]{1,0:T(8,128)(2,1)S(1)} %convolution_convert_fusion.4), channel_id=1, source_target_pairs={{0,16},{8,24},{16,0},{24,8},{1,17},{9,25},{17,1},{25,9},{2,18},{10... | collective-permute-start | bytes 1572872 | tf_op jit(solution)/shard_map/ppermute | solution.py:16
  72.8 23.6 %collective-permute-start.2 = (bf16[256,1024]{1,0:T(8,128)(2,1)S(1)}, bf16[256,1024]{1,0:T(8,128)(2,1)S(1)}, u32[]{:S(2)}, u32[]{:S(2)}) collective-permute-start(bf16[256,1024]{1,0:T(8,128)(2,1)S(1)} %convolution_convert_fusion.3), channel_id=1, source_target_pairs={{0,24},{8,16},{16,8},{24,0},{1,25},{9,17},{17,9},{25,1},{2,26},{10... | collective-permute-start | bytes 1572872 | tf_op jit(solution)/shard_map/ppermute | solution.py:16
  99.9 132.5 %reduce-scatter.3.cloned.1.call-start = ((), (), s32[]{:S(2)}) async-start(), calls=%async_computation.4 | async-start | bytes 4718592 | tf_op jit(solution)/shard_map/reduce_scatter | solution.py:140
  100.3 1.3 collective-permute-start.3
  101.6 3.7 %collective-permute-start.4 = (f32[256]{0:T(256)S(1)}, f32[256]{0:T(256)S(1)}, u32[]{:S(2)}, u32[]{:S(2)}) collective-permute-start(f32[256]{0:T(256)S(1)} %add.130), channel_id=1, source_target_pairs={{0,2},{1,3},{2,0},{3,1},{4,6},{5,7},{6,4},{7,5},{8,10},{9,11},{10,... | collective-permute-start | bytes 3080 | tf_op jit(solution)/shard_map/ppermute | solution.py:16
  105.3 13.3 %collective-permute-start.5 = (f32[256]{0:T(256)S(1)}, f32[256]{0:T(256)S(1)}, u32[]{:S(2)}, u32[]{:S(2)}) collective-permute-start(f32[256]{0:T(256)S(1)} %add.131), channel_id=1, source_target_pairs={{0,4},{1,5},{2,6},{3,7},{4,0},{5,1},{6,2},{7,3},{8,12},{9,13},{10,... | collective-permute-start | bytes 3080 | tf_op jit(solution)/shard_map/ppermute | solution.py:16
  118.6 54.1 %copy-start.7 = (bf16[256,1024]{1,0:T(8,128)(2,1)}, bf16[256,1024]{1,0:T(8,128)(2,1)S(1)}, u32[]{:S(2)}) copy-start(bf16[256,1024]{1,0:T(8,128)(2,1)S(1)} %convolution_convert_fusion.6) | copy-start | bytes 1572868
  161.0 10.6 %copy-start.3 = (bf16[256,64]{1,0:T(8,128)(2,1)}, bf16[256,64]{1,0:T(8,128)(2,1)S(1)}, u32[]{:S(2)}) copy-start(bf16[256,64]{1,0:T(8,128)(2,1)S(1)} %get-tuple-element.16) | copy-start | bytes 98308
  161.0 10.6 %copy-start.5 = (bf16[256,64]{1,0:T(8,128)(2,1)}, bf16[256,64]{1,0:T(8,128)(2,1)S(1)}, u32[]{:S(2)}) copy-start(bf16[256,64]{1,0:T(8,128)(2,1)S(1)} %get-tuple-element.17) | copy-start | bytes 98308
  170.6 1.0 copy-start
  170.8 3.6 %slice-start = ((s8[16777216]{0:T(1024)(128)(4,1)}), s8[4194304]{0:T(1024)(128)(4,1)S(1)}, s32[]{:S(2)}) async-start(s8[16777216]{0:T(1024)(128)(4,1)} %bitcast.126), calls=%async_computation.8 | async-start | bytes 8388608
  171.6 3.0 slice-start.1
  172.7 3.1 slice-start.2
  173.3 3.7 %slice-start.3 = ((s8[16777216]{0:T(1024)(128)(4,1)}), s8[4194304]{0:T(1024)(128)(4,1)S(1)}, s32[]{:S(2)}) async-start(s8[16777216]{0:T(1024)(128)(4,1)} %bitcast.126), calls=%async_computation.11 | async-start | bytes 8388608
  183.5 99.2 %reduce-scatter.5.cloned.1.call-start = ((), (), s32[]{:S(2)}) async-start(), calls=%async_computation.6 | async-start | bytes 4718592 | tf_op jit(solution)/shard_map/reduce_scatter | solution.py:197
  187.3 3.6 %copy-start.4 = (bf16[256,64]{1,0:T(8,128)(2,1)S(1)}, bf16[256,64]{1,0:T(8,128)(2,1)}, u32[]{:S(2)}) copy-start(bf16[256,64]{1,0:T(8,128)(2,1)} %copy-done.3) | copy-start | bytes 98308
  187.3 3.6 %copy-start.6 = (bf16[256,64]{1,0:T(8,128)(2,1)S(1)}, bf16[256,64]{1,0:T(8,128)(2,1)}, u32[]{:S(2)}) copy-start(bf16[256,64]{1,0:T(8,128)(2,1)} %copy-done.5) | copy-start | bytes 98308
  187.3 4.2 %copy-start.8 = (f32[256,64]{1,0:T(8,128)S(1)}, f32[256,64]{1,0:T(8,128)}, u32[]{:S(2)}) copy-start(f32[256,64]{1,0:T(8,128)} %get-tuple-element.18) | copy-start | bytes 196612
  219.4 1.2 copy-start.1
  219.4 63.4 %copy-start.2 = (bf16[256,1024]{1,0:T(8,128)(2,1)S(1)}, bf16[256,1024]{1,0:T(8,128)(2,1)}, u32[]{:S(2)}) copy-start(bf16[256,1024]{1,0:T(8,128)(2,1)} %param.17) | copy-start | bytes 1572868
  219.4 99.8 %copy-start.11 = (s32[1024]{0:T(1024)S(1)}, s32[1024]{0:T(1024)}, u32[]{:S(2)}) copy-start(s32[1024]{0:T(1024)} %param.10) | copy-start | bytes 12292
  219.4 99.7 %all-gather.11.cloned.1.call-start = ((), (), s32[]{:S(2)}) async-start(), calls=%async_computation.7 | async-start | bytes 2621440 | tf_op jit(solution)/shard_map/all_gather | solution.py:205
  221.1 1.2 collective-permute-start.6
  222.3 3.8 %collective-permute-start.7 = (f32[256]{0:T(256)S(1)}, f32[256]{0:T(256)S(1)}, u32[]{:S(2)}, u32[]{:S(2)}) collective-permute-start(f32[256]{0:T(256)S(1)} %add.144), channel_id=1, source_target_pairs={{0,2},{1,3},{2,0},{3,1},{4,6},{5,7},{6,4},{7,5},{8,10},{9,11},{10,... | collective-permute-start | bytes 3080 | tf_op jit(solution)/shard_map/ppermute | solution.py:16
  226.1 4.7 %collective-permute-start.8 = (f32[256]{0:T(256)S(1)}, f32[256]{0:T(256)S(1)}, u32[]{:S(2)}, u32[]{:S(2)}) collective-permute-start(f32[256]{0:T(256)S(1)} %add.145), channel_id=1, source_target_pairs={{0,4},{1,5},{2,6},{3,7},{4,0},{5,1},{6,2},{7,3},{8,12},{9,13},{10,... | collective-permute-start | bytes 3080 | tf_op jit(solution)/shard_map/ppermute | solution.py:16
Sparse Core Ops, SparseCore 0:
  9.6 49.8 all-gather.4
  61.1 45.8 all-gather.8
  109.2 45.8 all-gather.6
  183.6 48.7 reduce-scatter.2
  234.6 48.1 reduce-scatter.4
  285.7 33.4 all-gather.10

commit v2 on v1

v2 whole, which is shorter than its diff:
```python
import functools
import math

import jax
import jax.numpy as jnp
from jax import lax
from jax.experimental import pallas as pl
from jax.experimental.pallas import tpu as pltpu
from jax.sharding import PartitionSpec as P

HD = 128


epsilon = 1e-05


def swapped(value, axis, mask):
    pairs = [(source, source ^ mask) for source in range(lax.axis_size(axis))]
    return lax.ppermute(value, axis, pairs)


def summed(value, axis):
    mask = 1
    while mask < lax.axis_size(axis):
        value = value + swapped(value, axis, mask)
        mask *= 2
    return value


def frequencies():
    exponent = jnp.arange(0, HD, 2).astype(jnp.float32) / HD
    plain_rate = 500000.0 ** (-exponent)
    wavelength = 2.0 * math.pi / plain_rate
    smoothing = (8192.0 / wavelength - 1.0) / 3.0
    blended = (1.0 - smoothing) * plain_rate / 8.0 + smoothing * plain_rate
    return jnp.where(
        wavelength < 2048.0, plain_rate, jnp.where(wavelength > 8192.0, plain_rate / 8.0, blended)
    )


def rotate(vector_in, cosine_table, sine_table):
    half_size = vector_in.shape[-1] // 2
    first_half = vector_in[..., :half_size]
    second = vector_in[..., half_size:]
    return jnp.concatenate(
        [
            first_half * cosine_table - second * sine_table,
            second * cosine_table + first_half * sine_table,
        ],
        axis=-1,
    )


def unrotate(vector_in, cosine_table, sine_table):
    return rotate(vector_in, cosine_table, -sine_table)


VMEM_LIMIT = 56 * 2**20
ROWS_BY_ROWS = (((1,), (1,)), ((), ()))
COLS_BY_COLS = (((0,), (0,)), ((), ()))


def dot_f32(left, right, dims=(((1,), (0,)), ((), ()))):
    return lax.dot_general(left, right, dims, preferred_element_type=jnp.float32)


def attend(
    repeat, read_query, cosines, sines, seg_row, seg_col, keys, values, grad_ref, context_ref,
    query_grad_ref,
):
    rows = cosines.shape[0]
    score_scale = 1.0 / math.sqrt(HD)
    later = lax.broadcasted_iota(jnp.int32, (rows, rows), 0)
    sooner = lax.broadcasted_iota(jnp.int32, (rows, rows), 1)
    allowed = (seg_col == seg_row) & (sooner <= later)
    aligned = jnp.zeros((rows, HD), jnp.float32)
    key_parts, value_parts = [], []
    for group in range(len(keys)):
        key_part = jnp.zeros((rows, HD), jnp.float32)
        value_part = jnp.zeros((rows, HD), jnp.float32)
        for member in range(repeat):
            own = pl.ds((group * repeat + member) * HD, HD)
            plain = read_query(own)
            query = turn(plain, cosines, sines).astype(jnp.bfloat16)
            scores = dot_f32(query, keys[group], ROWS_BY_ROWS) * score_scale
            scores = jnp.where(allowed, scores, -1e30)
            exponents = jnp.exp(scores - jnp.max(scores, axis=1, keepdims=True))
            attention = exponents / jnp.sum(exponents, axis=1, keepdims=True)
            attention_bf = attention.astype(jnp.bfloat16)
            context_ref[:, own] = dot_f32(attention_bf, values[group]).astype(jnp.bfloat16)
            context_grad = grad_ref[:, own]
            grad_probs = dot_f32(context_grad, values[group], ROWS_BY_ROWS)
            mean = jnp.sum(grad_probs * attention, axis=1, keepdims=True)
            score_grad = (attention * (grad_probs - mean) * score_scale).astype(jnp.bfloat16)
            query_grad = turn(dot_f32(score_grad, keys[group]), cosines, -sines).astype(
                jnp.bfloat16
            )
            query_grad_ref[:, own] = query_grad
            aligned += query_grad.astype(jnp.float32) * plain
            key_part += dot_f32(score_grad, query, COLS_BY_COLS)
            value_part += dot_f32(attention_bf, context_grad, COLS_BY_COLS)
        key_parts.append(key_part)
        value_parts.append(value_part)
    return aligned, key_parts, value_parts


def turn(vector_in, cosines, sines):
    return vector_in * cosines + pltpu.roll(vector_in, HD // 2, 1) * sines


def attention_kernel(
    repeat, query_ref, scale_ref, cos_ref, sin_ref, seg_row_ref, seg_col_ref, key_ref, value_ref,
    grad_ref, context_ref, query_grad_ref, key_part_ref, value_part_ref, aligned_ref,
):
    row_scale = scale_ref[...]
    groups = [pl.ds(group * HD, HD) for group in range(key_ref.shape[1] // HD)]
    aligned, key_parts, value_parts = attend(
        repeat, lambda own: query_ref[:, own] * row_scale, cos_ref[...], sin_ref[...],
        seg_row_ref[...], seg_col_ref[...], [key_ref[:, shared] for shared in groups],
        [value_ref[:, shared] for shared in groups], grad_ref, context_ref, query_grad_ref,
    )
    for shared, key_part, value_part in zip(groups, key_parts, value_parts):
        key_part_ref[:, shared] = key_part
        value_part_ref[:, shared] = value_part
    aligned_ref[...] = jnp.sum(aligned, axis=1, keepdims=True)


def attention_parts(repeat, query_pre, inv_rms, cosines, sines, seg_row, keys, values, context_grad):
    rows = query_pre.shape[0]
    whole = pl.BlockSpec(memory_space=pltpu.VMEM)
    return pl.pallas_call(
        functools.partial(attention_kernel, repeat),
        in_specs=[whole] * 9,
        out_specs=[whole] * 5,
        out_shape=[
            jax.ShapeDtypeStruct(query_pre.shape, jnp.bfloat16),
            jax.ShapeDtypeStruct(query_pre.shape, jnp.bfloat16),
            jax.ShapeDtypeStruct(keys.shape, jnp.float32),
            jax.ShapeDtypeStruct(keys.shape, jnp.float32),
            jax.ShapeDtypeStruct((rows, 1), jnp.float32),
        ],
        compiler_params=pltpu.CompilerParams(vmem_limit_bytes=VMEM_LIMIT),
    )(
        query_pre, inv_rms, cosines, sines, seg_row[None, :], seg_row[:, None], keys, values,
        context_grad,
    )


def middle_kernel(
    repeat, gained_ref, q_weight_ref, kv_weight_ref, scale_ref, cos_ref, sin_ref, seg_row_ref,
    seg_col_ref, grad_ref, context_ref, aligned_ref, out_ref, gained, q_weight, kv_weight, out,
    query_sum, pair_sum, query_grad, sems,
):
    width, heads_cols = q_weight.shape
    pieces = sems.shape[1]
    step = width // pieces

    def part(piece):
        return pl.ds(pl.multiple_of(piece * step, step), step)

    def fetches(piece):
        span = part(piece)
        return (
            pltpu.make_async_copy(
                gained_ref.at[:, span], gained.at[:, span], sems.at[0, piece]
            ),
            pltpu.make_async_copy(q_weight_ref.at[span], q_weight.at[span], sems.at[1, piece]),
            pltpu.make_async_copy(kv_weight_ref.at[span], kv_weight.at[span], sems.at[2, piece]),
        )

    def returned(piece):
        span = part(piece)
        return pltpu.make_async_copy(out.at[:, span], out_ref.at[:, span], sems.at[3, piece])

    @pl.loop(0, pieces)
    def _(piece):
        for fetch in fetches(piece):
            fetch.start()

    query_sum[...] = jnp.zeros_like(query_sum)
    pair_sum[...] = jnp.zeros_like(pair_sum)

    @pl.loop(0, pieces)
    def _(piece):
        for fetch in fetches(piece):
            fetch.wait()
        span = part(piece)
        features = gained[:, span]
        query_sum[...] += dot_f32(features, q_weight[span, :])
        pair_sum[...] += dot_f32(features, kv_weight[span, :])

    row_scale = scale_ref[...]
    cosines, sines = cos_ref[...], sin_ref[...]
    groups = kv_weight.shape[1] // (2 * HD)
    pair_plain = pair_sum[...] * row_scale
    halves = [pair_plain[:, i * HD : (i + 1) * HD] for i in range(2 * groups)]
    aligned, key_parts, value_parts = attend(
        repeat, lambda own: query_sum[:, own] * row_scale, cosines, sines, seg_row_ref[...],
        seg_col_ref[...], [turn(half, cosines, sines).astype(jnp.bfloat16) for half in halves[::2]],
        [half.astype(jnp.bfloat16) for half in halves[1::2]], grad_ref, context_ref, query_grad,
    )
    pair_grads = []
    for key_part, value_part in zip(key_parts, value_parts):
        pair_grads.append(turn(key_part, cosines, -sines).astype(jnp.bfloat16))
        pair_grads.append(value_part.astype(jnp.bfloat16))
    for half, pair_grad in zip(halves, pair_grads):
        aligned += half * pair_grad.astype(jnp.float32)
    aligned_ref[...] = jnp.sum(aligned, axis=1, keepdims=True)
    pair_grad = jnp.concatenate(pair_grads, axis=1)

    @pl.loop(0, pieces)
    def _(piece):
        span = part(piece)
        out[:, span] = (
            dot_f32(query_grad[...], q_weight[span, :], ROWS_BY_ROWS)
            + dot_f32(pair_grad, kv_weight[span, :], ROWS_BY_ROWS)
        ).astype(out.dtype)
        returned(piece).start()

    @pl.loop(0, pieces)
    def _(piece):
        returned(piece).wait()


def middle(
    repeat, gained, q_weight, kv_weight, inv_rms, cosines, sines, seg_row, context_grad
):
    rows, width = gained.shape
    heads_cols, kv_cols = q_weight.shape[1], kv_weight.shape[1]
    whole, far = pl.BlockSpec(memory_space=pltpu.VMEM), pl.BlockSpec(memory_space=pl.ANY)
    return pl.pallas_call(
        functools.partial(middle_kernel, repeat),
        in_specs=[far] * 3 + [whole] * 6,
        out_specs=[whole] * 2 + [far],
        out_shape=[
            jax.ShapeDtypeStruct((rows, heads_cols), jnp.bfloat16),
            jax.ShapeDtypeStruct((rows, 1), jnp.float32),
            jax.ShapeDtypeStruct((rows, width), jnp.bfloat16),
        ],
        scratch_shapes=[
            pltpu.VMEM(gained.shape, jnp.bfloat16),
            pltpu.VMEM(q_weight.shape, jnp.bfloat16),
            pltpu.VMEM(kv_weight.shape, jnp.bfloat16),
            pltpu.VMEM(gained.shape, jnp.bfloat16),
            pltpu.VMEM((rows, heads_cols), jnp.float32),
            pltpu.VMEM((rows, kv_cols), jnp.float32),
            pltpu.VMEM((rows, heads_cols), jnp.bfloat16),
            pltpu.SemaphoreType.DMA((4, 8)),
        ],
        compiler_params=pltpu.CompilerParams(vmem_limit_bytes=VMEM_LIMIT),
    )(
        gained, q_weight, kv_weight, inv_rms, cosines, sines, seg_row[None, :], seg_row[:, None],
        context_grad,
    )


def stitch_kernel(packs, rank_ref, token_ref, source_ref, weight_ref, *refs):
    out_refs, product = refs[:packs], refs[-1]
    block = source_ref.shape[0]
    step = pl.program_id(0)
    here = pl.ds(pl.multiple_of(step * block, block), block)
    product[here, :] = dot_f32(source_ref[...], weight_ref[...]).astype(jnp.bfloat16)

    @pl.when(step == pl.num_programs(0) - 1)
    def _():
        pack_len = out_refs[0].shape[0]
        shape = (pack_len, product.shape[0])
        place = token_ref[...] - lax.broadcasted_iota(jnp.int32, shape, 0)
        for distance in range(packs):
            first = (rank_ref[0] ^ distance) * pack_len
            rows = (place == first).astype(jnp.float32).astype(jnp.bfloat16)
            out_refs[distance][...] = dot_f32(rows, product[...]).astype(jnp.bfloat16)


def stitched(packs, pack_len, rank, row_token, source, weight):
    rows, features = source.shape
    cols = weight.shape[1]
    block = min(512, rows)
    fixed = lambda i: (0, 0)
    return pl.pallas_call(
        functools.partial(stitch_kernel, packs),
        grid=(rows // block,),
        in_specs=[
            pl.BlockSpec(memory_space=pltpu.SMEM),
            pl.BlockSpec((1, rows), fixed),
            pl.BlockSpec((block, features), lambda i: (i, 0)),
            pl.BlockSpec(weight.shape, fixed),
        ],
        out_specs=[pl.BlockSpec((pack_len, cols), fixed)] * packs,
        out_shape=[jax.ShapeDtypeStruct((pack_len, cols), jnp.bfloat16)] * packs,
        scratch_shapes=[pltpu.VMEM((rows, cols), jnp.bfloat16)],
        compiler_params=pltpu.CompilerParams(vmem_limit_bytes=VMEM_LIMIT),
    )(rank.reshape(1), row_token[None, :], source, weight)


def back_kernel(query_ref, pair_ref, q_weight_ref, kv_weight_ref, out_ref):
    out_ref[...] = (
        dot_f32(query_ref[...], q_weight_ref[...], ROWS_BY_ROWS)
        + dot_f32(pair_ref[...], kv_weight_ref[...], ROWS_BY_ROWS)
    ).astype(out_ref.dtype)


def back_projected(grad_queries, grad_pairs, q_weight, kv_weight):
    rows = grad_queries.shape[0]
    width = q_weight.shape[0]
    block = 2048
    fixed = lambda i: (0, 0)
    return pl.pallas_call(
        back_kernel,
        grid=(width // block,),
        in_specs=[
            pl.BlockSpec(grad_queries.shape, fixed),
            pl.BlockSpec(grad_pairs.shape, fixed),
            pl.BlockSpec((block, q_weight.shape[1]), lambda i: (i, 0)),
            pl.BlockSpec((block, kv_weight.shape[1]), lambda i: (i, 0)),
        ],
        out_specs=pl.BlockSpec((rows, block), lambda i: (0, i)),
        out_shape=jax.ShapeDtypeStruct((rows, width), jnp.bfloat16),
        compiler_params=pltpu.CompilerParams(vmem_limit_bytes=VMEM_LIMIT),
    )(grad_queries, grad_pairs, q_weight, kv_weight)


def outer_kernel(*refs):
    features_ref, out_ref = refs[0], refs[-1]
    total = None
    for place, grad_ref in enumerate(refs[1:-1]):
        rows = grad_ref.shape[0]
        term = dot_f32(features_ref[:, pl.ds(place * rows, rows)], grad_ref[...])
        total = term if total is None else total + term
    out_ref[...] = total


def outer_summed(features, grads):
    block = min(512, features.shape[0])
    cols = grads[0].shape[1]
    return pl.pallas_call(
        outer_kernel,
        grid=(features.shape[0] // block,),
        in_specs=[pl.BlockSpec((block, features.shape[1]), lambda i: (i, 0))]
        + [pl.BlockSpec(grad.shape, lambda i: (0, 0)) for grad in grads],
        out_specs=pl.BlockSpec((block, cols), lambda i: (i, 0)),
        out_shape=jax.ShapeDtypeStruct((features.shape[0], cols), jnp.float32),
        compiler_params=pltpu.CompilerParams(vmem_limit_bytes=VMEM_LIMIT),
    )(features, *grads)


FIRST, SECOND, LAST = (1, 3, 0, 2), (2, 0, 3, 1), (3, 2, 1, 0)


def along(value, pairs):
    both = [(2 * start + core, 2 * end + core) for start, end in pairs for core in range(2)]
    return lax.ppermute(value, "tp", both)


def towards(table):
    return [(start, end) for start, end in enumerate(table)]


def arriving(table):
    return [(start, end) for end, start in enumerate(table)]


def after(value, done):
    value, done = lax.optimization_barrier((value, done))
    return value, done


def line_gather(block):
    beside = swapped(block, "tp", 1)
    first = along(block, arriving(FIRST))
    block, first = after(block, first)
    far = along(first, [(2, 3), (1, 0)])
    second = along(block, arriving(SECOND))
    near = along(block, [(1, 2), (2, 1)])
    last = far + near
    blocks = [block, beside]
    for own in (first, second, last):
        blocks += [own, swapped(own, "tp", 1)]
    return blocks


def line_scatter(parts):
    def joined(place):
        other = swapped(parts[2 * place + 1], "tp", 1)
        return parts[2 * place].astype(jnp.float32) + other.astype(jnp.float32)

    last = joined(0).astype(jnp.bfloat16)
    far = along(last, [(0, 1), (3, 2)])
    near = along(last, [(1, 2), (2, 1)])
    second = along(joined(1).astype(jnp.bfloat16), towards(SECOND))
    first = joined(2) + far.astype(jnp.float32)
    first = along(first.astype(jnp.bfloat16), towards(FIRST))
    own = joined(3) + near.astype(jnp.float32)
    return own, second, first


def line_total(own, second, first):
    return own + second.astype(jnp.float32) + first.astype(jnp.float32)


def line_stitch_kernel(packs, rank_ref, token_ref, weight_ref, *refs):
    blocks, out_refs = refs[:8], refs[8 : 8 + packs]
    rows, product, sems = refs[8 + packs :]
    block = rows.shape[0] // 8
    fetches = [
        pltpu.make_async_copy(blocks[i], rows.at[pl.ds(i * block, block)], sems.at[i])
        for i in range(8)
    ]
    for fetch in fetches:
        fetch.start()
    for half in range(2):
        here = pl.ds(half * 4 * block, 4 * block)
        for fetch in fetches[half * 4 : half * 4 + 4]:
            fetch.wait()
        product[here, :] = dot_f32(rows[here, :], weight_ref[...]).astype(jnp.bfloat16)
    pack_len = out_refs[0].shape[0]
    place = token_ref[...] - lax.broadcasted_iota(jnp.int32, (pack_len, product.shape[0]), 0)
    for distance in range(packs):
        first = (rank_ref[0] ^ distance) * pack_len
        chosen = (place == first).astype(jnp.float32).astype(jnp.bfloat16)
        out_refs[distance][...] = dot_f32(chosen, product[...]).astype(jnp.bfloat16)


def line_stitched(packs, pack_len, rank, token_row, blocks, weight):
    block, features = blocks[0].shape
    cols = weight.shape[1]
    whole, far = pl.BlockSpec(memory_space=pltpu.VMEM), pl.BlockSpec(memory_space=pl.ANY)
    return pl.pallas_call(
        functools.partial(line_stitch_kernel, packs),
        in_specs=[pl.BlockSpec(memory_space=pltpu.SMEM), whole, whole] + [far] * 8,
        out_specs=[whole] * packs,
        out_shape=[jax.ShapeDtypeStruct((pack_len, cols), jnp.bfloat16)] * packs,
        scratch_shapes=[
            pltpu.VMEM((8 * block, features), jnp.bfloat16),
            pltpu.VMEM((8 * block, cols), jnp.bfloat16),
            pltpu.SemaphoreType.DMA((8,)),
        ],
        compiler_params=pltpu.CompilerParams(vmem_limit_bytes=VMEM_LIMIT),
    )(rank.reshape(1), token_row, weight, *blocks)


def line_grad_kernel(ranks_ref, weight_ref, *refs):
    blocks, out_ref, features, total, sems = refs[:8], *refs[8:]
    step = pl.program_id(0)

    @pl.when(step == 0)
    def _():
        for i in range(8):
            pltpu.make_async_copy(blocks[i], features.at[i], sems.at[i]).start()
        total[...] = jnp.zeros_like(total)

    pltpu.make_async_copy(blocks[0], features.at[step], sems.at[step]).wait()
    total[...] += dot_f32(features[step], weight_ref[...], ROWS_BY_ROWS)

    @pl.when(step == 7)
    def _():
        out_ref[...] = total[...].astype(out_ref.dtype)


def line_grad_context(ranks, blocks, weight):
    rows, cols = blocks[0].shape
    heads_cols = weight.shape[0]
    far = pl.BlockSpec(memory_space=pl.ANY)
    return pl.pallas_call(
        line_grad_kernel,
        grid_spec=pltpu.PrefetchScalarGridSpec(
            num_scalar_prefetch=1,
            grid=(8,),
            in_specs=[pl.BlockSpec((heads_cols, cols), lambda i, ranks: (0, ranks[i]))] + [far] * 8,
            out_specs=pl.BlockSpec((rows, heads_cols), lambda i, ranks: (0, 0)),
            scratch_shapes=[
                pltpu.VMEM((8, rows, cols), jnp.bfloat16),
                pltpu.VMEM((rows, heads_cols), jnp.float32),
                pltpu.SemaphoreType.DMA((8,)),
            ],
        ),
        out_shape=jax.ShapeDtypeStruct((rows, heads_cols), jnp.bfloat16),
        compiler_params=pltpu.CompilerParams(vmem_limit_bytes=VMEM_LIMIT),
    )(ranks, weight, *blocks)


def line_attended_kernel(ranks_ref, context_ref, weight_ref, *out_refs):
    step = pl.program_id(0)
    product = dot_f32(context_ref[...], weight_ref[...]).astype(jnp.bfloat16)
    for i in range(8):

        @pl.when(step == i)
        def _(i=i):
            out_refs[i][...] = product


def line_attended(ranks, context, weight):
    rows, heads_cols = context.shape
    cols = weight.shape[1] // 8
    return pl.pallas_call(
        line_attended_kernel,
        grid_spec=pltpu.PrefetchScalarGridSpec(
            num_scalar_prefetch=1,
            grid=(8,),
            in_specs=[
                pl.BlockSpec((rows, heads_cols), lambda i, ranks: (0, 0)),
                pl.BlockSpec((heads_cols, cols), lambda i, ranks: (0, ranks[i])),
            ],
            out_specs=[pl.BlockSpec((rows, cols), lambda i, ranks: (0, 0))] * 8,
        ),
        out_shape=[jax.ShapeDtypeStruct((rows, cols), jnp.bfloat16)] * 8,
        compiler_params=pltpu.CompilerParams(vmem_limit_bytes=VMEM_LIMIT),
    )(ranks, context, weight)


def line_middle_kernel(
    repeat, from_ref, to_ref, gain_ref, cos_ref, sin_ref, seg_row_ref, seg_col_ref, grad_ref,
    q_weight_ref, kv_weight_ref, *refs,
):
    blocks, (context_ref, aligned_ref, scale_ref), out_refs = refs[:8], refs[8:11], refs[11:19]
    hidden, q_weight, kv_weight, out, query_sum, pair_sum, query_grad, sems, out_sems = refs[19:]
    width = q_weight.shape[0]
    rows, step = blocks[0].shape

    def part(rank):
        return pl.ds(pl.multiple_of(rank * step, step), step)

    def fetches(place):
        span = part(from_ref[place])
        return (
            pltpu.make_async_copy(q_weight_ref.at[span], q_weight.at[span], sems.at[1, place]),
            pltpu.make_async_copy(kv_weight_ref.at[span], kv_weight.at[span], sems.at[2, place]),
        )

    for place in range(8):
        pltpu.make_async_copy(blocks[place], hidden.at[place], sems.at[0, place]).start()
        for fetch in fetches(place):
            fetch.start()

    query_sum[...] = jnp.zeros_like(query_sum)
    pair_sum[...] = jnp.zeros_like(pair_sum)

    def project(place, squares):
        pltpu.make_async_copy(blocks[0], hidden.at[place], sems.at[0, place]).wait()
        for fetch in fetches(place):
            fetch.wait()
        span = part(from_ref[place])
        features = hidden[place].astype(jnp.float32)
        gained = (features * gain_ref[:, span]).astype(jnp.bfloat16)
        query_sum[...] += dot_f32(gained, q_weight[span, :])
        pair_sum[...] += dot_f32(gained, kv_weight[span, :])
        return squares + jnp.sum(features * features, axis=1, keepdims=True)

    squares = lax.fori_loop(0, 8, project, jnp.zeros((rows, 1), jnp.float32))
    row_scale = lax.rsqrt(squares / width + epsilon)
    scale_ref[...] = row_scale
    cosines, sines = cos_ref[...], sin_ref[...]
    groups = kv_weight.shape[1] // (2 * HD)
    pair_plain = pair_sum[...] * row_scale
    halves = [pair_plain[:, i * HD : (i + 1) * HD] for i in range(2 * groups)]
    aligned, key_parts, value_parts = attend(
        repeat, lambda own: query_sum[:, own] * row_scale, cosines, sines, seg_row_ref[...],
        seg_col_ref[...], [turn(half, cosines, sines).astype(jnp.bfloat16) for half in halves[::2]],
        [half.astype(jnp.bfloat16) for half in halves[1::2]], grad_ref, context_ref, query_grad,
    )
    pair_grads = []
    for key_part, value_part in zip(key_parts, value_parts):
        pair_grads.append(turn(key_part, cosines, -sines).astype(jnp.bfloat16))
        pair_grads.append(value_part.astype(jnp.bfloat16))
    for half, pair_grad in zip(halves, pair_grads):
        aligned += half * pair_grad.astype(jnp.float32)
    aligned_ref[...] = jnp.sum(aligned, axis=1, keepdims=True)
    pair_grad = jnp.concatenate(pair_grads, axis=1)

    @pl.loop(0, 8)
    def _(place):
        span = part(to_ref[place])
        out[place] = (
            dot_f32(query_grad[...], q_weight[span, :], ROWS_BY_ROWS)
            + dot_f32(pair_grad, kv_weight[span, :], ROWS_BY_ROWS)
        ).astype(out.dtype)
        for i in range(8):

            @pl.when(place == i)
            def _(i=i):
                pltpu.make_async_copy(out.at[i], out_refs[i], out_sems.at[i]).start()

    for i in range(8):
        pltpu.make_async_copy(out.at[i], out_refs[i], out_sems.at[i]).wait()


def line_middle(
    repeat, sources, targets, blocks, gain, q_weight, kv_weight, cosines, sines, seg_row,
    context_grad,
):
    rows, step = blocks[0].shape
    heads_cols, kv_cols = q_weight.shape[1], kv_weight.shape[1]
    whole, far = pl.BlockSpec(memory_space=pltpu.VMEM), pl.BlockSpec(memory_space=pl.ANY)
    scalars = pl.BlockSpec(memory_space=pltpu.SMEM)
    results = pl.pallas_call(
        functools.partial(line_middle_kernel, repeat),
        in_specs=[scalars] * 2 + [whole] * 6 + [far] * 10,
        out_specs=[whole] * 3 + [far] * 8,
        out_shape=[
            jax.ShapeDtypeStruct((rows, heads_cols), jnp.bfloat16),
            jax.ShapeDtypeStruct((rows, 1), jnp.float32),
            jax.ShapeDtypeStruct((rows, 1), jnp.float32),
        ]
        + [jax.ShapeDtypeStruct((rows, step), jnp.bfloat16)] * 8,
        scratch_shapes=[
            pltpu.VMEM((8, rows, step), jnp.bfloat16),
            pltpu.VMEM(q_weight.shape, jnp.bfloat16),
            pltpu.VMEM(kv_weight.shape, jnp.bfloat16),
            pltpu.VMEM((8, rows, step), jnp.bfloat16),
            pltpu.VMEM((rows, heads_cols), jnp.float32),
            pltpu.VMEM((rows, kv_cols), jnp.float32),
            pltpu.VMEM((rows, heads_cols), jnp.bfloat16),
            pltpu.SemaphoreType.DMA((3, 8)),
            pltpu.SemaphoreType.DMA((8,)),
        ],
        compiler_params=pltpu.CompilerParams(vmem_limit_bytes=VMEM_LIMIT),
    )(
        sources, targets, gain[None, :], cosines, sines, seg_row[None, :], seg_row[:, None],
        context_grad, q_weight, kv_weight, *blocks,
    )
    return results[0], results[1], results[2], results[3:]


def line_body(
    source, row_token, seg_ids, stitch_weight, norm_gain, q_weight, kv_weight, o_weight, out_grad
):
    tok_rank = lax.axis_index("tok")
    tp_rank = lax.axis_index("tp")
    packs = lax.axis_size("tok")
    pack_len = seg_ids.shape[1]
    width = q_weight.shape[0]
    own_cols = stitch_weight.shape[1]
    repeat = (q_weight.shape[1] // HD) // (kv_weight.shape[1] // (2 * HD))
    own_gain = lax.dynamic_slice_in_dim(norm_gain, tp_rank * own_cols, own_cols)
    chip, core = tp_rank // 2, tp_rank % 2

    def ranks(tables):
        chips = jnp.array(tables, jnp.int32)[:, chip]
        return jnp.stack([2 * chips + core, 2 * chips + 1 - core], axis=1).reshape(-1)

    stay = (0, 1, 2, 3)
    sources, targets = ranks((stay, FIRST, SECOND, LAST)), ranks((LAST, SECOND, FIRST, stay))

    within = jnp.arange(pack_len, dtype=jnp.int32)
    seg_row = seg_ids[0]
    earlier = jnp.sum((seg_row[None, :] < seg_row[:, None]).astype(jnp.int32), axis=1)
    angles = (within - earlier).astype(jnp.float32)[:, None] * frequencies()[None, :]
    cosine, sine = jnp.cos(angles), jnp.sin(angles)
    cosines = jnp.concatenate([cosine, cosine], axis=1)
    sines = jnp.concatenate([-sine, sine], axis=1)

    gathered = line_gather(source)
    token_row = row_token.reshape(8, -1)[sources].reshape(1, -1)
    late_grad, gathered[-2] = after(out_grad, gathered[-2])
    grad_blocks = line_gather(late_grad)
    placed = line_stitched(packs, pack_len, tok_rank, token_row, gathered, stitch_weight)
    hidden = placed[0].astype(jnp.float32)
    for distance in range(1, packs):
        hidden += swapped(placed[distance], "tok", distance).astype(jnp.float32)
    hidden_bf = hidden.astype(jnp.bfloat16)
    hidden_f = hidden_bf.astype(jnp.float32)
    hidden_blocks = line_gather(hidden_bf)
    grad_context = line_grad_context(sources, grad_blocks, o_weight)

    context, aligned, inv_rms, grad_parts = line_middle(
        repeat, sources, targets, hidden_blocks, norm_gain, q_weight, kv_weight, cosines, sines,
        seg_row, grad_context,
    )
    grad_own, grad_second, grad_first = line_scatter(grad_parts)
    aligned = summed(aligned[:, 0], "tp")
    context, aligned = after(context, aligned)
    attended_parts = line_attended(targets, context, o_weight)
    grad_sum = line_total(grad_own, grad_second, grad_first)
    attended_parts, grad_sum = after(attended_parts, grad_sum)
    grad_hidden = (
        out_grad.astype(jnp.float32)
        + inv_rms * own_gain * grad_sum
        - hidden_f * (inv_rms * inv_rms * aligned[:, None] / width)
    ).astype(jnp.bfloat16)
    every_pack = [grad_hidden] + [
        swapped(grad_hidden, "tok", distance) for distance in range(1, packs)
    ]
    token_order = (
        (tok_rank ^ jnp.arange(packs, dtype=jnp.int32))[:, None] * pack_len + within[None, :]
    ).reshape(-1)
    order = (token_row.reshape(-1, 1) == token_order[None, :]).astype(jnp.bfloat16)
    tokens_last = dot_f32(jnp.concatenate(gathered, axis=0), order, COLS_BY_COLS).astype(
        jnp.bfloat16
    )
    attended = line_scatter(attended_parts)
    late_hidden, *every_pack = lax.optimization_barrier((hidden_bf, *every_pack))
    stitch_grad = outer_summed(tokens_last, every_pack)
    attended = line_total(*attended)
    layer_out = (late_hidden.astype(jnp.float32) + attended).astype(jnp.bfloat16)
    return (layer_out, stitch_grad)


def body(
    source, row_token, seg_ids, stitch_weight, norm_gain, q_weight, kv_weight, o_weight, out_grad
):
    tok_rank = lax.axis_index("tok")
    tp_rank = lax.axis_index("tp")
    packs = lax.axis_size("tok")
    pack_len = seg_ids.shape[1]
    width = q_weight.shape[0]
    own_cols = stitch_weight.shape[1]
    own_gain = lax.dynamic_slice_in_dim(norm_gain, tp_rank * own_cols, own_cols)

    gathered = lax.all_gather(source, "tp", axis=0, tiled=True)
    placed = stitched(packs, pack_len, tok_rank, row_token, gathered, stitch_weight)
    within = jnp.arange(pack_len, dtype=jnp.int32)
    hidden = placed[0].astype(jnp.float32)
    for distance in range(1, packs):
        hidden += swapped(placed[distance], "tok", distance).astype(jnp.float32)
    hidden_bf = hidden.astype(jnp.bfloat16)
    hidden_f = hidden_bf.astype(jnp.float32)
    square_sum = summed(jnp.sum(hidden_f * hidden_f, axis=1), "tp")
    inv_rms = lax.rsqrt(square_sum / width + epsilon)[:, None]
    gained = lax.all_gather((hidden_f * own_gain).astype(jnp.bfloat16), "tp", axis=1, tiled=True)

    token_order = (
        (tok_rank ^ jnp.arange(packs, dtype=jnp.int32))[:, None] * pack_len + within[None, :]
    ).reshape(-1)
    order = (row_token[:, None] == token_order[None, :]).astype(jnp.bfloat16)
    tokens_last = dot_f32(gathered, order, COLS_BY_COLS).astype(jnp.bfloat16)

    seg_row = seg_ids[0]
    earlier = jnp.sum((seg_row[None, :] < seg_row[:, None]).astype(jnp.int32), axis=1)
    angles = (within - earlier).astype(jnp.float32)[:, None] * frequencies()[None, :]
    cosine, sine = jnp.cos(angles), jnp.sin(angles)
    cosines = jnp.concatenate([cosine, cosine], axis=1)
    sines = jnp.concatenate([-sine, sine], axis=1)
    local_heads = q_weight.shape[1] // HD
    kv_cols = kv_weight.shape[1]
    paired = kv_cols == HD
    kv_local = 1 if paired else kv_cols // (2 * HD)
    repeat = local_heads // kv_local
    every_grad = lax.all_gather(out_grad, "tp", axis=1, tiled=True)
    grad_context = lax.dot_general(
        every_grad, o_weight, (((1,), (1,)), ((), ())), preferred_element_type=jnp.float32
    ).astype(jnp.bfloat16)
    if paired:
        query_pre = jnp.dot(gained, q_weight, preferred_element_type=jnp.float32)
        projected = jnp.dot(gained, kv_weight, preferred_element_type=jnp.float32) * inv_rms
        is_key = tp_rank % 2 == 0
        own_part = jnp.where(is_key, rotate(projected, cosine, sine), projected).astype(
            jnp.bfloat16
        )
        partner = swapped(own_part, "tp", 1)
        keys = jnp.where(is_key, own_part, partner)
        values = jnp.where(is_key, partner, own_part)
        context, grad_queries, key_part, value_part, aligned = attention_parts(
            repeat, query_pre, inv_rms, cosines, sines, seg_row, keys, values, grad_context
        )
        outgoing = jnp.where(is_key, value_part, key_part)
        incoming = swapped(outgoing.astype(jnp.bfloat16), "tp", 1).astype(outgoing.dtype)
        own_sum = jnp.where(is_key, key_part, value_part) + incoming
        grad_pairs = jnp.where(is_key, unrotate(own_sum, cosine, sine), own_sum).astype(
            jnp.bfloat16
        )
        aligned += jnp.sum(grad_pairs.astype(jnp.float32) * projected, axis=1, keepdims=True)
        grad_normed = back_projected(grad_queries, grad_pairs, q_weight, kv_weight)
    else:
        context, aligned, grad_normed = middle(
            repeat, gained, q_weight, kv_weight, inv_rms, cosines, sines, seg_row, grad_context
        )
    aligned = summed(aligned[:, 0], "tp")[:, None]
    grad_sum = lax.psum_scatter(grad_normed, "tp", scatter_dimension=1, tiled=True)
    attended = jnp.dot(context, o_weight, preferred_element_type=jnp.float32).astype(jnp.bfloat16)
    attended, grad_sum = lax.optimization_barrier((attended, grad_sum))
    grad_hidden = (
        out_grad.astype(jnp.float32)
        + inv_rms * own_gain * grad_sum.astype(jnp.float32)
        - hidden_f * (inv_rms * inv_rms * aligned / width)
    ).astype(jnp.bfloat16)
    every_pack = [grad_hidden] + [
        swapped(grad_hidden, "tok", distance) for distance in range(1, packs)
    ]
    late_hidden, *every_pack = lax.optimization_barrier((hidden_bf, *every_pack))
    stitch_grad = outer_summed(tokens_last, every_pack)

    attended = lax.psum_scatter(attended, "tp", scatter_dimension=1, tiled=True)
    layer_out = (late_hidden.astype(jnp.float32) + attended.astype(jnp.float32)).astype(
        jnp.bfloat16
    )
    return (layer_out, stitch_grad)


def solution(mesh):
    placed = (
        P("tp", "tok"),
        P(),
        P("tok", None),
        P("tok", "tp"),
        P(),
        P(None, "tp"),
        P(None, "tp"),
        P("tp", None),
        P("tok", "tp"),
    )
    on_line = mesh.shape["tp"] == 8
    return jax.shard_map(
        line_body if on_line else body,
        mesh=mesh,
        in_specs=placed,
        out_specs=(P("tok", "tp"), P("tok", "tp")),
        check_vma=False,
    )
```

time: 340 us -> 314 us (0.924)
  matrix products: 92.5 us -> 6.54 us
  Pallas kernels: 0 us -> 72.3 us
  waiting for transfers between devices: 210 us -> 143 us
  starting transfers between devices: 6.08 us -> 56.8 us
  between operations: 14.6 us -> 1.46 us
  local copies, waits for them, and re-layouts: 9 us -> 17.3 us
  other arithmetic: 7.88 us -> 15.6 us
    all_gather x4 -> x0, waiting for transfers between devices: 122 us -> none  [the longest x1 50.7 us: body(): gathered = lax.all_gather(source, 'tp', axis=0, tiled=True)]
    ppermute x0 -> x20, waiting for transfers between devices: none -> 90.7 us  [along(): return lax.ppermute(value, 'tp', both)]
    dot_general x18 -> x1, matrix products: 92.5 us -> 6.54 us  [dot_f32(): lax.dot_general(left, right, dims, preferred_element_type=jnp.float32)]
    pallas_call x0 -> x5, Pallas kernels: none -> 72.3 us  [the longest x1 24.6 us: line_middle(): pl.pallas_call(functools.partial(line_middle_kernel, repeat), in_specs=[s...]
    reduce_scatter x2 -> x0, waiting for transfers between devices: 52 us -> none  [the longest x1 50.3 us: body(): lax.psum_scatter(grad_normed.astype(jnp.bfloat16), 'tp', scatter_dimensio...]
    ppermute x0 -> x20, starting transfers between devices: none -> 41.7 us  [along(): return lax.ppermute(value, 'tp', both)]
    ppermute x9 -> x29, waiting for transfers between devices: 34.4 us -> 52.3 us  [swapped(): return lax.ppermute(value, axis, pairs)]
    ppermute x9 -> x29, starting transfers between devices: 5.66 us -> 15.2 us  [swapped(): return lax.ppermute(value, axis, pairs)]
  transfers between devices with their start and end apart: 15 -> 49, of which waited for: 12 -> 16; matrix products, arithmetic and copies ran while one was open for 19% -> 10% of each run, Pallas kernels for 0% -> 12%
where the time goes in v2:
time: 314 us; the launch traced here: 313 us
  waiting for transfers between devices  143 us (46%)
  Pallas kernels  72.3 us (23%)
  starting transfers between devices  56.8 us (18%)
  local copies, waits for them, and re-layouts  17.3 us (6%)
  other arithmetic  15.6 us (5%)
  matrix products  6.54 us (2%)
    ppermute x20, waiting for transfers between devices, along(): return lax.ppermute(value, 'tp', both)  90.7 us
    ppermute x29, waiting for transfers between devices, swapped(): return lax.ppermute(value, axis, pairs)  52.3 us
    ppermute x20, starting transfers between devices, along(): return lax.ppermute(value, 'tp', both)  41.7 us
    pallas_call x1, Pallas kernels, line_middle(): pl.pallas_call(functools.partial(line_middle_kernel, repeat), in_specs=[s...  24.6 us
    ppermute x29, starting transfers between devices, swapped(): return lax.ppermute(value, axis, pairs)  15.2 us
    pallas_call x1, Pallas kernels, line_attended(): pl.pallas_call(line_attended_kernel, grid_spec=pltpu.PrefetchScalarGridSp...  13.8 us
    pallas_call x1, Pallas kernels, line_grad_context(): pl.pallas_call(line_grad_kernel, grid_spec=pltpu.PrefetchScalarGridSpec(n...  13.4 us
    unnamed x106, local copies, waits for them, and re-layouts  12.3 us
  transfers between devices with their start and end apart: 49, of which 16 were waited for; matrix products, arithmetic and copies ran while one was open for 10% of the time, Pallas kernels for 12%

profile of v2, /device:TPU:0, one launch (start us, length us, event | category | flops | bytes accessed | tf_op | source)
XLA Modules:
  0.0 312.9 jit_solution(15690906389853048461)
XLA Ops:
  0.6 4.1 %collective-permute-start = (bf16[128,2048]{1,0:T(8,128)(2,1)}, bf16[128,2048]{1,0:T(8,128)(2,1)S(1)}, u32[]{:S(2)}, u32[]{:S(2)}) collective-permute-start(bf16[128,2048]{1,0:T(8,128)(2,1)} %refs_0_), channel_id=1, source_target_pairs={{2,0},{3,1},{6,2},{7,3},{0,4},{1,5},{4,6},{5,7},{10,8},{11,9},{14,... | collective-permute-start | bytes 1572872 | tf_op jit(solution)/shard_map/ppermute | solution.py:352
  4.7 11.5 %collective-permute-done.refs_2_ = bf16[128,2048]{1,0:T(8,128)(2,1)S(1)} collective-permute-done((bf16[128,2048]{1,0:T(8,128)(2,1)}, bf16[128,2048]{1,0:T(8,128)(2,1)S(1)}, u32[]{:S(2)}, u32[]{:S(2)}) %collective-permute-start) | collective-permute-done | bytes 524320 | tf_op jit(solution)/shard_map/ppermute | solution.py:352
  18.2 5.1 %collective-permute-start.3 = (bf16[128,2048]{1,0:T(8,128)(2,1)}, bf16[128,2048]{1,0:T(8,128)(2,1)S(1)}, u32[]{:S(2)}, u32[]{:S(2)}) collective-permute-start(bf16[128,2048]{1,0:T(8,128)(2,1)} %refs_0_), channel_id=1, source_target_pairs={{4,0},{5,1},{0,2},{1,3},{6,4},{7,5},{2,6},{3,7},{12,8},{13,9},{8,1... | collective-permute-start | bytes 1572872 | tf_op jit(solution)/shard_map/ppermute | solution.py:352
  23.9 21.4 %collective-permute-done.5 = bf16[128,2048]{1,0:T(8,128)(2,1)S(1)} collective-permute-done((bf16[128,2048]{1,0:T(8,128)(2,1)S(1)}, bf16[128,2048]{1,0:T(8,128)(2,1)S(1)}, u32[]{:S(2)}, u32[]{:S(2)}) %collective-permute-start.5) | collective-permute-done | bytes 524320 | tf_op jit(solution)/shard_map/ppermute | solution.py:352
  49.2 11.5 %shard_map.122 = (bf16[256,1024]{1,0:T(8,128)(2,1)}, bf16[256,1024]{1,0:T(8,128)(2,1)}, bf16[256,1024]{1,0:T(8,128)(2,1)}, bf16[256,1024]{1,0:T(8,128)(2,1)}) custom-call(s32[1]{0:T(128)} %bitcast.rank_ref, s32[1,1024]{1,0:T(1,128)} %bitcast.16, bf16[2048,1024]{1,0:T(8,128)(2,1)} %weight_ref.3, bf16[128,2048]{1,0:T(8,128)(2,1)} %refs_0_, ...), custom_call_target="tpu_custom_call" | custom-call | tf_op jit(solution)/shard_map/pallas_call | solution.py:428
  64.3 11.5 %collective-permute-done.8 = bf16[256,1024]{1,0:T(8,128)(2,1)S(1)} collective-permute-done((bf16[256,1024]{1,0:T(8,128)(2,1)}, bf16[256,1024]{1,0:T(8,128)(2,1)S(1)}, u32[]{:S(2)}, u32[]{:S(2)}) %collective-permute-start.8) | collective-permute-done | bytes 524320 | tf_op jit(solution)/shard_map/ppermute | solution.py:19
  75.7 11.7 %collective-permute-done.9 = bf16[256,1024]{1,0:T(8,128)(2,1)S(1)} collective-permute-done((bf16[256,1024]{1,0:T(8,128)(2,1)}, bf16[256,1024]{1,0:T(8,128)(2,1)S(1)}, u32[]{:S(2)}, u32[]{:S(2)}) %collective-permute-start.9) | collective-permute-done | bytes 524320 | tf_op jit(solution)/shard_map/ppermute | solution.py:19
  89.7 3.3 %collective-permute-start.14 = (bf16[256,1024]{1,0:T(8,128)(2,1)S(1)}, bf16[256,1024]{1,0:T(8,128)(2,1)S(1)}, u32[]{:S(2)}, u32[]{:S(2)}) collective-permute-start(bf16[256,1024]{1,0:T(8,128)(2,1)S(1)} %copy-done.7), channel_id=1, source_target_pairs={{4,0},{5,1},{0,2},{1,3},{6,4},{7,5},{2,6},{3,7},{12,8},{13,9},{8,1... | collective-permute-start | bytes 1572872 | tf_op jit(solution)/shard_map/ppermute | solution.py:352
  94.3 9.6 %collective-permute-done.19.refs_2_ = bf16[256,1024]{1,0:T(8,128)(2,1)} collective-permute-done((bf16[256,1024]{1,0:T(8,128)(2,1)S(1)}, bf16[256,1024]{1,0:T(8,128)(2,1)}, u32[]{:S(2)}, u32[]{:S(2)}) %collective-permute-start.19) | collective-permute-done | bytes 524320 | tf_op jit(solution)/shard_map/ppermute | solution.py:352
  106.0 18.4 %collective-permute-done.14.refs_4_ = bf16[256,1024]{1,0:T(8,128)(2,1)S(1)} collective-permute-done((bf16[256,1024]{1,0:T(8,128)(2,1)S(1)}, bf16[256,1024]{1,0:T(8,128)(2,1)S(1)}, u32[]{:S(2)}, u32[]{:S(2)}) %collective-permute-start.14) | collective-permute-done | bytes 524320 | tf_op jit(solution)/shard_map/ppermute | solution.py:352
  124.4 1.9 collective-permute-done.16
  127.9 9.0 %collective-permute-start.22 = (bf16[256,1024]{1,0:T(8,128)(2,1)S(1)}, bf16[256,1024]{1,0:T(8,128)(2,1)}, u32[]{:S(2)}, u32[]{:S(2)}) collective-permute-start(bf16[256,1024]{1,0:T(8,128)(2,1)S(1)} %add_convert_fusion.7.refs_0_), channel_id=1, source_target_pairs={{4,0},{5,1},{0,2},{1,3},{6,4},{7,5},{2,6},{3,7},{12,8},{13,9},{8,1... | collective-permute-start | bytes 1572872 | tf_op jit(solution)/shard_map/ppermute | solution.py:352
  143.4 6.5 %collective-permute-done.22.refs_4_ = bf16[256,1024]{1,0:T(8,128)(2,1)} collective-permute-done((bf16[256,1024]{1,0:T(8,128)(2,1)S(1)}, bf16[256,1024]{1,0:T(8,128)(2,1)}, u32[]{:S(2)}, u32[]{:S(2)}) %collective-permute-start.22) | collective-permute-done | bytes 524320 | tf_op jit(solution)/shard_map/ppermute | solution.py:352
  152.1 13.4 %shard_map.123.grad_ref = bf16[256,1024]{1,0:T(8,128)(2,1)} custom-call(s32[8]{0:T(128)} %reshape.106.ranks_ref.from_ref, bf16[1024,8192]{1,0:T(8,128)(2,1)} %weight_ref.5, bf16[256,1024]{1,0:T(8,128)(2,1)} %refs_0_.1, bf16[256,1024]{1,0:T(8,128)(2,1)} %copy-done.26, bf16[256,1024]{1,0:T(8,128)(2,1)} %copy-done.23, bf16[256,1024]{1,0:T(8,128)(2,1)} %copy-done.27, ...), custom_call_target="tpu_custom_call" | custom-call | tf_op jit(solution)/shard_map/pallas_call | solution.py:464
  167.0 24.6 %shard_map.124 = (bf16[256,1024]{1,0:T(8,128)(2,1)}, f32[256,1]{1,0:T(8,128)}, f32[256,1]{1,0:T(8,128)}, bf16[256,1024]{1,0:T(8,128)(2,1)}, bf16[256,1024]{1,0:T...) custom-call(s32[8]{0:T(128)} %reshape.106.ranks_ref.from_ref, ...), custom_call_target="tpu_custom_call" | custom-call | tf_op jit(solution)/shard_map/pallas_call | solution.py:595
  195.2 3.9 %collective-permute-start.36 = (bf16[256,1024]{1,0:T(8,128)(2,1)S(1)}, bf16[256,1024]{1,0:T(8,128)(2,1)}, u32[]{:S(2)}, u32[]{:S(2)}) collective-permute-start(bf16[256,1024]{1,0:T(8,128)(2,1)S(1)} %add_convert_fusion.6), channel_id=1, source_target_pairs={{0,2},{1,3},{6,4},{7,5},{8,10},{9,11},{14,12},{15,13},{16,18},{17,... | collective-permute-start | bytes 1572872 | tf_op jit(solution)/shard_map/ppermute | solution.py:352
  199.2 2.0 copy-done.45
  205.2 5.4 %collective-permute-done.36 = bf16[256,1024]{1,0:T(8,128)(2,1)} collective-permute-done((bf16[256,1024]{1,0:T(8,128)(2,1)S(1)}, bf16[256,1024]{1,0:T(8,128)(2,1)}, u32[]{:S(2)}, u32[]{:S(2)}) %collective-permute-start.36) | collective-permute-done | bytes 524320 | tf_op jit(solution)/shard_map/ppermute | solution.py:352
  212.2 2.9 collective-permute-start.37
  215.0 1.9 constant_dynamic-update-slice_fusion.4
  217.9 14.6 %collective-permute-done.28 = f32[256]{0:T(256)S(1)} collective-permute-done((f32[256]{0:T(256)S(1)}, f32[256]{0:T(256)S(1)}, u32[]{:S(2)}, u32[]{:S(2)}) %collective-permute-start.28) | collective-permute-done | bytes 1056 | tf_op jit(solution)/shard_map/ppermute | solution.py:19
  232.5 3.2 %collective-permute-start.29 = (f32[256]{0:T(256)S(1)}, f32[256]{0:T(256)S(1)}, u32[]{:S(2)}, u32[]{:S(2)}) collective-permute-start(f32[256]{0:T(256)S(1)} %add.172), channel_id=1, source_target_pairs={{0,4},{1,5},{2,6},{3,7},{4,0},{5,1},{6,2},{7,3},{8,12},{9,13},{10,... | collective-permute-start | bytes 3080 | tf_op jit(solution)/shard_map/ppermute | solution.py:19
  236.6 1.9 collective-permute-done.29
  238.5 13.8 %shard_map.125 = (bf16[256,1024]{1,0:T(8,128)(2,1)}, bf16[256,1024]{1,0:T(8,128)(2,1)}, bf16[256,1024]{1,0:T(8,128)(2,1)}, bf16[256,1024]{1,0:T(8,128)(2,1)}, bf...) custom-call(s32[8]{0:T(128)} %reshape.107.to_ref.ranks_ref, ...), custom_call_target="tpu_custom_call" | custom-call | tf_op jit(solution)/shard_map/pallas_call | solution.py:495
  257.1 2.9 collective-permute-start.47
  264.3 7.5 %collective-permute-done.47 = bf16[256,1024]{1,0:T(8,128)(2,1)S(1)} collective-permute-done((bf16[256,1024]{1,0:T(8,128)(2,1)S(1)}, bf16[256,1024]{1,0:T(8,128)(2,1)S(1)}, u32[]{:S(2)}, u32[]{:S(2)}) %collective-permute-start.47) | collective-permute-done | bytes 524320 | tf_op jit(solution)/shard_map/ppermute | solution.py:352
  272.8 3.5 %collective-permute-done.40.refs_4_ = bf16[256,1024]{1,0:T(8,128)(2,1)S(1)} collective-permute-done((bf16[256,1024]{1,0:T(8,128)(2,1)S(1)}, bf16[256,1024]{1,0:T(8,128)(2,1)S(1)}, u32[]{:S(2)}, u32[]{:S(2)}) %collective-permute-start.40) | collective-permute-done | bytes 524320 | tf_op jit(solution)/shard_map/ppermute | solution.py:19
  276.2 1.8 collective-permute-start.45
  278.0 8.6 %collective-permute-done.39.refs_3_ = bf16[256,1024]{1,0:T(8,128)(2,1)S(1)} collective-permute-done((bf16[256,1024]{1,0:T(8,128)(2,1)S(1)}, bf16[256,1024]{1,0:T(8,128)(2,1)S(1)}, u32[]{:S(2)}, u32[]{:S(2)}) %collective-permute-start.39) | collective-permute-done | bytes 524320 | tf_op jit(solution)/shard_map/ppermute | solution.py:19
  286.6 6.5 %fusion.2.refs_0_ = bf16[2048,1024]{1,0:T(8,128)(2,1)} fusion(bf16[1024,2048]{1,0:T(8,128)(2,1)S(1)} %copy-done.46, s32[1024]{0:T(1024)S(1)} %bitcast.21, s32[1024]{0:T(1024)S(1)} %bitcast.17), kind=kOutput, calls=%fused_computation.3 | convolution fusion | flops 4298113024 | bytes 8396800 | tf_op jit(solution)/shard_map/dot_general | solution.py:64
  294.0 9.0 %shard_map.126 = f32[2048,1024]{1,0:T(8,128)} custom-call(bf16[2048,1024]{1,0:T(8,128)(2,1)} %fusion.2.refs_0_, bf16[256,1024]{1,0:T(8,128)(2,1)} %copy-done.9, bf16[256,1024]{1,0:T(8,128)(2,1)} %copy-done.36, bf16[256,1024]{1,0:T(8,128)(2,1)} %copy-done.35, bf16[256,1024]{1,0:T(8,128)(2,1)} %copy-done.34), custom_call_target="tpu_custom_call" | custom-call | tf_op jit(solution)/shard_map/pallas_call | solution.py:336
  303.1 8.5 %collective-permute-done.48 = bf16[256,1024]{1,0:T(8,128)(2,1)S(1)} collective-permute-done((bf16[256,1024]{1,0:T(8,128)(2,1)S(1)}, bf16[256,1024]{1,0:T(8,128)(2,1)S(1)}, u32[]{:S(2)}, u32[]{:S(2)}) %collective-permute-start.48) | collective-permute-done | bytes 524320 | tf_op jit(solution)/shard_map/ppermute | solution.py:352
  (216 shorter events, 50.1 us)
Async XLA Ops:
  16.9 28.3 %collective-permute-start.5 = (bf16[128,2048]{1,0:T(8,128)(2,1)S(1)}, bf16[128,2048]{1,0:T(8,128)(2,1)S(1)}, u32[]{:S(2)}, u32[]{:S(2)}) collective-permute-start(bf16[128,2048]{1,0:T(8,128)(2,1)S(1)} %collective-permute-done.refs_2_), channel_id=1, source_target_pairs={{4,6},{5,7},{2,0},{3,1},{12,14},{13,15},{10,8},{11,9},{20,22},{21,... | collective-permute-start | bytes 1572872 | tf_op jit(solution)/shard_map/ppermute | solution.py:352
  18.2 27.3 %collective-permute-start.3 = (bf16[128,2048]{1,0:T(8,128)(2,1)}, bf16[128,2048]{1,0:T(8,128)(2,1)S(1)}, u32[]{:S(2)}, u32[]{:S(2)}) collective-permute-start(bf16[128,2048]{1,0:T(8,128)(2,1)} %refs_0_), channel_id=1, source_target_pairs={{4,0},{5,1},{0,2},{1,3},{6,4},{7,5},{2,6},{3,7},{12,8},{13,9},{8,1... | collective-permute-start | bytes 1572872 | tf_op jit(solution)/shard_map/ppermute | solution.py:352
  23.4 24.7 %collective-permute-start.1 = (bf16[128,2048]{1,0:T(8,128)(2,1)}, bf16[128,2048]{1,0:T(8,128)(2,1)S(1)}, u32[]{:S(2)}, u32[]{:S(2)}) collective-permute-start(bf16[128,2048]{1,0:T(8,128)(2,1)} %refs_0_), channel_id=1, source_target_pairs={{0,1},{1,0},{2,3},{3,2},{4,5},{5,4},{6,7},{7,6},{8,9},{9,8},{10,11... | collective-permute-start | bytes 1572872 | tf_op jit(solution)/shard_map/ppermute | solution.py:19
  23.4 24.7 %collective-permute-start.2 = (bf16[128,2048]{1,0:T(8,128)(2,1)S(1)}, bf16[128,2048]{1,0:T(8,128)(2,1)}, u32[]{:S(2)}, u32[]{:S(2)}) collective-permute-start(bf16[128,2048]{1,0:T(8,128)(2,1)S(1)} %collective-permute-done.refs_2_), channel_id=1, source_target_pairs={{0,1},{1,0},{2,3},{3,2},{4,5},{5,4},{6,7},{7,6},{8,9},{9,8},{10,11... | collective-permute-start | bytes 1572872 | tf_op jit(solution)/shard_map/ppermute | solution.py:19
  62.3 25.2 %collective-permute-start.9 = (bf16[256,1024]{1,0:T(8,128)(2,1)}, bf16[256,1024]{1,0:T(8,128)(2,1)S(1)}, u32[]{:S(2)}, u32[]{:S(2)}) collective-permute-start(bf16[256,1024]{1,0:T(8,128)(2,1)} %get-tuple-element.54), channel_id=1, source_target_pairs={{0,16},{8,24},{16,0},{24,8},{1,17},{9,25},{17,1},{25,9},{2,18},{10... | collective-permute-start | bytes 1572872 | tf_op jit(solution)/shard_map/ppermute | solution.py:19
  63.8 23.7 %collective-permute-start.10 = (bf16[256,1024]{1,0:T(8,128)(2,1)}, bf16[256,1024]{1,0:T(8,128)(2,1)S(1)}, u32[]{:S(2)}, u32[]{:S(2)}) collective-permute-start(bf16[256,1024]{1,0:T(8,128)(2,1)} %get-tuple-element.55), channel_id=1, source_target_pairs={{0,24},{8,16},{16,8},{24,0},{1,25},{9,17},{17,9},{25,1},{2,26},{10... | collective-permute-start | bytes 1572872 | tf_op jit(solution)/shard_map/ppermute | solution.py:19
  64.3 24.7 %collective-permute-start.11 = (bf16[256,1024]{1,0:T(8,128)(2,1)S(1)}, bf16[256,1024]{1,0:T(8,128)(2,1)S(1)}, u32[]{:S(2)}, u32[]{:S(2)}) collective-permute-start(bf16[256,1024]{1,0:T(8,128)(2,1)S(1)} %copy-done.7), channel_id=1, source_target_pairs={{2,0},{3,1},{6,2},{7,3},{0,4},{1,5},{4,6},{5,7},{10,8},{11,9},{14,... | collective-permute-start | bytes 1572872 | tf_op jit(solution)/shard_map/ppermute | solution.py:352
  88.9 16.9 %collective-permute-start.17 = (bf16[256,1024]{1,0:T(8,128)(2,1)S(1)}, bf16[256,1024]{1,0:T(8,128)(2,1)S(1)}, u32[]{:S(2)}, u32[]{:S(2)}) collective-permute-start(bf16[256,1024]{1,0:T(8,128)(2,1)S(1)} %copy-done.7), channel_id=1, source_target_pairs={{2,4},{3,5},{4,2},{5,3},{10,12},{11,13},{12,10},{13,11},{18,20},{1... | collective-permute-start | bytes 1572872 | tf_op jit(solution)/shard_map/ppermute | solution.py:352
  89.7 34.7 %collective-permute-start.14 = (bf16[256,1024]{1,0:T(8,128)(2,1)S(1)}, bf16[256,1024]{1,0:T(8,128)(2,1)S(1)}, u32[]{:S(2)}, u32[]{:S(2)}) collective-permute-start(bf16[256,1024]{1,0:T(8,128)(2,1)S(1)} %copy-done.7), channel_id=1, source_target_pairs={{4,0},{5,1},{0,2},{1,3},{6,4},{7,5},{2,6},{3,7},{12,8},{13,9},{8,1... | collective-permute-start | bytes 1572872 | tf_op jit(solution)/shard_map/ppermute | solution.py:352
  93.0 33.3 %collective-permute-start.16 = (bf16[256,1024]{1,0:T(8,128)(2,1)S(1)}, bf16[256,1024]{1,0:T(8,128)(2,1)S(1)}, u32[]{:S(2)}, u32[]{:S(2)}) collective-permute-start(bf16[256,1024]{1,0:T(8,128)(2,1)S(1)} %collective-permute-done.11.refs_2_), channel_id=1, source_target_pairs={{4,6},{5,7},{2,0},{3,1},{12,14},{13,15},{10,8},{11,9},{20,22},{21,... | collective-permute-start | bytes 1572872 | tf_op jit(solution)/shard_map/ppermute | solution.py:352
  103.9 22.4 %collective-permute-start.25 = (bf16[256,1024]{1,0:T(8,128)(2,1)S(1)}, bf16[256,1024]{1,0:T(8,128)(2,1)S(1)}, u32[]{:S(2)}, u32[]{:S(2)}) collective-permute-start(bf16[256,1024]{1,0:T(8,128)(2,1)S(1)} %add_convert_fusion.7.refs_0_), channel_id=1, source_target_pairs={{2,4},{3,5},{4,2},{5,3},{10,12},{11,13},{12,10},{13,11},{18,20},{1... | collective-permute-start | bytes 1572872 | tf_op jit(solution)/shard_map/ppermute | solution.py:352
  104.6 36.2 %collective-permute-start.24 = (bf16[256,1024]{1,0:T(8,128)(2,1)}, bf16[256,1024]{1,0:T(8,128)(2,1)}, u32[]{:S(2)}, u32[]{:S(2)}) collective-permute-start(bf16[256,1024]{1,0:T(8,128)(2,1)} %collective-permute-done.19.refs_2_), channel_id=1, source_target_pairs={{4,6},{5,7},{2,0},{3,1},{12,14},{13,15},{10,8},{11,9},{20,22},{21,... | collective-permute-start | bytes 1572872 | tf_op jit(solution)/shard_map/ppermute | solution.py:352
  105.9 36.5 %collective-permute-start.12 = (bf16[256,1024]{1,0:T(8,128)(2,1)S(1)}, bf16[256,1024]{1,0:T(8,128)(2,1)S(1)}, u32[]{:S(2)}, u32[]{:S(2)}) collective-permute-start(bf16[256,1024]{1,0:T(8,128)(2,1)S(1)} %copy-done.7), channel_id=1, source_target_pairs={{0,1},{1,0},{2,3},{3,2},{4,5},{5,4},{6,7},{7,6},{8,9},{9,8},{10,11... | collective-permute-start | bytes 1572872 | tf_op jit(solution)/shard_map/ppermute | solution.py:19
  124.4 18.5 %collective-permute-start.13 = (bf16[256,1024]{1,0:T(8,128)(2,1)S(1)}, bf16[256,1024]{1,0:T(8,128)(2,1)S(1)}, u32[]{:S(2)}, u32[]{:S(2)}) collective-permute-start(bf16[256,1024]{1,0:T(8,128)(2,1)S(1)} %collective-permute-done.11.refs_2_), channel_id=1, source_target_pairs={{0,1},{1,0},{2,3},{3,2},{4,5},{5,4},{6,7},{7,6},{8,9},{9,8},{10,11... | collective-permute-start | bytes 1572872 | tf_op jit(solution)/shard_map/ppermute | solution.py:19
  126.2 16.7 %collective-permute-start.15 = (bf16[256,1024]{1,0:T(8,128)(2,1)S(1)}, bf16[256,1024]{1,0:T(8,128)(2,1)}, u32[]{:S(2)}, u32[]{:S(2)}) collective-permute-start(bf16[256,1024]{1,0:T(8,128)(2,1)S(1)} %collective-permute-done.14.refs_4_), channel_id=1, source_target_pairs={{0,1},{1,0},{2,3},{3,2},{4,5},{5,4},{6,7},{7,6},{8,9},{9,8},{10,11... | collective-permute-start | bytes 1572872 | tf_op jit(solution)/shard_map/ppermute | solution.py:19
  127.9 22.0 %collective-permute-start.22 = (bf16[256,1024]{1,0:T(8,128)(2,1)S(1)}, bf16[256,1024]{1,0:T(8,128)(2,1)}, u32[]{:S(2)}, u32[]{:S(2)}) collective-permute-start(bf16[256,1024]{1,0:T(8,128)(2,1)S(1)} %add_convert_fusion.7.refs_0_), channel_id=1, source_target_pairs={{4,0},{5,1},{0,2},{1,3},{6,4},{7,5},{2,6},{3,7},{12,8},{13,9},{8,1... | collective-permute-start | bytes 1572872 | tf_op jit(solution)/shard_map/ppermute | solution.py:352
  140.8 24.8 %collective-permute-start.20 = (bf16[256,1024]{1,0:T(8,128)(2,1)S(1)}, bf16[256,1024]{1,0:T(8,128)(2,1)S(1)}, u32[]{:S(2)}, u32[]{:S(2)}) collective-permute-start(bf16[256,1024]{1,0:T(8,128)(2,1)S(1)} %add_convert_fusion.7.refs_0_), channel_id=1, source_target_pairs={{0,1},{1,0},{2,3},{3,2},{4,5},{5,4},{6,7},{7,6},{8,9},{9,8},{10,11... | collective-permute-start | bytes 1572872 | tf_op jit(solution)/shard_map/ppermute | solution.py:19
  142.8 22.8 %collective-permute-start.21 = (bf16[256,1024]{1,0:T(8,128)(2,1)}, bf16[256,1024]{1,0:T(8,128)(2,1)S(1)}, u32[]{:S(2)}, u32[]{:S(2)}) collective-permute-start(bf16[256,1024]{1,0:T(8,128)(2,1)} %collective-permute-done.19.refs_2_), channel_id=1, source_target_pairs={{0,1},{1,0},{2,3},{3,2},{4,5},{5,4},{6,7},{7,6},{8,9},{9,8},{10,11... | collective-permute-start | bytes 1572872 | tf_op jit(solution)/shard_map/ppermute | solution.py:19
  143.0 22.7 %collective-permute-start.26 = (bf16[256,1024]{1,0:T(8,128)(2,1)S(1)}, bf16[256,1024]{1,0:T(8,128)(2,1)S(1)}, u32[]{:S(2)}, u32[]{:S(2)}) collective-permute-start(bf16[256,1024]{1,0:T(8,128)(2,1)S(1)} %add.169.refs_6_), channel_id=1, source_target_pairs={{0,1},{1,0},{2,3},{3,2},{4,5},{5,4},{6,7},{7,6},{8,9},{9,8},{10,11... | collective-permute-start | bytes 1572872 | tf_op jit(solution)/shard_map/ppermute | solution.py:19
  149.9 15.7 %collective-permute-start.23 = (bf16[256,1024]{1,0:T(8,128)(2,1)}, bf16[256,1024]{1,0:T(8,128)(2,1)S(1)}, u32[]{:S(2)}, u32[]{:S(2)}) collective-permute-start(bf16[256,1024]{1,0:T(8,128)(2,1)} %collective-permute-done.22.refs_4_), channel_id=1, source_target_pairs={{0,1},{1,0},{2,3},{3,2},{4,5},{5,4},{6,7},{7,6},{8,9},{9,8},{10,11... | collective-permute-start | bytes 1572872 | tf_op jit(solution)/shard_map/ppermute | solution.py:19
  201.4 50.9 %collective-permute-start.30 = (bf16[256,1024]{1,0:T(8,128)(2,1)}, bf16[256,1024]{1,0:T(8,128)(2,1)S(1)}, u32[]{:S(2)}, u32[]{:S(2)}) collective-permute-start(bf16[256,1024]{1,0:T(8,128)(2,1)} %get-tuple-element.74), channel_id=1, source_target_pairs={{0,1},{1,0},{2,3},{3,2},{4,5},{5,4},{6,7},{7,6},{8,9},{9,8},{10,11... | collective-permute-start | bytes 1572872 | tf_op jit(solution)/shard_map/ppermute | solution.py:19
  201.9 50.5 %collective-permute-start.32 = (bf16[256,1024]{1,0:T(8,128)(2,1)S(1)}, bf16[256,1024]{1,0:T(8,128)(2,1)S(1)}, u32[]{:S(2)}, u32[]{:S(2)}) collective-permute-start(bf16[256,1024]{1,0:T(8,128)(2,1)S(1)} %add_convert_fusion.6), channel_id=1, source_target_pairs={{2,4},{3,5},{4,2},{5,3},{10,12},{11,13},{12,10},{13,11},{18,20},{1... | collective-permute-start | bytes 1572872 | tf_op jit(solution)/shard_map/ppermute | solution.py:352
  203.8 48.5 %collective-permute-start.34 = (bf16[256,1024]{1,0:T(8,128)(2,1)S(1)}, bf16[256,1024]{1,0:T(8,128)(2,1)S(1)}, u32[]{:S(2)}, u32[]{:S(2)}) collective-permute-start(bf16[256,1024]{1,0:T(8,128)(2,1)S(1)} %add_convert_fusion.5), channel_id=1, source_target_pairs={{0,4},{1,5},{2,0},{3,1},{4,6},{5,7},{6,2},{7,3},{8,12},{9,13},{10,... | collective-permute-start | bytes 1572872 | tf_op jit(solution)/shard_map/ppermute | solution.py:352
  212.2 40.2 %collective-permute-start.37 = (bf16[256,1024]{1,0:T(8,128)(2,1)S(1)}, bf16[256,1024]{1,0:T(8,128)(2,1)S(1)}, u32[]{:S(2)}, u32[]{:S(2)}) collective-permute-start(bf16[256,1024]{1,0:T(8,128)(2,1)S(1)} %add_convert_fusion.4), channel_id=1, source_target_pairs={{0,2},{1,3},{2,6},{3,7},{4,0},{5,1},{6,4},{7,5},{8,10},{9,11},{10,... | collective-permute-start | bytes 1572872 | tf_op jit(solution)/shard_map/ppermute | solution.py:352
  216.9 15.6 %collective-permute-start.28 = (f32[256]{0:T(256)S(1)}, f32[256]{0:T(256)S(1)}, u32[]{:S(2)}, u32[]{:S(2)}) collective-permute-start(f32[256]{0:T(256)S(1)} %add.171), channel_id=1, source_target_pairs={{0,2},{1,3},{2,0},{3,1},{4,6},{5,7},{6,4},{7,5},{8,10},{9,11},{10,... | collective-permute-start | bytes 3080 | tf_op jit(solution)/shard_map/ppermute | solution.py:19
  260.4 15.8 %collective-permute-start.40 = (bf16[256,1024]{1,0:T(8,128)(2,1)S(1)}, bf16[256,1024]{1,0:T(8,128)(2,1)S(1)}, u32[]{:S(2)}, u32[]{:S(2)}) collective-permute-start(bf16[256,1024]{1,0:T(8,128)(2,1)S(1)} %subtract_convert_fusion.refs_1_), channel_id=1, source_target_pairs={{0,24},{8,16},{16,8},{24,0},{1,25},{9,17},{17,9},{25,1},{2,26},{10... | collective-permute-start | bytes 1572872 | tf_op jit(solution)/shard_map/ppermute | solution.py:19
  261.9 24.7 %collective-permute-start.39 = (bf16[256,1024]{1,0:T(8,128)(2,1)S(1)}, bf16[256,1024]{1,0:T(8,128)(2,1)S(1)}, u32[]{:S(2)}, u32[]{:S(2)}) collective-permute-start(bf16[256,1024]{1,0:T(8,128)(2,1)S(1)} %subtract_convert_fusion.refs_1_), channel_id=1, source_target_pairs={{0,16},{8,24},{16,0},{24,8},{1,17},{9,25},{17,1},{25,9},{2,18},{10... | collective-permute-start | bytes 1572872 | tf_op jit(solution)/shard_map/ppermute | solution.py:19
  263.4 29.8 %collective-permute-start.38 = (bf16[256,1024]{1,0:T(8,128)(2,1)S(1)}, bf16[256,1024]{1,0:T(8,128)(2,1)S(1)}, u32[]{:S(2)}, u32[]{:S(2)}) collective-permute-start(bf16[256,1024]{1,0:T(8,128)(2,1)S(1)} %subtract_convert_fusion.refs_1_), channel_id=1, source_target_pairs={{0,8},{8,0},{16,24},{24,16},{1,9},{9,1},{17,25},{25,17},{2,10},{10... | collective-permute-start | bytes 1572872 | tf_op jit(solution)/shard_map/ppermute | solution.py:19
  264.2 38.8 %collective-permute-start.41 = (bf16[256,1024]{1,0:T(8,128)(2,1)}, bf16[256,1024]{1,0:T(8,128)(2,1)S(1)}, u32[]{:S(2)}, u32[]{:S(2)}) collective-permute-start(bf16[256,1024]{1,0:T(8,128)(2,1)} %get-tuple-element.85), channel_id=1, source_target_pairs={{0,1},{1,0},{2,3},{3,2},{4,5},{5,4},{6,7},{7,6},{8,9},{9,8},{10,11... | collective-permute-start | bytes 1572872 | tf_op jit(solution)/shard_map/ppermute | solution.py:19
  271.8 31.3 %collective-permute-start.43 = (bf16[256,1024]{1,0:T(8,128)(2,1)S(1)}, bf16[256,1024]{1,0:T(8,128)(2,1)S(1)}, u32[]{:S(2)}, u32[]{:S(2)}) collective-permute-start(bf16[256,1024]{1,0:T(8,128)(2,1)S(1)} %add_convert_fusion.3), channel_id=1, source_target_pairs={{2,4},{3,5},{4,2},{5,3},{10,12},{11,13},{12,10},{13,11},{18,20},{1... | collective-permute-start | bytes 1572872 | tf_op jit(solution)/shard_map/ppermute | solution.py:352
  276.2 26.8 %collective-permute-start.45 = (bf16[256,1024]{1,0:T(8,128)(2,1)S(1)}, bf16[256,1024]{1,0:T(8,128)(2,1)S(1)}, u32[]{:S(2)}, u32[]{:S(2)}) collective-permute-start(bf16[256,1024]{1,0:T(8,128)(2,1)S(1)} %add_convert_fusion.2), channel_id=1, source_target_pairs={{0,4},{1,5},{2,0},{3,1},{4,6},{5,7},{6,2},{7,3},{8,12},{9,13},{10,... | collective-permute-start | bytes 1572872 | tf_op jit(solution)/shard_map/ppermute | solution.py:352
  286.6 24.9 %collective-permute-start.48 = (bf16[256,1024]{1,0:T(8,128)(2,1)S(1)}, bf16[256,1024]{1,0:T(8,128)(2,1)S(1)}, u32[]{:S(2)}, u32[]{:S(2)}) collective-permute-start(bf16[256,1024]{1,0:T(8,128)(2,1)S(1)} %add_convert_fusion.1), channel_id=1, source_target_pairs={{0,2},{1,3},{2,6},{3,7},{4,0},{5,1},{6,4},{7,5},{8,10},{9,11},{10,... | collective-permute-start | bytes 1572872 | tf_op jit(solution)/shard_map/ppermute | solution.py:352
  (66 other events, 1012.9 us)

commit v3 on v2

--- a/solution.py
+++ b/solution.py
@@ -344,7 +344,7 @@
     )(features, *grads)
 
 
-FIRST, SECOND, LAST = (1, 3, 0, 2), (2, 0, 3, 1), (3, 2, 1, 0)
+STAY, FIRST, SECOND, LAST = (0, 1, 2, 3), (1, 3, 0, 2), (2, 0, 3, 1), (3, 2, 1, 0)
 
 
 def along(value, pairs):
@@ -365,18 +365,25 @@
     return value, done
 
 
-def line_gather(block):
-    beside = swapped(block, "tp", 1)
-    first = along(block, arriving(FIRST))
-    block, first = after(block, first)
+def gather_begun(block):
+    return along(block, arriving(FIRST))
+
+
+def gather_rest(block, first):
     far = along(first, [(2, 3), (1, 0)])
     second = along(block, arriving(SECOND))
     near = along(block, [(1, 2), (2, 1)])
+    return far, second, near
+
+
+def early_blocks(block, first):
+    return [block, swapped(block, "tp", 1), first, swapped(first, "tp", 1)]
+
+
+def late_blocks(rest):
+    far, second, near = rest
     last = far + near
-    blocks = [block, beside]
-    for own in (first, second, last):
-        blocks += [own, swapped(own, "tp", 1)]
-    return blocks
+    return [second, swapped(second, "tp", 1), last, swapped(last, "tp", 1)]
 
 
 def line_scatter(parts):
@@ -398,122 +405,179 @@
     return own + second.astype(jnp.float32) + first.astype(jnp.float32)
 
 
-def line_stitch_kernel(packs, rank_ref, token_ref, weight_ref, *refs):
-    blocks, out_refs = refs[:8], refs[8 : 8 + packs]
-    rows, product, sems = refs[8 + packs :]
-    block = rows.shape[0] // 8
+def line_stitch_half(blocks, rows, rows_ref, weight_ref, product, here, sems, out_sem):
+    block = blocks[0].shape[0]
     fetches = [
         pltpu.make_async_copy(blocks[i], rows.at[pl.ds(i * block, block)], sems.at[i])
-        for i in range(8)
+        for i in range(4)
     ]
     for fetch in fetches:
         fetch.start()
-    for half in range(2):
-        here = pl.ds(half * 4 * block, 4 * block)
-        for fetch in fetches[half * 4 : half * 4 + 4]:
-            fetch.wait()
-        product[here, :] = dot_f32(rows[here, :], weight_ref[...]).astype(jnp.bfloat16)
+    for fetch in fetches:
+        fetch.wait()
+    kept = pltpu.make_async_copy(rows, rows_ref, out_sem)
+    kept.start()
+    product[here, :] = dot_f32(rows[...], weight_ref[...]).astype(jnp.bfloat16)
+    return kept
+
+
+def line_stitch_early_kernel(weight_ref, *refs):
+    blocks, (product_ref, rows_ref, rows, sems, out_sem) = refs[:4], refs[4:]
+    everything = pl.ds(0, rows.shape[0])
+    line_stitch_half(
+        blocks, rows, rows_ref, weight_ref, product_ref, everything, sems, out_sem
+    ).wait()
+
+
+def line_stitch_kernel(packs, rank_ref, token_ref, weight_ref, early_ref, *refs):
+    blocks, out_refs = refs[:4], refs[4 : 4 + packs]
+    rows_ref, rows, product, sems, out_sem = refs[4 + packs :]
+    half = rows.shape[0]
+    kept = line_stitch_half(
+        blocks, rows, rows_ref, weight_ref, product, pl.ds(half, half), sems, out_sem
+    )
+    product[pl.ds(0, half), :] = early_ref[...]
     pack_len = out_refs[0].shape[0]
     place = token_ref[...] - lax.broadcasted_iota(jnp.int32, (pack_len, product.shape[0]), 0)
     for distance in range(packs):
         first = (rank_ref[0] ^ distance) * pack_len
         chosen = (place == first).astype(jnp.float32).astype(jnp.bfloat16)
         out_refs[distance][...] = dot_f32(chosen, product[...]).astype(jnp.bfloat16)
-
-
-def line_stitched(packs, pack_len, rank, token_row, blocks, weight):
+    kept.wait()
+
+
+def line_stitched_early(blocks, weight):
     block, features = blocks[0].shape
     cols = weight.shape[1]
     whole, far = pl.BlockSpec(memory_space=pltpu.VMEM), pl.BlockSpec(memory_space=pl.ANY)
     return pl.pallas_call(
+        line_stitch_early_kernel,
+        in_specs=[whole] + [far] * 4,
+        out_specs=[whole, far],
+        out_shape=[
+            jax.ShapeDtypeStruct((4 * block, cols), jnp.bfloat16),
+            jax.ShapeDtypeStruct((4 * block, features), jnp.bfloat16),
+        ],
+        scratch_shapes=[
+            pltpu.VMEM((4 * block, features), jnp.bfloat16),
+            pltpu.SemaphoreType.DMA((4,)),
+            pltpu.SemaphoreType.DMA,
+        ],
+        compiler_params=pltpu.CompilerParams(vmem_limit_bytes=VMEM_LIMIT),
+    )(weight, *blocks)
+
+
+def line_stitched(packs, pack_len, rank, token_row, early, blocks, weight):
+    block, features = blocks[0].shape
+    cols = weight.shape[1]
+    whole, far = pl.BlockSpec(memory_space=pltpu.VMEM), pl.BlockSpec(memory_space=pl.ANY)
+    results = pl.pallas_call(
         functools.partial(line_stitch_kernel, packs),
-        in_specs=[pl.BlockSpec(memory_space=pltpu.SMEM), whole, whole] + [far] * 8,
-        out_specs=[whole] * packs,
-        out_shape=[jax.ShapeDtypeStruct((pack_len, cols), jnp.bfloat16)] * packs,
+        in_specs=[pl.BlockSpec(memory_space=pltpu.SMEM)] + [whole] * 3 + [far] * 4,
+        out_specs=[whole] * packs + [far],
+        out_shape=[jax.ShapeDtypeStruct((pack_len, cols), jnp.bfloat16)] * packs
+        + [jax.ShapeDtypeStruct((4 * block, features), jnp.bfloat16)],
         scratch_shapes=[
-            pltpu.VMEM((8 * block, features), jnp.bfloat16),
+            pltpu.VMEM((4 * block, features), jnp.bfloat16),
             pltpu.VMEM((8 * block, cols), jnp.bfloat16),
-            pltpu.SemaphoreType.DMA((8,)),
-        ],
-        compiler_params=pltpu.CompilerParams(vmem_limit_bytes=VMEM_LIMIT),
-    )(rank.reshape(1), token_row, weight, *blocks)
-
-
-def line_grad_kernel(ranks_ref, weight_ref, *refs):
+            pltpu.SemaphoreType.DMA((4,)),
+            pltpu.SemaphoreType.DMA,
+        ],
+        compiler_params=pltpu.CompilerParams(vmem_limit_bytes=VMEM_LIMIT),
+    )(rank.reshape(1), token_row, weight, early, *blocks)
+    return results[:packs], results[packs]
+
+
+def line_grad_kernel(chips_ref, core_ref, weight_ref, *refs):
     blocks, out_ref, features, total, sems = refs[:8], *refs[8:]
     step = pl.program_id(0)
+    cols = blocks[0].shape[1]
+
+    def fetch(place, half):
+        core = core_ref[0] if half == 0 else 1 - core_ref[0]
+        there = features.at[place, :, pl.ds(pl.multiple_of(core * cols, cols), cols)]
+        return there, sems.at[place, half]
 
     @pl.when(step == 0)
     def _():
         for i in range(8):
-            pltpu.make_async_copy(blocks[i], features.at[i], sems.at[i]).start()
+            pltpu.make_async_copy(blocks[i], *fetch(i // 2, i % 2)).start()
         total[...] = jnp.zeros_like(total)
 
-    pltpu.make_async_copy(blocks[0], features.at[step], sems.at[step]).wait()
+    for half in range(2):
+        pltpu.make_async_copy(blocks[half], *fetch(step, half)).wait()
     total[...] += dot_f32(features[step], weight_ref[...], ROWS_BY_ROWS)
 
-    @pl.when(step == 7)
+    @pl.when(step == 3)
     def _():
         out_ref[...] = total[...].astype(out_ref.dtype)
 
 
-def line_grad_context(ranks, blocks, weight):
+def line_grad_context(chips, core, blocks, weight):
     rows, cols = blocks[0].shape
     heads_cols = weight.shape[0]
     far = pl.BlockSpec(memory_space=pl.ANY)
     return pl.pallas_call(
         line_grad_kernel,
         grid_spec=pltpu.PrefetchScalarGridSpec(
-            num_scalar_prefetch=1,
-            grid=(8,),
-            in_specs=[pl.BlockSpec((heads_cols, cols), lambda i, ranks: (0, ranks[i]))] + [far] * 8,
-            out_specs=pl.BlockSpec((rows, heads_cols), lambda i, ranks: (0, 0)),
+            num_scalar_prefetch=2,
+            grid=(4,),
+            in_specs=[pl.BlockSpec((heads_cols, 2 * cols), lambda i, chips, core: (0, chips[i]))]
+            + [far] * 8,
+            out_specs=pl.BlockSpec((rows, heads_cols), lambda i, chips, core: (0, 0)),
             scratch_shapes=[
-                pltpu.VMEM((8, rows, cols), jnp.bfloat16),
+                pltpu.VMEM((4, rows, 2 * cols), jnp.bfloat16),
                 pltpu.VMEM((rows, heads_cols), jnp.float32),
-                pltpu.SemaphoreType.DMA((8,)),
+                pltpu.SemaphoreType.DMA((4, 2)),
             ],
         ),
         out_shape=jax.ShapeDtypeStruct((rows, heads_cols), jnp.bfloat16),
         compiler_params=pltpu.CompilerParams(vmem_limit_bytes=VMEM_LIMIT),
-    )(ranks, weight, *blocks)
-
-
-def line_attended_kernel(ranks_ref, context_ref, weight_ref, *out_refs):
+    )(chips, core.reshape(1), weight, *blocks)
+
+
+def line_attended_kernel(chips_ref, core_ref, context_ref, weight_ref, *refs):
+    out_refs, product = refs[:8], refs[8]
     step = pl.program_id(0)
-    product = dot_f32(context_ref[...], weight_ref[...]).astype(jnp.bfloat16)
-    for i in range(8):
+    cols = out_refs[0].shape[1]
+    product[...] = dot_f32(context_ref[...], weight_ref[...]).astype(jnp.bfloat16)
+    for i in range(4):
 
         @pl.when(step == i)
         def _(i=i):
-            out_refs[i][...] = product
-
-
-def line_attended(ranks, context, weight):
+            for half in range(2):
+                core = core_ref[0] if half == 0 else 1 - core_ref[0]
+                here = pl.ds(pl.multiple_of(core * cols, cols), cols)
+                out_refs[2 * i + half][...] = product[:, here]
+
+
+def line_attended(chips, core, context, weight):
     rows, heads_cols = context.shape
     cols = weight.shape[1] // 8
+    fixed = lambda i, chips, core: (0, 0)
     return pl.pallas_call(
         line_attended_kernel,
         grid_spec=pltpu.PrefetchScalarGridSpec(
-            num_scalar_prefetch=1,
-            grid=(8,),
+            num_scalar_prefetch=2,
+            grid=(4,),
             in_specs=[
-                pl.BlockSpec((rows, heads_cols), lambda i, ranks: (0, 0)),
-                pl.BlockSpec((heads_cols, cols), lambda i, ranks: (0, ranks[i])),
+                pl.BlockSpec((rows, heads_cols), fixed),
+                pl.BlockSpec((heads_cols, 2 * cols), lambda i, chips, core: (0, chips[i])),
             ],
-            out_specs=[pl.BlockSpec((rows, cols), lambda i, ranks: (0, 0))] * 8,
+            out_specs=[pl.BlockSpec((rows, cols), fixed)] * 8,
+            scratch_shapes=[pltpu.VMEM((rows, 2 * cols), jnp.bfloat16)],
         ),
         out_shape=[jax.ShapeDtypeStruct((rows, cols), jnp.bfloat16)] * 8,
         compiler_params=pltpu.CompilerParams(vmem_limit_bytes=VMEM_LIMIT),
-    )(ranks, context, weight)
+    )(chips, core.reshape(1), context, weight)
 
 
 def line_middle_kernel(
     repeat, from_ref, to_ref, gain_ref, cos_ref, sin_ref, seg_row_ref, seg_col_ref, grad_ref,
     q_weight_ref, kv_weight_ref, *refs,
 ):
-    blocks, (context_ref, aligned_ref, scale_ref), out_refs = refs[:8], refs[8:11], refs[11:19]
-    hidden, q_weight, kv_weight, out, query_sum, pair_sum, query_grad, sems, out_sems = refs[19:]
+    blocks, context_ref, out_refs = refs[:8], refs[8], refs[9:17]
+    hidden, q_weight, kv_weight, out, query_sum, pair_sum, query_grad, sems, out_sems = refs[17:]
     width = q_weight.shape[0]
     rows, step = blocks[0].shape
 
@@ -548,7 +612,6 @@
 
     squares = lax.fori_loop(0, 8, project, jnp.zeros((rows, 1), jnp.float32))
     row_scale = lax.rsqrt(squares / width + epsilon)
-    scale_ref[...] = row_scale
     cosines, sines = cos_ref[...], sin_ref[...]
     groups = kv_weight.shape[1] // (2 * HD)
     pair_plain = pair_sum[...] * row_scale
@@ -564,15 +627,17 @@
         pair_grads.append(value_part.astype(jnp.bfloat16))
     for half, pair_grad in zip(halves, pair_grads):
         aligned += half * pair_grad.astype(jnp.float32)
-    aligned_ref[...] = jnp.sum(aligned, axis=1, keepdims=True)
+    aligned = jnp.sum(aligned, axis=1, keepdims=True) * (row_scale * row_scale / width)
     pair_grad = jnp.concatenate(pair_grads, axis=1)
 
     @pl.loop(0, 8)
     def _(place):
         span = part(to_ref[place])
+        grad_normed = dot_f32(query_grad[...], q_weight[span, :], ROWS_BY_ROWS)
+        grad_normed += dot_f32(pair_grad, kv_weight[span, :], ROWS_BY_ROWS)
+        features = hidden[6 - 2 * (place // 2) + place % 2].astype(jnp.float32)
         out[place] = (
-            dot_f32(query_grad[...], q_weight[span, :], ROWS_BY_ROWS)
-            + dot_f32(pair_grad, kv_weight[span, :], ROWS_BY_ROWS)
+            grad_normed * (row_scale * gain_ref[:, span]) - features * aligned
         ).astype(out.dtype)
         for i in range(8):
 
@@ -595,12 +660,8 @@
     results = pl.pallas_call(
         functools.partial(line_middle_kernel, repeat),
         in_specs=[scalars] * 2 + [whole] * 6 + [far] * 10,
-        out_specs=[whole] * 3 + [far] * 8,
-        out_shape=[
-            jax.ShapeDtypeStruct((rows, heads_cols), jnp.bfloat16),
-            jax.ShapeDtypeStruct((rows, 1), jnp.float32),
-            jax.ShapeDtypeStruct((rows, 1), jnp.float32),
-        ]
+        out_specs=[whole] + [far] * 8,
+        out_shape=[jax.ShapeDtypeStruct((rows, heads_cols), jnp.bfloat16)]
         + [jax.ShapeDtypeStruct((rows, step), jnp.bfloat16)] * 8,
         scratch_shapes=[
             pltpu.VMEM((8, rows, step), jnp.bfloat16),
@@ -618,7 +679,7 @@
         sources, targets, gain[None, :], cosines, sines, seg_row[None, :], seg_row[:, None],
         context_grad, q_weight, kv_weight, *blocks,
     )
-    return results[0], results[1], results[2], results[3:]
+    return results[0], results[1:]
 
 
 def line_body(
@@ -631,15 +692,17 @@
     width = q_weight.shape[0]
     own_cols = stitch_weight.shape[1]
     repeat = (q_weight.shape[1] // HD) // (kv_weight.shape[1] // (2 * HD))
-    own_gain = lax.dynamic_slice_in_dim(norm_gain, tp_rank * own_cols, own_cols)
     chip, core = tp_rank // 2, tp_rank % 2
 
+    def chips(tables):
+        return jnp.array(tables, jnp.int32)[:, chip]
+
     def ranks(tables):
-        chips = jnp.array(tables, jnp.int32)[:, chip]
-        return jnp.stack([2 * chips + core, 2 * chips + 1 - core], axis=1).reshape(-1)
-
-    stay = (0, 1, 2, 3)
-    sources, targets = ranks((stay, FIRST, SECOND, LAST)), ranks((LAST, SECOND, FIRST, stay))
+        pairs = 2 * chips(tables)
+        return jnp.stack([pairs + core, pairs + 1 - core], axis=1).reshape(-1)
+
+    arrival, departure = (STAY, FIRST, SECOND, LAST), (LAST, SECOND, FIRST, STAY)
+    sources, targets = ranks(arrival), ranks(departure)
 
     within = jnp.arange(pack_len, dtype=jnp.int32)
     seg_row = seg_ids[0]
@@ -649,33 +712,42 @@
     cosines = jnp.concatenate([cosine, cosine], axis=1)
     sines = jnp.concatenate([-sine, sine], axis=1)
 
-    gathered = line_gather(source)
     token_row = row_token.reshape(8, -1)[sources].reshape(1, -1)
-    late_grad, gathered[-2] = after(out_grad, gathered[-2])
-    grad_blocks = line_gather(late_grad)
-    placed = line_stitched(packs, pack_len, tok_rank, token_row, gathered, stitch_weight)
+    first = gather_begun(source)
+    source, (first, token_row) = after(source, (first, token_row))
+    rest = gather_rest(source, first)
+    early_source = early_blocks(source, first)
+    early_product, early_rows = line_stitched_early(early_source, stitch_weight)
+    out_grad, (rest, early_product) = after(out_grad, (rest, early_product))
+    late_source = late_blocks(rest)
+    grad_first = gather_begun(out_grad)
+    placed, late_rows = line_stitched(
+        packs, pack_len, tok_rank, token_row, early_product, late_source, stitch_weight
+    )
+    received = [swapped(placed[distance], "tok", distance) for distance in range(1, packs)]
+    received[0], grad_first = after(received[0], grad_first)
+    grad_rest = gather_rest(out_grad, grad_first)
     hidden = placed[0].astype(jnp.float32)
-    for distance in range(1, packs):
-        hidden += swapped(placed[distance], "tok", distance).astype(jnp.float32)
+    for part in received:
+        hidden += part.astype(jnp.float32)
     hidden_bf = hidden.astype(jnp.bfloat16)
-    hidden_f = hidden_bf.astype(jnp.float32)
-    hidden_blocks = line_gather(hidden_bf)
-    grad_context = line_grad_context(sources, grad_blocks, o_weight)
-
-    context, aligned, inv_rms, grad_parts = line_middle(
+    hidden_first = gather_begun(hidden_bf)
+    (hidden_bf, hidden_first), grad_rest = after((hidden_bf, hidden_first), grad_rest)
+    hidden_rest = gather_rest(hidden_bf, hidden_first)
+    grad_blocks = early_blocks(out_grad, grad_first) + late_blocks(grad_rest)
+    grad_context = line_grad_context(chips(arrival), core, grad_blocks, o_weight)
+    hidden_rest, grad_context = after(hidden_rest, grad_context)
+    hidden_blocks = early_blocks(hidden_bf, hidden_first) + late_blocks(hidden_rest)
+
+    context, grad_parts = line_middle(
         repeat, sources, targets, hidden_blocks, norm_gain, q_weight, kv_weight, cosines, sines,
         seg_row, grad_context,
     )
     grad_own, grad_second, grad_first = line_scatter(grad_parts)
-    aligned = summed(aligned[:, 0], "tp")
-    context, aligned = after(context, aligned)
-    attended_parts = line_attended(targets, context, o_weight)
-    grad_sum = line_total(grad_own, grad_second, grad_first)
-    attended_parts, grad_sum = after(attended_parts, grad_sum)
+    attended_parts = line_attended(chips(departure), core, context, o_weight)
+    attended_parts, grad_second = after(attended_parts, grad_second)
     grad_hidden = (
-        out_grad.astype(jnp.float32)
-        + inv_rms * own_gain * grad_sum
-        - hidden_f * (inv_rms * inv_rms * aligned[:, None] / width)
+        out_grad.astype(jnp.float32) + line_total(grad_own, grad_second, grad_first)
     ).astype(jnp.bfloat16)
     every_pack = [grad_hidden] + [
         swapped(grad_hidden, "tok", distance) for distance in range(1, packs)
@@ -684,9 +756,11 @@
         (tok_rank ^ jnp.arange(packs, dtype=jnp.int32))[:, None] * pack_len + within[None, :]
     ).reshape(-1)
     order = (token_row.reshape(-1, 1) == token_order[None, :]).astype(jnp.bfloat16)
-    tokens_last = dot_f32(jnp.concatenate(gathered, axis=0), order, COLS_BY_COLS).astype(
-        jnp.bfloat16
-    )
+    half = early_rows.shape[0]
+    tokens_last = (
+        dot_f32(early_rows, order[:half], COLS_BY_COLS)
+        + dot_f32(late_rows, order[half:], COLS_BY_COLS)
+    ).astype(jnp.bfloat16)
     attended = line_scatter(attended_parts)
     late_hidden, *every_pack = lax.optimization_barrier((hidden_bf, *every_pack))
     stitch_grad = outer_summed(tokens_last, every_pack)

time: 314 us -> 271 us (0.86)
  waiting for transfers between devices: 143 us -> 111 us
  local copies, waits for them, and re-layouts: 17.3 us -> 8.43 us
    ppermute x20, waiting for transfers between devices: 90.7 us -> 67.6 us  [along(): return lax.ppermute(value, 'tp', both)]
    ppermute x29 -> x26, waiting for transfers between devices: 52.3 us -> 43.9 us  [swapped(): return lax.ppermute(value, axis, pairs)]
    unnamed x106 -> x81, local copies, waits for them, and re-layouts: 12.3 us -> 4.95 us
    pallas_call x0 -> x1, Pallas kernels: none -> 7.03 us  [line_stitched_early(): pl.pallas_call(line_stitch_early_kernel, in_specs=[whole] + [far] * 4, ou...]
    ppermute x29 -> x26, starting transfers between devices: 15.2 us -> 12.1 us  [swapped(): return lax.ppermute(value, axis, pairs)]
    dot_general x1 -> x2, matrix products: 6.54 us -> 7.32 us  [dot_f32(): lax.dot_general(left, right, dims, preferred_element_type=jnp.float32)]
  transfers between devices with their start and end apart: 49 -> 46, of which waited for: 16 -> 16; matrix products, arithmetic and copies ran while one was open for 10% -> 8% of each run, Pallas kernels for 12% -> 18%
where the time goes in v3:
time: 271 us; the launch traced here: 270 us
  waiting for transfers between devices  111 us (41%)
  Pallas kernels  73.8 us (27%)
  starting transfers between devices  54.4 us (20%)
  other arithmetic  13.2 us (5%)
  local copies, waits for them, and re-layouts  8.43 us (3%)
  matrix products  7.32 us (3%)
    ppermute x20, waiting for transfers between devices, along(): return lax.ppermute(value, 'tp', both)  67.6 us
    ppermute x26, waiting for transfers between devices, swapped(): return lax.ppermute(value, axis, pairs)  43.9 us
    ppermute x20, starting transfers between devices, along(): return lax.ppermute(value, 'tp', both)  42.3 us
    pallas_call x1, Pallas kernels, line_middle(): pl.pallas_call(functools.partial(line_middle_kernel, repeat), in_specs=[s...  24.5 us
    ppermute x26, starting transfers between devices, swapped(): return lax.ppermute(value, axis, pairs)  12.1 us
    pallas_call x1, Pallas kernels, line_grad_context(): pl.pallas_call(line_grad_kernel, grid_spec=pltpu.PrefetchScalarGridSpec(n...  11.8 us
    pallas_call x1, Pallas kernels, line_attended(): pl.pallas_call(line_attended_kernel, grid_spec=pltpu.PrefetchScalarGridSp...  11.6 us
    pallas_call x1, Pallas kernels, line_stitched(): pl.pallas_call(functools.partial(line_stitch_kernel, packs), in_specs=[pl...  9.9 us
  transfers between devices with their start and end apart: 46, of which 16 were waited for; matrix products, arithmetic and copies ran while one was open for 8% of the time, Pallas kernels for 18%

profile of v3, /device:TPU:0, one launch (start us, length us, event | category | flops | bytes accessed | tf_op | source)
XLA Modules:
  0.0 269.9 jit_solution(14538770986523634437)
XLA Ops:
  0.7 4.1 %collective-permute-start = (bf16[128,2048]{1,0:T(8,128)(2,1)}, bf16[128,2048]{1,0:T(8,128)(2,1)S(1)}, u32[]{:S(2)}, u32[]{:S(2)}) collective-permute-start(bf16[128,2048]{1,0:T(8,128)(2,1)} %refs_0_), channel_id=1, source_target_pairs={{2,0},{3,1},{6,2},{7,3},{0,4},{1,5},{4,6},{5,7},{10,8},{11,9},{14,... | collective-permute-start | bytes 1572872 | tf_op jit(solution)/shard_map/ppermute | solution.py:352
  7.3 8.9 %collective-permute-done.refs_2_ = bf16[128,2048]{1,0:T(8,128)(2,1)S(1)} collective-permute-done((bf16[128,2048]{1,0:T(8,128)(2,1)}, bf16[128,2048]{1,0:T(8,128)(2,1)S(1)}, u32[]{:S(2)}, u32[]{:S(2)}) %collective-permute-start) | collective-permute-done | bytes 524320 | tf_op jit(solution)/shard_map/ppermute | solution.py:352
  18.7 6.4 %collective-permute-start.2 = (bf16[128,2048]{1,0:T(8,128)(2,1)}, bf16[128,2048]{1,0:T(8,128)(2,1)S(1)}, u32[]{:S(2)}, u32[]{:S(2)}) collective-permute-start(bf16[128,2048]{1,0:T(8,128)(2,1)} %refs_0_), channel_id=1, source_target_pairs={{4,0},{5,1},{0,2},{1,3},{6,4},{7,5},{2,6},{3,7},{12,8},{13,9},{8,1... | collective-permute-start | bytes 1572872 | tf_op jit(solution)/shard_map/ppermute | solution.py:352
  26.8 7.0 %shard_map.140 = (bf16[512,1024]{1,0:T(8,128)(2,1)}, bf16[512,2048]{1,0:T(8,128)(2,1)}) custom-call(bf16[2048,1024]{1,0:T(8,128)(2,1)} %weight_ref.5, bf16[128,2048]{1,0:T(8,128)(2,1)} %refs_0_, bf16[128,2048]{1,0:T(8,128)(2,1)} %copy-done.26, bf16[128,2048]{1,0:T(8,128)(2,1)} %copy-done.14, bf16[128,2048]{1,0:T(8,128)(2,1)} %copy-done.25), custom_call_target="tpu_custom_call" | custom-call | tf_op jit(solution)/shard_map/pallas_call | solution.py:453
  33.8 14.0 %collective-permute-done.2.refs_0_ = bf16[128,2048]{1,0:T(8,128)(2,1)S(1)} collective-permute-done((bf16[128,2048]{1,0:T(8,128)(2,1)}, bf16[128,2048]{1,0:T(8,128)(2,1)S(1)}, u32[]{:S(2)}, u32[]{:S(2)}) %collective-permute-start.2) | collective-permute-done | bytes 524320 | tf_op jit(solution)/shard_map/ppermute | solution.py:352
  51.5 9.9 %shard_map.141 = (bf16[256,1024]{1,0:T(8,128)(2,1)}, bf16[256,1024]{1,0:T(8,128)(2,1)}, bf16[256,1024]{1,0:T(8,128)(2,1)}, bf16[256,1024]{1,0:T(8,128)(2,1)}, bf16[512,2048]{1,0:T(8,128)(2,1)}) custom-call(s32[1]{0:T(128)} %bitcast.rank_ref, s32[1,1024]{1,0:T(1,128)} %bitcast.20, bf16[2048,1024]{1,0:T(8,128)(2,1)} %weight_ref.5, ...), custom_call_target="tpu_custom_call" | custom-call | tf_op jit(solution)/shard_map/pallas_call | solution.py:474
  61.4 1.6 collective-permute-start.8
  62.9 1.5 collective-permute-start.10
  65.6 3.1 %collective-permute-start.14 = (bf16[256,1024]{1,0:T(8,128)(2,1)S(1)}, bf16[256,1024]{1,0:T(8,128)(2,1)S(1)}, u32[]{:S(2)}, u32[]{:S(2)}) collective-permute-start(bf16[256,1024]{1,0:T(8,128)(2,1)S(1)} %copy-done.4), channel_id=1, source_target_pairs={{4,0},{5,1},{0,2},{1,3},{6,4},{7,5},{2,6},{3,7},{12,8},{13,9},{8,1... | collective-permute-start | bytes 1572872 | tf_op jit(solution)/shard_map/ppermute | solution.py:352
  68.7 7.7 %collective-permute-done.8 = bf16[256,1024]{1,0:T(8,128)(2,1)S(1)} collective-permute-done((bf16[256,1024]{1,0:T(8,128)(2,1)}, bf16[256,1024]{1,0:T(8,128)(2,1)S(1)}, u32[]{:S(2)}, u32[]{:S(2)}) %collective-permute-start.8) | collective-permute-done | bytes 524320 | tf_op jit(solution)/shard_map/ppermute | solution.py:19
  77.7 10.4 %collective-permute-done.10 = bf16[256,1024]{1,0:T(8,128)(2,1)S(1)} collective-permute-done((bf16[256,1024]{1,0:T(8,128)(2,1)}, bf16[256,1024]{1,0:T(8,128)(2,1)S(1)}, u32[]{:S(2)}, u32[]{:S(2)}) %collective-permute-start.10) | collective-permute-done | bytes 524320 | tf_op jit(solution)/shard_map/ppermute | solution.py:19
  88.1 1.4 add_convert_fusion.9.refs_0_
  91.0 11.0 %collective-permute-done.13 = bf16[256,1024]{1,0:T(8,128)(2,1)S(1)} collective-permute-done((bf16[256,1024]{1,0:T(8,128)(2,1)S(1)}, bf16[256,1024]{1,0:T(8,128)(2,1)S(1)}, u32[]{:S(2)}, u32[]{:S(2)}) %collective-permute-start.13) | collective-permute-done | bytes 524320 | tf_op jit(solution)/shard_map/ppermute | solution.py:352
  101.9 10.3 %collective-permute-done.12.refs_2_ = bf16[256,1024]{1,0:T(8,128)(2,1)} collective-permute-done((bf16[256,1024]{1,0:T(8,128)(2,1)S(1)}, bf16[256,1024]{1,0:T(8,128)(2,1)}, u32[]{:S(2)}, u32[]{:S(2)}) %collective-permute-start.12) | collective-permute-done | bytes 524320 | tf_op jit(solution)/shard_map/ppermute | solution.py:352
  115.9 6.2 %collective-permute-start.17 = (bf16[256,1024]{1,0:T(8,128)(2,1)S(1)}, bf16[256,1024]{1,0:T(8,128)(2,1)}, u32[]{:S(2)}, u32[]{:S(2)}) collective-permute-start(bf16[256,1024]{1,0:T(8,128)(2,1)S(1)} %add_convert_fusion.9.refs_0_), channel_id=1, source_target_pairs={{4,0},{5,1},{0,2},{1,3},{6,4},{7,5},{2,6},{3,7},{12,8},{13,9},{8,1... | collective-permute-start | bytes 1572872 | tf_op jit(solution)/shard_map/ppermute | solution.py:352
  126.3 11.8 %shard_map.142.grad_ref = bf16[256,1024]{1,0:T(8,128)(2,1)} custom-call(s32[4]{0:T(128)} %get-tuple-element.116.chips_ref, s32[1]{0:T(128)} %bitcast.8.core_ref, bf16[1024,8192]{1,0:T(8,128)(2,1)} %weight_ref.7, bf16[256,1024]{1,0:T(8,128)(2,1)} %refs_0_.1, bf16[256,1024]{1,0:T(8,128)(2,1)} %copy-done.16, bf16[256,1024]{1,0:T(8,128)(2,1)} %copy-done.11, ...), custom_call_target="tpu_custom_call" | custom-call | tf_op jit(solution)/shard_map/pallas_call | solution.py:520
  138.1 6.0 %collective-permute-done.17.refs_4_ = bf16[256,1024]{1,0:T(8,128)(2,1)} collective-permute-done((bf16[256,1024]{1,0:T(8,128)(2,1)S(1)}, bf16[256,1024]{1,0:T(8,128)(2,1)}, u32[]{:S(2)}, u32[]{:S(2)}) %collective-permute-start.17) | collective-permute-done | bytes 524320 | tf_op jit(solution)/shard_map/ppermute | solution.py:352
  149.0 24.5 %shard_map.143 = (bf16[256,1024]{1,0:T(8,128)(2,1)}, bf16[256,1024]{1,0:T(8,128)(2,1)}, bf16[256,1024]{1,0:T(8,128)(2,1)}, bf16[256,1024]{1,0:T(8,128)(2,1)}, bf...) custom-call(s32[8]{0:T(128)} %reshape.110.from_ref, ...), custom_call_target="tpu_custom_call" | custom-call | tf_op jit(solution)/shard_map/pallas_call | solution.py:660
  174.2 1.5 collective-permute-done.28
  176.9 1.4 collective-permute-start.33
  180.5 11.6 %shard_map.144 = (bf16[256,1024]{1,0:T(8,128)(2,1)}, bf16[256,1024]{1,0:T(8,128)(2,1)}, bf16[256,1024]{1,0:T(8,128)(2,1)}, bf16[256,1024]{1,0:T(8,128)(2,1)}, bf...) custom-call(s32[4]{0:T(128)} %get-tuple-element.120.chips_ref, ...), custom_call_target="tpu_custom_call" | custom-call | tf_op jit(solution)/shard_map/pallas_call | solution.py:558
  193.0 8.2 %collective-permute-done.31 = bf16[256,1024]{1,0:T(8,128)(2,1)S(1)} collective-permute-done((bf16[256,1024]{1,0:T(8,128)(2,1)S(1)}, bf16[256,1024]{1,0:T(8,128)(2,1)S(1)}, u32[]{:S(2)}, u32[]{:S(2)}) %collective-permute-start.31) | collective-permute-done | bytes 524320 | tf_op jit(solution)/shard_map/ppermute | solution.py:352
  201.5 3.6 %collective-permute-start.34 = (bf16[256,1024]{1,0:T(8,128)(2,1)S(1)}, bf16[256,1024]{1,0:T(8,128)(2,1)S(1)}, u32[]{:S(2)}, u32[]{:S(2)}) collective-permute-start(bf16[256,1024]{1,0:T(8,128)(2,1)S(1)} %add_convert_fusion.6), channel_id=1, source_target_pairs={{0,2},{1,3},{2,6},{3,7},{4,0},{5,1},{6,4},{7,5},{8,10},{9,11},{10,... | collective-permute-start | bytes 1572872 | tf_op jit(solution)/shard_map/ppermute | solution.py:352
  205.1 2.6 fusion
  208.8 9.0 %collective-permute-start.44 = (bf16[256,1024]{1,0:T(8,128)(2,1)S(1)}, bf16[256,1024]{1,0:T(8,128)(2,1)S(1)}, u32[]{:S(2)}, u32[]{:S(2)}) collective-permute-start(bf16[256,1024]{1,0:T(8,128)(2,1)S(1)} %add_convert_fusion.4), channel_id=1, source_target_pairs={{0,2},{1,3},{6,4},{7,5},{8,10},{9,11},{14,12},{15,13},{16,18},{17,... | collective-permute-start | bytes 1572872 | tf_op jit(solution)/shard_map/ppermute | solution.py:352
  217.8 8.7 %collective-permute-done.34 = bf16[256,1024]{1,0:T(8,128)(2,1)S(1)} collective-permute-done((bf16[256,1024]{1,0:T(8,128)(2,1)S(1)}, bf16[256,1024]{1,0:T(8,128)(2,1)S(1)}, u32[]{:S(2)}, u32[]{:S(2)}) %collective-permute-start.34) | collective-permute-done | bytes 524320 | tf_op jit(solution)/shard_map/ppermute | solution.py:352
  227.2 2.5 collective-permute-start.37
  232.0 11.0 %collective-permute-done.37.refs_4_ = bf16[256,1024]{1,0:T(8,128)(2,1)S(1)} collective-permute-done((bf16[256,1024]{1,0:T(8,128)(2,1)S(1)}, bf16[256,1024]{1,0:T(8,128)(2,1)S(1)}, u32[]{:S(2)}, u32[]{:S(2)}) %collective-permute-start.37) | collective-permute-done | bytes 524320 | tf_op jit(solution)/shard_map/ppermute | solution.py:19
  243.0 10.3 %collective-permute-done.36.refs_3_ = bf16[256,1024]{1,0:T(8,128)(2,1)S(1)} collective-permute-done((bf16[256,1024]{1,0:T(8,128)(2,1)S(1)}, bf16[256,1024]{1,0:T(8,128)(2,1)S(1)}, u32[]{:S(2)}, u32[]{:S(2)}) %collective-permute-start.36) | collective-permute-done | bytes 524320 | tf_op jit(solution)/shard_map/ppermute | solution.py:19
  253.3 4.8 %add_convert_fusion.refs_0_ = bf16[2048,1024]{1,0:T(8,128)(2,1)} fusion(f32[2048,1024]{1,0:T(8,128)S(1)} %fusion, bf16[512,2048]{1,0:T(8,128)(2,1)S(1)} %copy-done.35, pred[1024,1024]{1,0:T(32,128)(4,1)S(1)} %broadcast_compare_fusion), kind=kOutput, calls=%fused_computation.1 | convolution fusion | flops 2151677952 | bytes 15204352 | tf_op jit(solution)/shard_map/dot_general | solution.py:64
  258.9 9.0 %shard_map.145 = f32[2048,1024]{1,0:T(8,128)} custom-call(bf16[2048,1024]{1,0:T(8,128)(2,1)} %add_convert_fusion.refs_0_, bf16[256,1024]{1,0:T(8,128)(2,1)} %copy-done.7, bf16[256,1024]{1,0:T(8,128)(2,1)} %copy-done.22, bf16[256,1024]{1,0:T(8,128)(2,1)} %copy-done.21, bf16[256,1024]{1,0:T(8,128)(2,1)} %copy-done.19), custom_call_target="tpu_custom_call" | custom-call | tf_op jit(solution)/shard_map/pallas_call | solution.py:336
  268.4 1.4 add_convert_fusion.1
  (182 shorter events, 37.5 us)
Async XLA Ops:
  16.8 17.1 %collective-permute-start.1 = (bf16[128,2048]{1,0:T(8,128)(2,1)S(1)}, bf16[128,2048]{1,0:T(8,128)(2,1)S(1)}, u32[]{:S(2)}, u32[]{:S(2)}) collective-permute-start(bf16[128,2048]{1,0:T(8,128)(2,1)S(1)} %collective-permute-done.refs_2_), channel_id=1, source_target_pairs={{4,6},{5,7},{2,0},{3,1},{12,14},{13,15},{10,8},{11,9},{20,22},{21,... | collective-permute-start | bytes 1572872 | tf_op jit(solution)/shard_map/ppermute | solution.py:352
  18.0 15.8 %collective-permute-start.3 = (bf16[128,2048]{1,0:T(8,128)(2,1)}, bf16[128,2048]{1,0:T(8,128)(2,1)S(1)}, u32[]{:S(2)}, u32[]{:S(2)}) collective-permute-start(bf16[128,2048]{1,0:T(8,128)(2,1)} %refs_0_), channel_id=1, source_target_pairs={{2,4},{3,5},{4,2},{5,3},{10,12},{11,13},{12,10},{13,11},{18,20},{1... | collective-permute-start | bytes 1572872 | tf_op jit(solution)/shard_map/ppermute | solution.py:352
  18.7 29.1 %collective-permute-start.2 = (bf16[128,2048]{1,0:T(8,128)(2,1)}, bf16[128,2048]{1,0:T(8,128)(2,1)S(1)}, u32[]{:S(2)}, u32[]{:S(2)}) collective-permute-start(bf16[128,2048]{1,0:T(8,128)(2,1)} %refs_0_), channel_id=1, source_target_pairs={{4,0},{5,1},{0,2},{1,3},{6,4},{7,5},{2,6},{3,7},{12,8},{13,9},{8,1... | collective-permute-start | bytes 1572872 | tf_op jit(solution)/shard_map/ppermute | solution.py:352
  48.5 17.1 %collective-permute-start.9 = (bf16[256,1024]{1,0:T(8,128)(2,1)S(1)}, bf16[256,1024]{1,0:T(8,128)(2,1)S(1)}, u32[]{:S(2)}, u32[]{:S(2)}) collective-permute-start(bf16[256,1024]{1,0:T(8,128)(2,1)S(1)} %copy-done.4), channel_id=1, source_target_pairs={{2,0},{3,1},{6,2},{7,3},{0,4},{1,5},{4,6},{5,7},{10,8},{11,9},{14,... | collective-permute-start | bytes 1572872 | tf_op jit(solution)/shard_map/ppermute | solution.py:352
  62.9 25.1 %collective-permute-start.10 = (bf16[256,1024]{1,0:T(8,128)(2,1)}, bf16[256,1024]{1,0:T(8,128)(2,1)S(1)}, u32[]{:S(2)}, u32[]{:S(2)}) collective-permute-start(bf16[256,1024]{1,0:T(8,128)(2,1)} %get-tuple-element.71), channel_id=1, source_target_pairs={{0,16},{8,24},{16,0},{24,8},{1,17},{9,25},{17,1},{25,9},{2,18},{10... | collective-permute-start | bytes 1572872 | tf_op jit(solution)/shard_map/ppermute | solution.py:19
  64.4 23.6 %collective-permute-start.11 = (bf16[256,1024]{1,0:T(8,128)(2,1)}, bf16[256,1024]{1,0:T(8,128)(2,1)S(1)}, u32[]{:S(2)}, u32[]{:S(2)}) collective-permute-start(bf16[256,1024]{1,0:T(8,128)(2,1)} %get-tuple-element.72), channel_id=1, source_target_pairs={{0,24},{8,16},{16,8},{24,0},{1,25},{9,17},{17,9},{25,1},{2,26},{10... | collective-permute-start | bytes 1572872 | tf_op jit(solution)/shard_map/ppermute | solution.py:19
  64.9 25.5 %collective-permute-start.15 = (bf16[256,1024]{1,0:T(8,128)(2,1)S(1)}, bf16[256,1024]{1,0:T(8,128)(2,1)S(1)}, u32[]{:S(2)}, u32[]{:S(2)}) collective-permute-start(bf16[256,1024]{1,0:T(8,128)(2,1)S(1)} %copy-done.4), channel_id=1, source_target_pairs={{2,4},{3,5},{4,2},{5,3},{10,12},{11,13},{12,10},{13,11},{18,20},{1... | collective-permute-start | bytes 1572872 | tf_op jit(solution)/shard_map/ppermute | solution.py:352
  65.6 25.3 %collective-permute-start.14 = (bf16[256,1024]{1,0:T(8,128)(2,1)S(1)}, bf16[256,1024]{1,0:T(8,128)(2,1)S(1)}, u32[]{:S(2)}, u32[]{:S(2)}) collective-permute-start(bf16[256,1024]{1,0:T(8,128)(2,1)S(1)} %copy-done.4), channel_id=1, source_target_pairs={{4,0},{5,1},{0,2},{1,3},{6,4},{7,5},{2,6},{3,7},{12,8},{13,9},{8,1... | collective-permute-start | bytes 1572872 | tf_op jit(solution)/shard_map/ppermute | solution.py:352
  76.4 25.5 %collective-permute-start.13 = (bf16[256,1024]{1,0:T(8,128)(2,1)S(1)}, bf16[256,1024]{1,0:T(8,128)(2,1)S(1)}, u32[]{:S(2)}, u32[]{:S(2)}) collective-permute-start(bf16[256,1024]{1,0:T(8,128)(2,1)S(1)} %collective-permute-done.9.refs_2_), channel_id=1, source_target_pairs={{4,6},{5,7},{2,0},{3,1},{12,14},{13,15},{10,8},{11,9},{20,22},{21,... | collective-permute-start | bytes 1572872 | tf_op jit(solution)/shard_map/ppermute | solution.py:352
  89.5 22.7 %collective-permute-start.12 = (bf16[256,1024]{1,0:T(8,128)(2,1)S(1)}, bf16[256,1024]{1,0:T(8,128)(2,1)}, u32[]{:S(2)}, u32[]{:S(2)}) collective-permute-start(bf16[256,1024]{1,0:T(8,128)(2,1)S(1)} %add_convert_fusion.9.refs_0_), channel_id=1, source_target_pairs={{2,0},{3,1},{6,2},{7,3},{0,4},{1,5},{4,6},{5,7},{10,8},{11,9},{14,... | collective-permute-start | bytes 1572872 | tf_op jit(solution)/shard_map/ppermute | solution.py:352
  90.4 23.9 %collective-permute-start.19 = (bf16[256,1024]{1,0:T(8,128)(2,1)S(1)}, bf16[256,1024]{1,0:T(8,128)(2,1)S(1)}, u32[]{:S(2)}, u32[]{:S(2)}) collective-permute-start(bf16[256,1024]{1,0:T(8,128)(2,1)S(1)} %copy-done.4), channel_id=1, source_target_pairs={{0,1},{1,0},{2,3},{3,2},{4,5},{5,4},{6,7},{7,6},{8,9},{9,8},{10,11... | collective-permute-start | bytes 1572872 | tf_op jit(solution)/shard_map/ppermute | solution.py:19
  90.4 24.6 %collective-permute-start.20 = (bf16[256,1024]{1,0:T(8,128)(2,1)S(1)}, bf16[256,1024]{1,0:T(8,128)(2,1)S(1)}, u32[]{:S(2)}, u32[]{:S(2)}) collective-permute-start(bf16[256,1024]{1,0:T(8,128)(2,1)S(1)} %collective-permute-done.9.refs_2_), channel_id=1, source_target_pairs={{0,1},{1,0},{2,3},{3,2},{4,5},{5,4},{6,7},{7,6},{8,9},{9,8},{10,11... | collective-permute-start | bytes 1572872 | tf_op jit(solution)/shard_map/ppermute | solution.py:19
  113.0 25.0 %collective-permute-start.16 = (bf16[256,1024]{1,0:T(8,128)(2,1)}, bf16[256,1024]{1,0:T(8,128)(2,1)}, u32[]{:S(2)}, u32[]{:S(2)}) collective-permute-start(bf16[256,1024]{1,0:T(8,128)(2,1)} %collective-permute-done.12.refs_2_), channel_id=1, source_target_pairs={{4,6},{5,7},{2,0},{3,1},{12,14},{13,15},{10,8},{11,9},{20,22},{21,... | collective-permute-start | bytes 1572872 | tf_op jit(solution)/shard_map/ppermute | solution.py:352
  114.3 23.7 %collective-permute-start.18 = (bf16[256,1024]{1,0:T(8,128)(2,1)S(1)}, bf16[256,1024]{1,0:T(8,128)(2,1)S(1)}, u32[]{:S(2)}, u32[]{:S(2)}) collective-permute-start(bf16[256,1024]{1,0:T(8,128)(2,1)S(1)} %add_convert_fusion.9.refs_0_), channel_id=1, source_target_pairs={{2,4},{3,5},{4,2},{5,3},{10,12},{11,13},{12,10},{13,11},{18,20},{1... | collective-permute-start | bytes 1572872 | tf_op jit(solution)/shard_map/ppermute | solution.py:352
  115.9 28.1 %collective-permute-start.17 = (bf16[256,1024]{1,0:T(8,128)(2,1)S(1)}, bf16[256,1024]{1,0:T(8,128)(2,1)}, u32[]{:S(2)}, u32[]{:S(2)}) collective-permute-start(bf16[256,1024]{1,0:T(8,128)(2,1)S(1)} %add_convert_fusion.9.refs_0_), channel_id=1, source_target_pairs={{4,0},{5,1},{0,2},{1,3},{6,4},{7,5},{2,6},{3,7},{12,8},{13,9},{8,1... | collective-permute-start | bytes 1572872 | tf_op jit(solution)/shard_map/ppermute | solution.py:352
  125.7 21.6 %collective-permute-start.24 = (bf16[256,1024]{1,0:T(8,128)(2,1)}, bf16[256,1024]{1,0:T(8,128)(2,1)S(1)}, u32[]{:S(2)}, u32[]{:S(2)}) collective-permute-start(bf16[256,1024]{1,0:T(8,128)(2,1)} %collective-permute-done.12.refs_2_), channel_id=1, source_target_pairs={{0,1},{1,0},{2,3},{3,2},{4,5},{5,4},{6,7},{7,6},{8,9},{9,8},{10,11... | collective-permute-start | bytes 1572872 | tf_op jit(solution)/shard_map/ppermute | solution.py:19
  125.8 21.5 %collective-permute-start.23 = (bf16[256,1024]{1,0:T(8,128)(2,1)S(1)}, bf16[256,1024]{1,0:T(8,128)(2,1)S(1)}, u32[]{:S(2)}, u32[]{:S(2)}) collective-permute-start(bf16[256,1024]{1,0:T(8,128)(2,1)S(1)} %add_convert_fusion.9.refs_0_), channel_id=1, source_target_pairs={{0,1},{1,0},{2,3},{3,2},{4,5},{5,4},{6,7},{7,6},{8,9},{9,8},{10,11... | collective-permute-start | bytes 1572872 | tf_op jit(solution)/shard_map/ppermute | solution.py:19
  174.1 27.2 %collective-permute-start.32 = (bf16[256,1024]{1,0:T(8,128)(2,1)}, bf16[256,1024]{1,0:T(8,128)(2,1)S(1)}, u32[]{:S(2)}, u32[]{:S(2)}) collective-permute-start(bf16[256,1024]{1,0:T(8,128)(2,1)} %get-tuple-element.100), channel_id=1, source_target_pairs={{0,1},{1,0},{2,3},{3,2},{4,5},{5,4},{6,7},{7,6},{8,9},{9,8},{10,11... | collective-permute-start | bytes 1572872 | tf_op jit(solution)/shard_map/ppermute | solution.py:19
  176.9 24.3 %collective-permute-start.33 = (bf16[256,1024]{1,0:T(8,128)(2,1)S(1)}, bf16[256,1024]{1,0:T(8,128)(2,1)S(1)}, u32[]{:S(2)}, u32[]{:S(2)}) collective-permute-start(bf16[256,1024]{1,0:T(8,128)(2,1)S(1)} %add_convert_fusion.8), channel_id=1, source_target_pairs={{0,2},{1,3},{6,4},{7,5},{8,10},{9,11},{14,12},{15,13},{16,18},{17,... | collective-permute-start | bytes 1572872 | tf_op jit(solution)/shard_map/ppermute | solution.py:352
  179.6 21.6 %collective-permute-start.31 = (bf16[256,1024]{1,0:T(8,128)(2,1)S(1)}, bf16[256,1024]{1,0:T(8,128)(2,1)S(1)}, u32[]{:S(2)}, u32[]{:S(2)}) collective-permute-start(bf16[256,1024]{1,0:T(8,128)(2,1)S(1)} %add_convert_fusion.7), channel_id=1, source_target_pairs={{0,4},{1,5},{2,0},{3,1},{4,6},{5,7},{6,2},{7,3},{8,12},{9,13},{10,... | collective-permute-start | bytes 1572872 | tf_op jit(solution)/shard_map/ppermute | solution.py:352
  180.4 28.1 %collective-permute-start.27 = (bf16[256,1024]{1,0:T(8,128)(2,1)}, bf16[256,1024]{1,0:T(8,128)(2,1)S(1)}, u32[]{:S(2)}, u32[]{:S(2)}) collective-permute-start(bf16[256,1024]{1,0:T(8,128)(2,1)} %get-tuple-element.84), channel_id=1, source_target_pairs={{0,1},{1,0},{2,3},{3,2},{4,5},{5,4},{6,7},{7,6},{8,9},{9,8},{10,11... | collective-permute-start | bytes 1572872 | tf_op jit(solution)/shard_map/ppermute | solution.py:19
  192.1 16.7 %collective-permute-start.29 = (bf16[256,1024]{1,0:T(8,128)(2,1)S(1)}, bf16[256,1024]{1,0:T(8,128)(2,1)S(1)}, u32[]{:S(2)}, u32[]{:S(2)}) collective-permute-start(bf16[256,1024]{1,0:T(8,128)(2,1)S(1)} %add_convert_fusion.8), channel_id=1, source_target_pairs={{2,4},{3,5},{4,2},{5,3},{10,12},{11,13},{12,10},{13,11},{18,20},{1... | collective-permute-start | bytes 1572872 | tf_op jit(solution)/shard_map/ppermute | solution.py:352
  201.5 25.0 %collective-permute-start.34 = (bf16[256,1024]{1,0:T(8,128)(2,1)S(1)}, bf16[256,1024]{1,0:T(8,128)(2,1)S(1)}, u32[]{:S(2)}, u32[]{:S(2)}) collective-permute-start(bf16[256,1024]{1,0:T(8,128)(2,1)S(1)} %add_convert_fusion.6), channel_id=1, source_target_pairs={{0,2},{1,3},{2,6},{3,7},{4,0},{5,1},{6,4},{7,5},{8,10},{9,11},{10,... | collective-permute-start | bytes 1572872 | tf_op jit(solution)/shard_map/ppermute | solution.py:352
  207.7 60.2 %collective-permute-start.38 = (bf16[256,1024]{1,0:T(8,128)(2,1)S(1)}, bf16[256,1024]{1,0:T(8,128)(2,1)S(1)}, u32[]{:S(2)}, u32[]{:S(2)}) collective-permute-start(bf16[256,1024]{1,0:T(8,128)(2,1)S(1)} %copy-done.37), channel_id=1, source_target_pairs={{0,1},{1,0},{2,3},{3,2},{4,5},{5,4},{6,7},{7,6},{8,9},{9,8},{10,11... | collective-permute-start | bytes 1572872 | tf_op jit(solution)/shard_map/ppermute | solution.py:19
  208.0 21.7 %collective-permute-start.41 = (bf16[256,1024]{1,0:T(8,128)(2,1)S(1)}, bf16[256,1024]{1,0:T(8,128)(2,1)S(1)}, u32[]{:S(2)}, u32[]{:S(2)}) collective-permute-start(bf16[256,1024]{1,0:T(8,128)(2,1)S(1)} %copy-done.39), channel_id=1, source_target_pairs={{0,1},{1,0},{2,3},{3,2},{4,5},{5,4},{6,7},{7,6},{8,9},{9,8},{10,11... | collective-permute-start | bytes 1572872 | tf_op jit(solution)/shard_map/ppermute | solution.py:19
  208.5 21.9 %collective-permute-start.43 = (bf16[256,1024]{1,0:T(8,128)(2,1)S(1)}, bf16[256,1024]{1,0:T(8,128)(2,1)S(1)}, u32[]{:S(2)}, u32[]{:S(2)}) collective-permute-start(bf16[256,1024]{1,0:T(8,128)(2,1)S(1)} %copy-done.38), channel_id=1, source_target_pairs={{0,1},{1,0},{2,3},{3,2},{4,5},{5,4},{6,7},{7,6},{8,9},{9,8},{10,11... | collective-permute-start | bytes 1572872 | tf_op jit(solution)/shard_map/ppermute | solution.py:19
  208.8 22.2 %collective-permute-start.44 = (bf16[256,1024]{1,0:T(8,128)(2,1)S(1)}, bf16[256,1024]{1,0:T(8,128)(2,1)S(1)}, u32[]{:S(2)}, u32[]{:S(2)}) collective-permute-start(bf16[256,1024]{1,0:T(8,128)(2,1)S(1)} %add_convert_fusion.4), channel_id=1, source_target_pairs={{0,2},{1,3},{6,4},{7,5},{8,10},{9,11},{14,12},{15,13},{16,18},{17,... | collective-permute-start | bytes 1572872 | tf_op jit(solution)/shard_map/ppermute | solution.py:352
  227.2 15.8 %collective-permute-start.37 = (bf16[256,1024]{1,0:T(8,128)(2,1)S(1)}, bf16[256,1024]{1,0:T(8,128)(2,1)S(1)}, u32[]{:S(2)}, u32[]{:S(2)}) collective-permute-start(bf16[256,1024]{1,0:T(8,128)(2,1)S(1)} %add_convert_fusion.5.refs_1_), channel_id=1, source_target_pairs={{0,24},{8,16},{16,8},{24,0},{1,25},{9,17},{17,9},{25,1},{2,26},{10... | collective-permute-start | bytes 1572872 | tf_op jit(solution)/shard_map/ppermute | solution.py:19
  229.7 23.6 %collective-permute-start.36 = (bf16[256,1024]{1,0:T(8,128)(2,1)S(1)}, bf16[256,1024]{1,0:T(8,128)(2,1)S(1)}, u32[]{:S(2)}, u32[]{:S(2)}) collective-permute-start(bf16[256,1024]{1,0:T(8,128)(2,1)S(1)} %add_convert_fusion.5.refs_1_), channel_id=1, source_target_pairs={{0,16},{8,24},{16,0},{24,8},{1,17},{9,25},{17,1},{25,9},{2,18},{10... | collective-permute-start | bytes 1572872 | tf_op jit(solution)/shard_map/ppermute | solution.py:19
  230.4 27.6 %collective-permute-start.35 = (bf16[256,1024]{1,0:T(8,128)(2,1)S(1)}, bf16[256,1024]{1,0:T(8,128)(2,1)S(1)}, u32[]{:S(2)}, u32[]{:S(2)}) collective-permute-start(bf16[256,1024]{1,0:T(8,128)(2,1)S(1)} %add_convert_fusion.5.refs_1_), channel_id=1, source_target_pairs={{0,8},{8,0},{16,24},{24,16},{1,9},{9,1},{17,25},{25,17},{2,10},{10... | collective-permute-start | bytes 1572872 | tf_op jit(solution)/shard_map/ppermute | solution.py:19
  231.0 36.9 %collective-permute-start.40 = (bf16[256,1024]{1,0:T(8,128)(2,1)S(1)}, bf16[256,1024]{1,0:T(8,128)(2,1)S(1)}, u32[]{:S(2)}, u32[]{:S(2)}) collective-permute-start(bf16[256,1024]{1,0:T(8,128)(2,1)S(1)} %add_convert_fusion.4), channel_id=1, source_target_pairs={{2,4},{3,5},{4,2},{5,3},{10,12},{11,13},{12,10},{13,11},{18,20},{1... | collective-permute-start | bytes 1572872 | tf_op jit(solution)/shard_map/ppermute | solution.py:352
  243.0 24.9 %collective-permute-start.42 = (bf16[256,1024]{1,0:T(8,128)(2,1)S(1)}, bf16[256,1024]{1,0:T(8,128)(2,1)S(1)}, u32[]{:S(2)}, u32[]{:S(2)}) collective-permute-start(bf16[256,1024]{1,0:T(8,128)(2,1)S(1)} %add_convert_fusion.3), channel_id=1, source_target_pairs={{0,4},{1,5},{2,0},{3,1},{4,6},{5,7},{6,2},{7,3},{8,12},{9,13},{10,... | collective-permute-start | bytes 1572872 | tf_op jit(solution)/shard_map/ppermute | solution.py:352
  (54 other events, 742.1 us)

commit v4 on v3

--- a/solution.py
+++ b/solution.py
@@ -347,6 +347,15 @@
 STAY, FIRST, SECOND, LAST = (0, 1, 2, 3), (1, 3, 0, 2), (2, 0, 3, 1), (3, 2, 1, 0)
 
 
+OUTWARD = [(0, 1), (1, 0), (2, 3), (3, 2)]
+INSIDE = [(0, 1), (1, 0), (2, 4), (3, 5), (4, 2), (5, 3), (6, 7), (7, 6)]
+
+
+def is_inner():
+    chip = lax.axis_index("tp") // 2
+    return (chip == 1) | (chip == 2)
+
+
 def along(value, pairs):
     both = [(2 * start + core, 2 * end + core) for start, end in pairs for core in range(2)]
     return lax.ppermute(value, "tp", both)
@@ -369,40 +378,47 @@
     return along(block, arriving(FIRST))
 
 
-def gather_rest(block, first):
-    far = along(first, [(2, 3), (1, 0)])
-    second = along(block, arriving(SECOND))
-    near = along(block, [(1, 2), (2, 1)])
-    return far, second, near
+def gather_second(block):
+    return along(block, arriving(SECOND))
+
+
+def gather_last(block, first):
+    return along(first, OUTWARD), lax.ppermute(block, "tp", INSIDE)
 
 
 def early_blocks(block, first):
     return [block, swapped(block, "tp", 1), first, swapped(first, "tp", 1)]
 
 
-def late_blocks(rest):
-    far, second, near = rest
-    last = far + near
+def late_blocks(second, last):
+    far, near = last
+    last = jnp.where(is_inner(), near, far)
     return [second, swapped(second, "tp", 1), last, swapped(last, "tp", 1)]
 
 
-def line_scatter(parts):
-    def joined(place):
-        other = swapped(parts[2 * place + 1], "tp", 1)
-        return parts[2 * place].astype(jnp.float32) + other.astype(jnp.float32)
-
-    last = joined(0).astype(jnp.bfloat16)
-    far = along(last, [(0, 1), (3, 2)])
-    near = along(last, [(1, 2), (2, 1)])
-    second = along(joined(1).astype(jnp.bfloat16), towards(SECOND))
-    first = joined(2) + far.astype(jnp.float32)
-    first = along(first.astype(jnp.bfloat16), towards(FIRST))
-    own = joined(3) + near.astype(jnp.float32)
-    return own, second, first
-
-
-def line_total(own, second, first):
-    return own + second.astype(jnp.float32) + first.astype(jnp.float32)
+def both_cores(parts, place):
+    other = swapped(parts[2 * place + 1], "tp", 1)
+    return parts[2 * place].astype(jnp.float32) + other.astype(jnp.float32)
+
+
+def scatter_begun(parts):
+    last = both_cores(parts, 0).astype(jnp.bfloat16)
+    return last, along(last, OUTWARD), lax.ppermute(last, "tp", INSIDE)
+
+
+def scatter_second(parts):
+    return along(both_cores(parts, 1).astype(jnp.bfloat16), towards(SECOND))
+
+
+def scatter_first(parts, far):
+    first = both_cores(parts, 2)
+    first += jnp.where(is_inner(), far.astype(jnp.float32), 0.0)
+    return along(first.astype(jnp.bfloat16), towards(FIRST))
+
+
+def scatter_total(parts, near, second, first):
+    total = both_cores(parts, 3) + jnp.where(is_inner(), near.astype(jnp.float32), 0.0)
+    return total + second.astype(jnp.float32) + first.astype(jnp.float32)
 
 
 def line_stitch_half(blocks, rows, rows_ref, weight_ref, product, here, sems, out_sem):
@@ -572,9 +588,124 @@
     )(chips, core.reshape(1), context, weight)
 
 
+def line_project(
+    places, from_ref, gain_ref, q_weight_ref, kv_weight_ref, blocks, hidden, q_weight, kv_weight,
+    sems, query_sum, pair_sum, squares,
+):
+    rows, step = blocks[0].shape
+
+    def part(place):
+        return pl.ds(pl.multiple_of(from_ref[place] * step, step), step)
+
+    def fetches(place):
+        span = part(place)
+        return (
+            pltpu.make_async_copy(q_weight_ref.at[span], q_weight.at[span], sems.at[1, place]),
+            pltpu.make_async_copy(kv_weight_ref.at[span], kv_weight.at[span], sems.at[2, place]),
+        )
+
+    def features(place):
+        return pltpu.make_async_copy(blocks[0], hidden.at[place], sems.at[0, place])
+
+    later = [place for place in range(len(blocks)) if place not in places]
+    for place in [*places, *later]:
+        pltpu.make_async_copy(blocks[place], hidden.at[place], sems.at[0, place]).start()
+        for fetch in fetches(place):
+            fetch.start()
+
+    def project(place, squares):
+        features(place).wait()
+        for fetch in fetches(place):
+            fetch.wait()
+        span = part(place)
+        wide = hidden[place].astype(jnp.float32)
+        gained = (wide * gain_ref[:, span]).astype(jnp.bfloat16)
+        query_sum[...] += dot_f32(gained, q_weight[span, :])
+        pair_sum[...] += dot_f32(gained, kv_weight[span, :])
+        return squares + jnp.sum(wide * wide, axis=1, keepdims=True)
+
+    squares = lax.fori_loop(places[0], places[-1] + 1, project, squares)
+
+    def finish():
+        for place in later:
+            features(place).wait()
+            for fetch in fetches(place):
+                fetch.wait()
+
+    return squares, finish
+
+
+def line_projected_kernel(
+    from_ref, gain_ref, q_weight_ref, kv_weight_ref, *refs,
+):
+    blocks, (query_sum, pair_sum, squares_ref) = refs[:4], refs[4:7]
+    hidden, q_weight, kv_weight, sems = refs[7:]
+    query_sum[...] = jnp.zeros_like(query_sum)
+    pair_sum[...] = jnp.zeros_like(pair_sum)
+    squares, _ = line_project(
+        range(4), from_ref, gain_ref, q_weight_ref, kv_weight_ref, blocks, hidden, q_weight,
+        kv_weight, sems, query_sum, pair_sum, jnp.zeros(squares_ref.shape, jnp.float32),
+    )
+    squares_ref[...] = squares
+
+
+def line_projected(sources, blocks, gain, q_weight, kv_weight):
+    rows, step = blocks[0].shape
+    heads_cols, kv_cols = q_weight.shape[1], kv_weight.shape[1]
+    whole, far = pl.BlockSpec(memory_space=pltpu.VMEM), pl.BlockSpec(memory_space=pl.ANY)
+    return pl.pallas_call(
+        line_projected_kernel,
+        in_specs=[pl.BlockSpec(memory_space=pltpu.SMEM), whole] + [far] * 6,
+        out_specs=[whole] * 3,
+        out_shape=[
+            jax.ShapeDtypeStruct((rows, heads_cols), jnp.float32),
+            jax.ShapeDtypeStruct((rows, kv_cols), jnp.float32),
+            jax.ShapeDtypeStruct((rows, 1), jnp.float32),
+        ],
+        scratch_shapes=[
+            pltpu.VMEM((4, rows, step), jnp.bfloat16),
+            pltpu.VMEM(q_weight.shape, jnp.bfloat16),
+            pltpu.VMEM(kv_weight.shape, jnp.bfloat16),
+            pltpu.SemaphoreType.DMA((3, 4)),
+        ],
+        compiler_params=pltpu.CompilerParams(vmem_limit_bytes=VMEM_LIMIT),
+    )(sources, gain[None, :], q_weight, kv_weight, *blocks)
+
+
+def line_tokens_kernel(token_ref, order_ref, early_ref, late_ref, out_ref):
+    half = early_ref.shape[0]
+    total = None
+    for place, rows_ref in enumerate((early_ref, late_ref)):
+        tokens = token_ref[pl.ds(place * half, half), :]
+        chosen = (tokens == order_ref[...]).astype(jnp.float32).astype(jnp.bfloat16)
+        term = dot_f32(rows_ref[...], chosen, COLS_BY_COLS)
+        total = term if total is None else total + term
+    out_ref[...] = total.astype(out_ref.dtype)
+
+
+def line_tokens_last(token_col, token_order, early_rows, late_rows):
+    half, features = early_rows.shape
+    tokens = token_order.shape[1]
+    block = min(1024, features)
+    fixed = lambda i: (0, 0)
+    return pl.pallas_call(
+        line_tokens_kernel,
+        grid=(features // block,),
+        in_specs=[
+            pl.BlockSpec((2 * half, 1), fixed),
+            pl.BlockSpec((1, tokens), fixed),
+            pl.BlockSpec((half, block), lambda i: (0, i)),
+            pl.BlockSpec((half, block), lambda i: (0, i)),
+        ],
+        out_specs=pl.BlockSpec((block, tokens), lambda i: (i, 0)),
+        out_shape=jax.ShapeDtypeStruct((features, tokens), jnp.bfloat16),
+        compiler_params=pltpu.CompilerParams(vmem_limit_bytes=VMEM_LIMIT),
+    )(token_col, token_order, early_rows, late_rows)
+
+
 def line_middle_kernel(
     repeat, from_ref, to_ref, gain_ref, cos_ref, sin_ref, seg_row_ref, seg_col_ref, grad_ref,
-    q_weight_ref, kv_weight_ref, *refs,
+    early_query_ref, early_pair_ref, early_squares_ref, q_weight_ref, kv_weight_ref, *refs,
 ):
     blocks, context_ref, out_refs = refs[:8], refs[8], refs[9:17]
     hidden, q_weight, kv_weight, out, query_sum, pair_sum, query_grad, sems, out_sems = refs[17:]
@@ -584,33 +715,12 @@
     def part(rank):
         return pl.ds(pl.multiple_of(rank * step, step), step)
 
-    def fetches(place):
-        span = part(from_ref[place])
-        return (
-            pltpu.make_async_copy(q_weight_ref.at[span], q_weight.at[span], sems.at[1, place]),
-            pltpu.make_async_copy(kv_weight_ref.at[span], kv_weight.at[span], sems.at[2, place]),
-        )
-
-    for place in range(8):
-        pltpu.make_async_copy(blocks[place], hidden.at[place], sems.at[0, place]).start()
-        for fetch in fetches(place):
-            fetch.start()
-
-    query_sum[...] = jnp.zeros_like(query_sum)
-    pair_sum[...] = jnp.zeros_like(pair_sum)
-
-    def project(place, squares):
-        pltpu.make_async_copy(blocks[0], hidden.at[place], sems.at[0, place]).wait()
-        for fetch in fetches(place):
-            fetch.wait()
-        span = part(from_ref[place])
-        features = hidden[place].astype(jnp.float32)
-        gained = (features * gain_ref[:, span]).astype(jnp.bfloat16)
-        query_sum[...] += dot_f32(gained, q_weight[span, :])
-        pair_sum[...] += dot_f32(gained, kv_weight[span, :])
-        return squares + jnp.sum(features * features, axis=1, keepdims=True)
-
-    squares = lax.fori_loop(0, 8, project, jnp.zeros((rows, 1), jnp.float32))
+    query_sum[...] = early_query_ref[...]
+    pair_sum[...] = early_pair_ref[...]
+    squares, finish = line_project(
+        range(4, 8), from_ref, gain_ref, q_weight_ref, kv_weight_ref, blocks, hidden, q_weight,
+        kv_weight, sems, query_sum, pair_sum, early_squares_ref[...],
+    )
     row_scale = lax.rsqrt(squares / width + epsilon)
     cosines, sines = cos_ref[...], sin_ref[...]
     groups = kv_weight.shape[1] // (2 * HD)
@@ -629,6 +739,7 @@
         aligned += half * pair_grad.astype(jnp.float32)
     aligned = jnp.sum(aligned, axis=1, keepdims=True) * (row_scale * row_scale / width)
     pair_grad = jnp.concatenate(pair_grads, axis=1)
+    finish()
 
     @pl.loop(0, 8)
     def _(place):
@@ -650,8 +761,8 @@
 
 
 def line_middle(
-    repeat, sources, targets, blocks, gain, q_weight, kv_weight, cosines, sines, seg_row,
-    context_grad,
+    repeat, sources, targets, blocks, early_sums, gain, q_weight, kv_weight, cosines, sines, seg_row,
+    seg_col, context_grad,
 ):
     rows, step = blocks[0].shape
     heads_cols, kv_cols = q_weight.shape[1], kv_weight.shape[1]
@@ -659,7 +770,7 @@
     scalars = pl.BlockSpec(memory_space=pltpu.SMEM)
     results = pl.pallas_call(
         functools.partial(line_middle_kernel, repeat),
-        in_specs=[scalars] * 2 + [whole] * 6 + [far] * 10,
+        in_specs=[scalars] * 2 + [whole] * 9 + [far] * 10,
         out_specs=[whole] + [far] * 8,
         out_shape=[jax.ShapeDtypeStruct((rows, heads_cols), jnp.bfloat16)]
         + [jax.ShapeDtypeStruct((rows, step), jnp.bfloat16)] * 8,
@@ -676,8 +787,8 @@
         ],
         compiler_params=pltpu.CompilerParams(vmem_limit_bytes=VMEM_LIMIT),
     )(
-        sources, targets, gain[None, :], cosines, sines, seg_row[None, :], seg_row[:, None],
-        context_grad, q_weight, kv_weight, *blocks,
+        sources, targets, gain[None, :], cosines, sines, seg_row[None, :], seg_col,
+        context_grad, *early_sums, q_weight, kv_weight, *blocks,
     )
     return results[0], results[1:]
 
@@ -714,57 +825,69 @@
 
     token_row = row_token.reshape(8, -1)[sources].reshape(1, -1)
     first = gather_begun(source)
-    source, (first, token_row) = after(source, (first, token_row))
-    rest = gather_rest(source, first)
+    seg_col, token_col = seg_row[:, None], token_row.reshape(-1, 1)
+    arrivals, departures = chips(arrival), chips(departure)
+    small = (token_row, token_col, seg_col, cosines, sines, sources, targets, arrivals, departures)
+    source, (first, small) = after(source, (first, small))
+    token_row, token_col, seg_col, cosines, sines, sources, targets, arrivals, departures = small
+    second, last = gather_second(source), gather_last(source, first)
     early_source = early_blocks(source, first)
     early_product, early_rows = line_stitched_early(early_source, stitch_weight)
-    out_grad, (rest, early_product) = after(out_grad, (rest, early_product))
-    late_source = late_blocks(rest)
-    grad_first = gather_begun(out_grad)
+    out_grad, (second, last, early_product) = after(out_grad, (second, last, early_product))
+    late_source = late_blocks(second, last)
+    og_first = gather_begun(out_grad)
     placed, late_rows = line_stitched(
         packs, pack_len, tok_rank, token_row, early_product, late_source, stitch_weight
     )
     received = [swapped(placed[distance], "tok", distance) for distance in range(1, packs)]
-    received[0], grad_first = after(received[0], grad_first)
-    grad_rest = gather_rest(out_grad, grad_first)
+    received[0], og_first = after(received[0], og_first)
+    og_second, og_last = gather_second(out_grad), gather_last(out_grad, og_first)
     hidden = placed[0].astype(jnp.float32)
     for part in received:
         hidden += part.astype(jnp.float32)
     hidden_bf = hidden.astype(jnp.bfloat16)
     hidden_first = gather_begun(hidden_bf)
-    (hidden_bf, hidden_first), grad_rest = after((hidden_bf, hidden_first), grad_rest)
-    hidden_rest = gather_rest(hidden_bf, hidden_first)
-    grad_blocks = early_blocks(out_grad, grad_first) + late_blocks(grad_rest)
-    grad_context = line_grad_context(chips(arrival), core, grad_blocks, o_weight)
-    hidden_rest, grad_context = after(hidden_rest, grad_context)
-    hidden_blocks = early_blocks(hidden_bf, hidden_first) + late_blocks(hidden_rest)
+    early_rows, hidden_bf = after(early_rows, hidden_bf)
+    token_order = (
+        (tok_rank ^ jnp.arange(packs, dtype=jnp.int32))[:, None] * pack_len + within[None, :]
+    ).reshape(-1)
+    tokens_last = line_tokens_last(token_col, token_order[None, :], early_rows, late_rows)
+    (hidden_bf, hidden_first), (og_second, og_last, tokens_last) = after(
+        (hidden_bf, hidden_first), (og_second, og_last, tokens_last)
+    )
+    hidden_second, hidden_last = gather_second(hidden_bf), gather_last(hidden_bf, hidden_first)
+    og_blocks = early_blocks(out_grad, og_first) + late_blocks(og_second, og_last)
+    grad_context = line_grad_context(arrivals, core, og_blocks, o_weight)
+    early_hidden = early_blocks(hidden_bf, hidden_first)
+    early_sums = line_projected(sources, early_hidden, norm_gain, q_weight, kv_weight)
+    hidden_last, (hidden_second, grad_context, early_sums) = after(
+        hidden_last, (hidden_second, grad_context, early_sums)
+    )
+    hidden_blocks = early_hidden + late_blocks(hidden_second, hidden_last)
 
     context, grad_parts = line_middle(
-        repeat, sources, targets, hidden_blocks, norm_gain, q_weight, kv_weight, cosines, sines,
-        seg_row, grad_context,
-    )
-    grad_own, grad_second, grad_first = line_scatter(grad_parts)
-    attended_parts = line_attended(chips(departure), core, context, o_weight)
-    attended_parts, grad_second = after(attended_parts, grad_second)
-    grad_hidden = (
-        out_grad.astype(jnp.float32) + line_total(grad_own, grad_second, grad_first)
-    ).astype(jnp.bfloat16)
+        repeat, sources, targets, hidden_blocks, early_sums, norm_gain, q_weight, kv_weight,
+        cosines, sines, seg_row, seg_col, grad_context,
+    )
+    last, far, near = scatter_begun(grad_parts)
+    context, last = after(context, last)
+    attended_parts = line_attended(departures, core, context, o_weight)
+    second = scatter_second(grad_parts)
+    far, (near, attended_parts) = after(far, (near, attended_parts))
+    first = scatter_first(grad_parts, far)
+    attended_parts, second = after(attended_parts, second)
+    grad_sum = scatter_total(grad_parts, near, second, first)
+    grad_hidden = (out_grad.astype(jnp.float32) + grad_sum).astype(jnp.bfloat16)
     every_pack = [grad_hidden] + [
         swapped(grad_hidden, "tok", distance) for distance in range(1, packs)
     ]
-    token_order = (
-        (tok_rank ^ jnp.arange(packs, dtype=jnp.int32))[:, None] * pack_len + within[None, :]
-    ).reshape(-1)
-    order = (token_row.reshape(-1, 1) == token_order[None, :]).astype(jnp.bfloat16)
-    half = early_rows.shape[0]
-    tokens_last = (
-        dot_f32(early_rows, order[:half], COLS_BY_COLS)
-        + dot_f32(late_rows, order[half:], COLS_BY_COLS)
-    ).astype(jnp.bfloat16)
-    attended = line_scatter(attended_parts)
+    _, far, near = scatter_begun(attended_parts)
+    second = scatter_second(attended_parts)
+    far, near = after(far, near)
+    first = scatter_first(attended_parts, far)
     late_hidden, *every_pack = lax.optimization_barrier((hidden_bf, *every_pack))
     stitch_grad = outer_summed(tokens_last, every_pack)
-    attended = line_total(*attended)
+    attended = scatter_total(attended_parts, near, second, first)
     layer_out = (late_hidden.astype(jnp.float32) + attended).astype(jnp.bfloat16)
     return (layer_out, stitch_grad)
 

time: 271 us -> 247 us (0.911)
  waiting for transfers between devices: 111 us -> 94.1 us
  starting transfers between devices: 54.4 us -> 40.2 us
  Pallas kernels: 73.8 us -> 86.5 us
  matrix products: 7.32 us -> 0 us
  local copies, waits for them, and re-layouts: 8.43 us -> 11.7 us
    ppermute x20 -> x15, starting transfers between devices: 42.3 us -> 26.3 us  [along(): return lax.ppermute(value, 'tp', both)]
    pallas_call x0 -> x2, Pallas kernels: none -> 15.4 us  [the longest x1 8.03 us: line_tokens_last(): pl.pallas_call(line_tokens_kernel, grid=(features // block,), in_specs=[p...]
    ppermute x26, waiting for transfers between devices: 43.9 us -> 31.8 us  [swapped(): return lax.ppermute(value, axis, pairs)]
    dot_general x2 -> x0, matrix products: 7.32 us -> none  [dot_f32(): lax.dot_general(left, right, dims, preferred_element_type=jnp.float32)]
    ppermute x20 -> x15, waiting for transfers between devices: 67.6 us -> 62.3 us  [along(): return lax.ppermute(value, 'tp', both)]
    pallas_call x1, Pallas kernels: 24.5 us -> 21.6 us  [line_middle(): pl.pallas_call(functools.partial(line_middle_kernel, repeat), in_specs=[s...]
    add x4 -> x0, other arithmetic: 2.77 us -> none  [the longest x3 1.55 us: late_blocks(): last = far + near]
    unnamed x81 -> x77, local copies, waits for them, and re-layouts: 4.95 us -> 7.19 us
  transfers between devices with their start and end apart: 46 -> 46, of which waited for: 16 -> 16; matrix products, arithmetic and copies ran while one was open for 8% -> 7% of each run, Pallas kernels for 18% -> 26%
where the time goes in v4:
time: 247 us
  waiting for transfers between devices  94.1 us (38%)
  Pallas kernels  86.5 us (35%)
  starting transfers between devices  40.2 us (16%)
  other arithmetic  12.9 us (5%)
  local copies, waits for them, and re-layouts  11.7 us (5%)
    ppermute x15, waiting for transfers between devices, along(): return lax.ppermute(value, 'tp', both)  62.3 us
    ppermute x26, waiting for transfers between devices, swapped(): return lax.ppermute(value, axis, pairs)  31.8 us
    ppermute x15, starting transfers between devices, along(): return lax.ppermute(value, 'tp', both)  26.3 us
    pallas_call x1, Pallas kernels, line_middle(): pl.pallas_call(functools.partial(line_middle_kernel, repeat), in_specs=[s...  21.6 us
    ppermute x26, starting transfers between devices, swapped(): return lax.ppermute(value, axis, pairs)  13.3 us
    pallas_call x1, Pallas kernels, line_grad_context(): pl.pallas_call(line_grad_kernel, grid_spec=pltpu.PrefetchScalarGridSpec(n...  11.9 us
    pallas_call x1, Pallas kernels, line_attended(): pl.pallas_call(line_attended_kernel, grid_spec=pltpu.PrefetchScalarGridSp...  11.6 us
    pallas_call x1, Pallas kernels, line_stitched(): pl.pallas_call(functools.partial(line_stitch_kernel, packs), in_specs=[pl...  9.9 us
  transfers between devices with their start and end apart: 46, of which 16 were waited for; matrix products, arithmetic and copies ran while one was open for 7% of the time, Pallas kernels for 26%

profile of v4, /device:TPU:0, one launch (start us, length us, event | category | flops | bytes accessed | tf_op | source)
XLA Modules:
  0.0 246.7 jit_solution(16337125577373390559)
XLA Ops:
  0.6 4.1 %collective-permute-start = (bf16[128,2048]{1,0:T(8,128)(2,1)}, bf16[128,2048]{1,0:T(8,128)(2,1)S(1)}, u32[]{:S(2)}, u32[]{:S(2)}) collective-permute-start(bf16[128,2048]{1,0:T(8,128)(2,1)} %refs_0_), channel_id=1, source_target_pairs={{2,0},{3,1},{6,2},{7,3},{0,4},{1,5},{4,6},{5,7},{10,8},{11,9},{14,... | collective-permute-start | bytes 1572872 | tf_op jit(solution)/shard_map/ppermute | solution.py:361
  11.2 5.1 %collective-permute-done.refs_2_ = bf16[128,2048]{1,0:T(8,128)(2,1)S(1)} collective-permute-done((bf16[128,2048]{1,0:T(8,128)(2,1)}, bf16[128,2048]{1,0:T(8,128)(2,1)S(1)}, u32[]{:S(2)}, u32[]{:S(2)}) %collective-permute-start) | collective-permute-done | bytes 524320 | tf_op jit(solution)/shard_map/ppermute | solution.py:361
  16.7 2.3 collective-permute-start.4
  19.0 2.3 collective-permute-start.3
  22.8 7.0 %shard_map.140 = (bf16[512,1024]{1,0:T(8,128)(2,1)}, bf16[512,2048]{1,0:T(8,128)(2,1)}) custom-call(bf16[2048,1024]{1,0:T(8,128)(2,1)} %weight_ref.5, bf16[128,2048]{1,0:T(8,128)(2,1)} %refs_0_, bf16[128,2048]{1,0:T(8,128)(2,1)} %copy-done.30, bf16[128,2048]{1,0:T(8,128)(2,1)} %copy-done.14, bf16[128,2048]{1,0:T(8,128)(2,1)} %copy-done.28), custom_call_target="tpu_custom_call" | custom-call | tf_op jit(solution)/shard_map/pallas_call | solution.py:469
  31.3 12.6 %collective-permute-done.3.refs_0_ = bf16[128,2048]{1,0:T(8,128)(2,1)S(1)} collective-permute-done((bf16[128,2048]{1,0:T(8,128)(2,1)}, bf16[128,2048]{1,0:T(8,128)(2,1)S(1)}, u32[]{:S(2)}, u32[]{:S(2)}) %collective-permute-start.3) | collective-permute-done | bytes 524320 | tf_op jit(solution)/shard_map/ppermute | solution.py:361
  44.6 2.4 collective-permute-start.9
  48.0 9.9 %shard_map.141 = (bf16[256,1024]{1,0:T(8,128)(2,1)}, bf16[256,1024]{1,0:T(8,128)(2,1)}, bf16[256,1024]{1,0:T(8,128)(2,1)}, bf16[256,1024]{1,0:T(8,128)(2,1)}, bf16[512,2048]{1,0:T(8,128)(2,1)}) custom-call(s32[1]{0:T(128)} %bitcast.8.rank_ref, s32[1,1024]{1,0:T(1,128)} %bitcast.21, bf16[2048,1024]{1,0:T(8,128)(2,1)} %weight_ref.5, ...), custom_call_target="tpu_custom_call" | custom-call | tf_op jit(solution)/shard_map/pallas_call | solution.py:490
  57.9 1.6 collective-permute-start.8
  61.5 2.5 %collective-permute-start.13 = (bf16[256,1024]{1,0:T(8,128)(2,1)S(1)}, bf16[256,1024]{1,0:T(8,128)(2,1)S(1)}, u32[]{:S(2)}, u32[]{:S(2)}) collective-permute-start(bf16[256,1024]{1,0:T(8,128)(2,1)S(1)} %copy-done.10), channel_id=1, source_target_pairs={{4,0},{5,1},{0,2},{1,3},{6,4},{7,5},{2,6},{3,7},{12,8},{13,9},{8,1... | collective-permute-start | bytes 1572872 | tf_op jit(solution)/shard_map/ppermute | solution.py:361
  64.0 9.0 %collective-permute-done.8 = bf16[256,1024]{1,0:T(8,128)(2,1)S(1)} collective-permute-done((bf16[256,1024]{1,0:T(8,128)(2,1)}, bf16[256,1024]{1,0:T(8,128)(2,1)S(1)}, u32[]{:S(2)}, u32[]{:S(2)}) %collective-permute-start.8) | collective-permute-done | bytes 524320 | tf_op jit(solution)/shard_map/ppermute | solution.py:19
  73.9 10.4 %collective-permute-done.10 = bf16[256,1024]{1,0:T(8,128)(2,1)S(1)} collective-permute-done((bf16[256,1024]{1,0:T(8,128)(2,1)}, bf16[256,1024]{1,0:T(8,128)(2,1)S(1)}, u32[]{:S(2)}, u32[]{:S(2)}) %collective-permute-start.10) | collective-permute-done | bytes 524320 | tf_op jit(solution)/shard_map/ppermute | solution.py:19
  85.7 2.3 collective-permute-start.12
  89.7 8.0 %shard_map.142.refs_0_ = bf16[2048,1024]{1,0:T(8,128)(2,1)} custom-call(s32[1024,1]{1,0:T(8,128)} %copy.26.token_ref, s32[1,1024]{1,0:T(1,128)} %bitcast.23, bf16[512,2048]{1,0:T(8,128)(2,1)} %get-tuple-element.107.early_ref, bf16[512,2048]{1,0:T(8,128)(2,1)} %get-tuple-element.108.late_ref), custom_call_target="tpu_custom_call" | custom-call | tf_op jit(solution)/shard_map/pallas_call | solution.py:691
  98.3 8.6 %collective-permute-done.12.refs_2_ = bf16[256,1024]{1,0:T(8,128)(2,1)S(1)} collective-permute-done((bf16[256,1024]{1,0:T(8,128)(2,1)S(1)}, bf16[256,1024]{1,0:T(8,128)(2,1)S(1)}, u32[]{:S(2)}, u32[]{:S(2)}) %collective-permute-start.12) | collective-permute-done | bytes 524320 | tf_op jit(solution)/shard_map/ppermute | solution.py:361
  109.2 2.0 collective-permute-start.18
  112.1 7.4 %shard_map.144 = (f32[256,1024]{1,0:T(8,128)}, f32[256,256]{1,0:T(8,128)}, f32[256,1]{1,0:T(8,128)}) custom-call(s32[8]{0:T(128)} %reshape.115.from_ref, f32[1,8192]{1,0:T(1,128)} %bitcast.19, bf16[8192,1024]{1,0:T(8,128)(2,1)} %q_weight_ref.3, bf16[8192,256]{1,0:T(8,128)(2,1)} %kv_weight_ref.3, bf16[256,1024]{1,0:T(8,128)(2,1)} %copy-done.2, ...), custom_call_target="tpu_custom_call" | custom-call | tf_op jit(solution)/shard_map/pallas_call | solution.py:656
  120.5 11.9 %shard_map.143.grad_ref = bf16[256,1024]{1,0:T(8,128)(2,1)} custom-call(s32[4]{0:T(128)} %get-tuple-element.116.chips_ref, s32[1]{0:T(128)} %bitcast.10.core_ref, bf16[1024,8192]{1,0:T(8,128)(2,1)} %weight_ref.7, bf16[256,1024]{1,0:T(8,128)(2,1)} %refs_0_.1, bf16[256,1024]{1,0:T(8,128)(2,1)} %copy-done.19, bf16[256,1024]{1,0:T(8,128)(2,1)} %copy-done.13, ...), custom_call_target="tpu_custom_call" | custom-call | tf_op jit(solution)/shard_map/pallas_call | solution.py:536
  132.4 2.0 collective-permute-done.16
  138.0 21.6 %shard_map.145 = (bf16[256,1024]{1,0:T(8,128)(2,1)}, bf16[256,1024]{1,0:T(8,128)(2,1)}, bf16[256,1024]{1,0:T(8,128)(2,1)}, bf16[256,1024]{1,0:T(8,128)(2,1)}, bf...) custom-call(s32[8]{0:T(128)} %reshape.115.from_ref, ...), custom_call_target="tpu_custom_call" | custom-call | tf_op jit(solution)/shard_map/pallas_call | solution.py:771
  160.2 1.6 collective-permute-done.28
  163.2 3.4 %collective-permute-start.29 = (bf16[256,1024]{1,0:T(8,128)(2,1)S(1)}, bf16[256,1024]{1,0:T(8,128)(2,1)S(1)}, u32[]{:S(2)}, u32[]{:S(2)}) collective-permute-start(bf16[256,1024]{1,0:T(8,128)(2,1)S(1)} %add_convert_fusion.7), channel_id=1, source_target_pairs={{0,2},{1,3},{2,0},{3,1},{4,6},{5,7},{6,4},{7,5},{8,10},{9,11},{10,... | collective-permute-start | bytes 1572872 | tf_op jit(solution)/shard_map/ppermute | solution.py:361
  168.5 11.6 %shard_map.146 = (bf16[256,1024]{1,0:T(8,128)(2,1)}, bf16[256,1024]{1,0:T(8,128)(2,1)}, bf16[256,1024]{1,0:T(8,128)(2,1)}, bf16[256,1024]{1,0:T(8,128)(2,1)}, bf...) custom-call(s32[4]{0:T(128)} %get-tuple-element.134.chips_ref, ...), custom_call_target="tpu_custom_call" | custom-call | tf_op jit(solution)/shard_map/pallas_call | solution.py:574
  180.2 9.7 %collective-permute-done.32 = bf16[256,1024]{1,0:T(8,128)(2,1)S(1)} collective-permute-done((bf16[256,1024]{1,0:T(8,128)(2,1)S(1)}, bf16[256,1024]{1,0:T(8,128)(2,1)S(1)}, u32[]{:S(2)}, u32[]{:S(2)}) %collective-permute-start.32) | collective-permute-done | bytes 524320 | tf_op jit(solution)/shard_map/ppermute | solution.py:361
  190.1 1.8 collective-permute-start.34
  194.3 11.7 %collective-permute-done.34 = bf16[256,1024]{1,0:T(8,128)(2,1)S(1)} collective-permute-done((bf16[256,1024]{1,0:T(8,128)(2,1)S(1)}, bf16[256,1024]{1,0:T(8,128)(2,1)S(1)}, u32[]{:S(2)}, u32[]{:S(2)}) %collective-permute-start.34) | collective-permute-done | bytes 524320 | tf_op jit(solution)/shard_map/ppermute | solution.py:361
  206.9 2.5 %collective-permute-start.37 = (bf16[256,1024]{1,0:T(8,128)(2,1)S(1)}, bf16[256,1024]{1,0:T(8,128)(2,1)S(1)}, u32[]{:S(2)}, u32[]{:S(2)}) collective-permute-start(bf16[256,1024]{1,0:T(8,128)(2,1)S(1)} %add_convert_fusion.4.refs_1_), channel_id=1, source_target_pairs={{0,24},{8,16},{16,8},{24,0},{1,25},{9,17},{17,9},{25,1},{2,26},{10... | collective-permute-start | bytes 1572872 | tf_op jit(solution)/shard_map/ppermute | solution.py:19
  210.2 8.9 %collective-permute-done.40 = bf16[256,1024]{1,0:T(8,128)(2,1)S(1)} collective-permute-done((bf16[256,1024]{1,0:T(8,128)(2,1)S(1)}, bf16[256,1024]{1,0:T(8,128)(2,1)S(1)}, u32[]{:S(2)}, u32[]{:S(2)}) %collective-permute-start.40) | collective-permute-done | bytes 524320 | tf_op jit(solution)/shard_map/ppermute | solution.py:361
  220.7 1.7 collective-permute-start.43
  223.1 9.3 %collective-permute-done.36.refs_3_ = bf16[256,1024]{1,0:T(8,128)(2,1)S(1)} collective-permute-done((bf16[256,1024]{1,0:T(8,128)(2,1)S(1)}, bf16[256,1024]{1,0:T(8,128)(2,1)S(1)}, u32[]{:S(2)}, u32[]{:S(2)}) %collective-permute-start.36) | collective-permute-done | bytes 524320 | tf_op jit(solution)/shard_map/ppermute | solution.py:19
  234.0 9.0 %shard_map.147 = f32[2048,1024]{1,0:T(8,128)} custom-call(bf16[2048,1024]{1,0:T(8,128)(2,1)} %shard_map.142.refs_0_, bf16[256,1024]{1,0:T(8,128)(2,1)} %copy-done.12, bf16[256,1024]{1,0:T(8,128)(2,1)} %copy-done.32, bf16[256,1024]{1,0:T(8,128)(2,1)} %copy-done.26, bf16[256,1024]{1,0:T(8,128)(2,1)} %copy-done.23), custom_call_target="tpu_custom_call" | custom-call | tf_op jit(solution)/shard_map/pallas_call | solution.py:336
  243.0 2.2 collective-permute-done.45
  (177 shorter events, 39.0 us)
Async XLA Ops:
  0.6 15.6 %collective-permute-start = (bf16[128,2048]{1,0:T(8,128)(2,1)}, bf16[128,2048]{1,0:T(8,128)(2,1)S(1)}, u32[]{:S(2)}, u32[]{:S(2)}) collective-permute-start(bf16[128,2048]{1,0:T(8,128)(2,1)} %refs_0_), channel_id=1, source_target_pairs={{2,0},{3,1},{6,2},{7,3},{0,4},{1,5},{4,6},{5,7},{10,8},{11,9},{14,... | collective-permute-start | bytes 1572872 | tf_op jit(solution)/shard_map/ppermute | solution.py:361
  16.7 14.6 %collective-permute-start.4 = (bf16[128,2048]{1,0:T(8,128)(2,1)S(1)}, bf16[128,2048]{1,0:T(8,128)(2,1)S(1)}, u32[]{:S(2)}, u32[]{:S(2)}) collective-permute-start(bf16[128,2048]{1,0:T(8,128)(2,1)S(1)} %collective-permute-done.refs_2_), channel_id=1, source_target_pairs={{0,2},{1,3},{2,0},{3,1},{4,6},{5,7},{6,4},{7,5},{8,10},{9,11},{10,... | collective-permute-start | bytes 1572872 | tf_op jit(solution)/shard_map/ppermute | solution.py:361
  19.0 12.3 %collective-permute-start.5 = (bf16[128,2048]{1,0:T(8,128)(2,1)}, bf16[128,2048]{1,0:T(8,128)(2,1)}, u32[]{:S(2)}, u32[]{:S(2)}) collective-permute-start(bf16[128,2048]{1,0:T(8,128)(2,1)} %refs_0_), channel_id=1, source_target_pairs={{0,1},{1,0},{2,4},{3,5},{4,2},{5,3},{6,7},{7,6},{8,9},{9,8},{10,12... | collective-permute-start | bytes 1572872 | tf_op jit(solution)/shard_map/ppermute | solution.py:386
  19.0 24.9 %collective-permute-start.3 = (bf16[128,2048]{1,0:T(8,128)(2,1)}, bf16[128,2048]{1,0:T(8,128)(2,1)S(1)}, u32[]{:S(2)}, u32[]{:S(2)}) collective-permute-start(bf16[128,2048]{1,0:T(8,128)(2,1)} %refs_0_), channel_id=1, source_target_pairs={{4,0},{5,1},{0,2},{1,3},{6,4},{7,5},{2,6},{3,7},{12,8},{13,9},{8,1... | collective-permute-start | bytes 1572872 | tf_op jit(solution)/shard_map/ppermute | solution.py:361
  44.6 16.8 %collective-permute-start.9 = (bf16[256,1024]{1,0:T(8,128)(2,1)S(1)}, bf16[256,1024]{1,0:T(8,128)(2,1)S(1)}, u32[]{:S(2)}, u32[]{:S(2)}) collective-permute-start(bf16[256,1024]{1,0:T(8,128)(2,1)S(1)} %copy-done.10), channel_id=1, source_target_pairs={{2,0},{3,1},{6,2},{7,3},{0,4},{1,5},{4,6},{5,7},{10,8},{11,9},{14,... | collective-permute-start | bytes 1572872 | tf_op jit(solution)/shard_map/ppermute | solution.py:361
  57.9 15.1 %collective-permute-start.8 = (bf16[256,1024]{1,0:T(8,128)(2,1)}, bf16[256,1024]{1,0:T(8,128)(2,1)S(1)}, u32[]{:S(2)}, u32[]{:S(2)}) collective-permute-start(bf16[256,1024]{1,0:T(8,128)(2,1)} %get-tuple-element.99), channel_id=1, source_target_pairs={{0,8},{8,0},{16,24},{24,16},{1,9},{9,1},{17,25},{25,17},{2,10},{10... | collective-permute-start | bytes 1572872 | tf_op jit(solution)/shard_map/ppermute | solution.py:19
  59.5 24.8 %collective-permute-start.10 = (bf16[256,1024]{1,0:T(8,128)(2,1)}, bf16[256,1024]{1,0:T(8,128)(2,1)S(1)}, u32[]{:S(2)}, u32[]{:S(2)}) collective-permute-start(bf16[256,1024]{1,0:T(8,128)(2,1)} %get-tuple-element.102), channel_id=1, source_target_pairs={{0,16},{8,24},{16,0},{24,8},{1,17},{9,25},{17,1},{25,9},{2,18},{10... | collective-permute-start | bytes 1572872 | tf_op jit(solution)/shard_map/ppermute | solution.py:19
  61.0 23.3 %collective-permute-start.11 = (bf16[256,1024]{1,0:T(8,128)(2,1)}, bf16[256,1024]{1,0:T(8,128)(2,1)S(1)}, u32[]{:S(2)}, u32[]{:S(2)}) collective-permute-start(bf16[256,1024]{1,0:T(8,128)(2,1)} %get-tuple-element.103), channel_id=1, source_target_pairs={{0,24},{8,16},{16,8},{24,0},{1,25},{9,17},{17,9},{25,1},{2,26},{10... | collective-permute-start | bytes 1572872 | tf_op jit(solution)/shard_map/ppermute | solution.py:19
  61.5 36.3 %collective-permute-start.15 = (bf16[256,1024]{1,0:T(8,128)(2,1)S(1)}, bf16[256,1024]{1,0:T(8,128)(2,1)S(1)}, u32[]{:S(2)}, u32[]{:S(2)}) collective-permute-start(bf16[256,1024]{1,0:T(8,128)(2,1)S(1)} %copy-done.10), channel_id=1, source_target_pairs={{0,1},{1,0},{2,4},{3,5},{4,2},{5,3},{6,7},{7,6},{8,9},{9,8},{10,12... | collective-permute-start | bytes 1572872 | tf_op jit(solution)/shard_map/ppermute | solution.py:386
  61.5 36.9 %collective-permute-start.13 = (bf16[256,1024]{1,0:T(8,128)(2,1)S(1)}, bf16[256,1024]{1,0:T(8,128)(2,1)S(1)}, u32[]{:S(2)}, u32[]{:S(2)}) collective-permute-start(bf16[256,1024]{1,0:T(8,128)(2,1)S(1)} %copy-done.10), channel_id=1, source_target_pairs={{4,0},{5,1},{0,2},{1,3},{6,4},{7,5},{2,6},{3,7},{12,8},{13,9},{8,1... | collective-permute-start | bytes 1572872 | tf_op jit(solution)/shard_map/ppermute | solution.py:361
  73.0 25.3 %collective-permute-start.14 = (bf16[256,1024]{1,0:T(8,128)(2,1)S(1)}, bf16[256,1024]{1,0:T(8,128)(2,1)}, u32[]{:S(2)}, u32[]{:S(2)}) collective-permute-start(bf16[256,1024]{1,0:T(8,128)(2,1)S(1)} %collective-permute-done.9.refs_2_), channel_id=1, source_target_pairs={{0,2},{1,3},{2,0},{3,1},{4,6},{5,7},{6,4},{7,5},{8,10},{9,11},{10,... | collective-permute-start | bytes 1572872 | tf_op jit(solution)/shard_map/ppermute | solution.py:361
  85.7 21.3 %collective-permute-start.12 = (bf16[256,1024]{1,0:T(8,128)(2,1)S(1)}, bf16[256,1024]{1,0:T(8,128)(2,1)S(1)}, u32[]{:S(2)}, u32[]{:S(2)}) collective-permute-start(bf16[256,1024]{1,0:T(8,128)(2,1)S(1)} %add_convert_fusion.8.refs_0_), channel_id=1, source_target_pairs={{2,0},{3,1},{6,2},{7,3},{0,4},{1,5},{4,6},{5,7},{10,8},{11,9},{14,... | collective-permute-start | bytes 1572872 | tf_op jit(solution)/shard_map/ppermute | solution.py:361
  89.7 19.0 %collective-permute-start.19 = (bf16[256,1024]{1,0:T(8,128)(2,1)S(1)}, bf16[256,1024]{1,0:T(8,128)(2,1)S(1)}, u32[]{:S(2)}, u32[]{:S(2)}) collective-permute-start(bf16[256,1024]{1,0:T(8,128)(2,1)S(1)} %copy-done.10), channel_id=1, source_target_pairs={{0,1},{1,0},{2,3},{3,2},{4,5},{5,4},{6,7},{7,6},{8,9},{9,8},{10,11... | collective-permute-start | bytes 1572872 | tf_op jit(solution)/shard_map/ppermute | solution.py:19
  109.2 25.2 %collective-permute-start.16 = (bf16[256,1024]{1,0:T(8,128)(2,1)S(1)}, bf16[256,1024]{1,0:T(8,128)(2,1)S(1)}, u32[]{:S(2)}, u32[]{:S(2)}) collective-permute-start(bf16[256,1024]{1,0:T(8,128)(2,1)S(1)} %collective-permute-done.12.refs_2_), channel_id=1, source_target_pairs={{0,2},{1,3},{2,0},{3,1},{4,6},{5,7},{6,4},{7,5},{8,10},{9,11},{10,... | collective-permute-start | bytes 1572872 | tf_op jit(solution)/shard_map/ppermute | solution.py:361
  109.2 25.1 %collective-permute-start.18 = (bf16[256,1024]{1,0:T(8,128)(2,1)S(1)}, bf16[256,1024]{1,0:T(8,128)(2,1)S(1)}, u32[]{:S(2)}, u32[]{:S(2)}) collective-permute-start(bf16[256,1024]{1,0:T(8,128)(2,1)S(1)} %add_convert_fusion.8.refs_0_), channel_id=1, source_target_pairs={{4,0},{5,1},{0,2},{1,3},{6,4},{7,5},{2,6},{3,7},{12,8},{13,9},{8,1... | collective-permute-start | bytes 1572872 | tf_op jit(solution)/shard_map/ppermute | solution.py:361
  111.2 23.1 %collective-permute-start.17 = (bf16[256,1024]{1,0:T(8,128)(2,1)S(1)}, bf16[256,1024]{1,0:T(8,128)(2,1)S(1)}, u32[]{:S(2)}, u32[]{:S(2)}) collective-permute-start(bf16[256,1024]{1,0:T(8,128)(2,1)S(1)} %add_convert_fusion.8.refs_0_), channel_id=1, source_target_pairs={{0,1},{1,0},{2,4},{3,5},{4,2},{5,3},{6,7},{7,6},{8,9},{9,8},{10,12... | collective-permute-start | bytes 1572872 | tf_op jit(solution)/shard_map/ppermute | solution.py:386
  163.0 17.1 %collective-permute-start.30 = (bf16[256,1024]{1,0:T(8,128)(2,1)S(1)}, bf16[256,1024]{1,0:T(8,128)(2,1)S(1)}, u32[]{:S(2)}, u32[]{:S(2)}) collective-permute-start(bf16[256,1024]{1,0:T(8,128)(2,1)S(1)} %add_convert_fusion.7), channel_id=1, source_target_pairs={{0,1},{1,0},{2,4},{3,5},{4,2},{5,3},{6,7},{7,6},{8,9},{9,8},{10,12... | collective-permute-start | bytes 1572872 | tf_op jit(solution)/shard_map/ppermute | solution.py:406
  163.2 16.9 %collective-permute-start.29 = (bf16[256,1024]{1,0:T(8,128)(2,1)S(1)}, bf16[256,1024]{1,0:T(8,128)(2,1)S(1)}, u32[]{:S(2)}, u32[]{:S(2)}) collective-permute-start(bf16[256,1024]{1,0:T(8,128)(2,1)S(1)} %add_convert_fusion.7), channel_id=1, source_target_pairs={{0,2},{1,3},{2,0},{3,1},{4,6},{5,7},{6,4},{7,5},{8,10},{9,11},{10,... | collective-permute-start | bytes 1572872 | tf_op jit(solution)/shard_map/ppermute | solution.py:361
  167.9 21.9 %collective-permute-start.32 = (bf16[256,1024]{1,0:T(8,128)(2,1)S(1)}, bf16[256,1024]{1,0:T(8,128)(2,1)S(1)}, u32[]{:S(2)}, u32[]{:S(2)}) collective-permute-start(bf16[256,1024]{1,0:T(8,128)(2,1)S(1)} %add_convert_fusion.6), channel_id=1, source_target_pairs={{0,4},{1,5},{2,0},{3,1},{4,6},{5,7},{6,2},{7,3},{8,12},{9,13},{10,... | collective-permute-start | bytes 1572872 | tf_op jit(solution)/shard_map/ppermute | solution.py:361
  167.9 21.9 %collective-permute-start.33 = (bf16[256,1024]{1,0:T(8,128)(2,1)}, bf16[256,1024]{1,0:T(8,128)(2,1)S(1)}, u32[]{:S(2)}, u32[]{:S(2)}) collective-permute-start(bf16[256,1024]{1,0:T(8,128)(2,1)} %get-tuple-element.158), channel_id=1, source_target_pairs={{0,1},{1,0},{2,3},{3,2},{4,5},{5,4},{6,7},{7,6},{8,9},{9,8},{10,11... | collective-permute-start | bytes 1572872 | tf_op jit(solution)/shard_map/ppermute | solution.py:19
  168.0 25.9 %collective-permute-start.27 = (bf16[256,1024]{1,0:T(8,128)(2,1)}, bf16[256,1024]{1,0:T(8,128)(2,1)S(1)}, u32[]{:S(2)}, u32[]{:S(2)}) collective-permute-start(bf16[256,1024]{1,0:T(8,128)(2,1)} %get-tuple-element.131), channel_id=1, source_target_pairs={{0,1},{1,0},{2,3},{3,2},{4,5},{5,4},{6,7},{7,6},{8,9},{9,8},{10,11... | collective-permute-start | bytes 1572872 | tf_op jit(solution)/shard_map/ppermute | solution.py:19
  190.1 15.9 %collective-permute-start.34 = (bf16[256,1024]{1,0:T(8,128)(2,1)S(1)}, bf16[256,1024]{1,0:T(8,128)(2,1)S(1)}, u32[]{:S(2)}, u32[]{:S(2)}) collective-permute-start(bf16[256,1024]{1,0:T(8,128)(2,1)S(1)} %add_convert_fusion.5), channel_id=1, source_target_pairs={{0,2},{1,3},{2,6},{3,7},{4,0},{5,1},{6,4},{7,5},{8,10},{9,11},{10,... | collective-permute-start | bytes 1572872 | tf_op jit(solution)/shard_map/ppermute | solution.py:361
  191.9 51.1 %collective-permute-start.38 = (bf16[256,1024]{1,0:T(8,128)(2,1)}, bf16[256,1024]{1,0:T(8,128)(2,1)S(1)}, u32[]{:S(2)}, u32[]{:S(2)}) collective-permute-start(bf16[256,1024]{1,0:T(8,128)(2,1)} %get-tuple-element.162), channel_id=1, source_target_pairs={{0,1},{1,0},{2,3},{3,2},{4,5},{5,4},{6,7},{7,6},{8,9},{9,8},{10,11... | collective-permute-start | bytes 1572872 | tf_op jit(solution)/shard_map/ppermute | solution.py:19
  192.1 14.8 %collective-permute-start.42 = (bf16[256,1024]{1,0:T(8,128)(2,1)}, bf16[256,1024]{1,0:T(8,128)(2,1)S(1)}, u32[]{:S(2)}, u32[]{:S(2)}) collective-permute-start(bf16[256,1024]{1,0:T(8,128)(2,1)} %get-tuple-element.167), channel_id=1, source_target_pairs={{0,1},{1,0},{2,3},{3,2},{4,5},{5,4},{6,7},{7,6},{8,9},{9,8},{10,11... | collective-permute-start | bytes 1572872 | tf_op jit(solution)/shard_map/ppermute | solution.py:19
  192.4 28.2 %collective-permute-start.44 = (bf16[256,1024]{1,0:T(8,128)(2,1)}, bf16[256,1024]{1,0:T(8,128)(2,1)S(1)}, u32[]{:S(2)}, u32[]{:S(2)}) collective-permute-start(bf16[256,1024]{1,0:T(8,128)(2,1)} %get-tuple-element.169), channel_id=1, source_target_pairs={{0,1},{1,0},{2,3},{3,2},{4,5},{5,4},{6,7},{7,6},{8,9},{9,8},{10,11... | collective-permute-start | bytes 1572872 | tf_op jit(solution)/shard_map/ppermute | solution.py:19
  193.9 15.7 %collective-permute-start.41 = (bf16[256,1024]{1,0:T(8,128)(2,1)S(1)}, bf16[256,1024]{1,0:T(8,128)(2,1)S(1)}, u32[]{:S(2)}, u32[]{:S(2)}) collective-permute-start(bf16[256,1024]{1,0:T(8,128)(2,1)S(1)} %add_convert_fusion.3), channel_id=1, source_target_pairs={{0,1},{1,0},{2,4},{3,5},{4,2},{5,3},{6,7},{7,6},{8,9},{9,8},{10,12... | collective-permute-start | bytes 1572872 | tf_op jit(solution)/shard_map/ppermute | solution.py:406
  206.0 13.2 %collective-permute-start.40 = (bf16[256,1024]{1,0:T(8,128)(2,1)S(1)}, bf16[256,1024]{1,0:T(8,128)(2,1)S(1)}, u32[]{:S(2)}, u32[]{:S(2)}) collective-permute-start(bf16[256,1024]{1,0:T(8,128)(2,1)S(1)} %add_convert_fusion.3), channel_id=1, source_target_pairs={{0,2},{1,3},{2,0},{3,1},{4,6},{5,7},{6,4},{7,5},{8,10},{9,11},{10,... | collective-permute-start | bytes 1572872 | tf_op jit(solution)/shard_map/ppermute | solution.py:361
  206.9 15.8 %collective-permute-start.37 = (bf16[256,1024]{1,0:T(8,128)(2,1)S(1)}, bf16[256,1024]{1,0:T(8,128)(2,1)S(1)}, u32[]{:S(2)}, u32[]{:S(2)}) collective-permute-start(bf16[256,1024]{1,0:T(8,128)(2,1)S(1)} %add_convert_fusion.4.refs_1_), channel_id=1, source_target_pairs={{0,24},{8,16},{16,8},{24,0},{1,25},{9,17},{17,9},{25,1},{2,26},{10... | collective-permute-start | bytes 1572872 | tf_op jit(solution)/shard_map/ppermute | solution.py:19
  209.7 22.7 %collective-permute-start.36 = (bf16[256,1024]{1,0:T(8,128)(2,1)S(1)}, bf16[256,1024]{1,0:T(8,128)(2,1)S(1)}, u32[]{:S(2)}, u32[]{:S(2)}) collective-permute-start(bf16[256,1024]{1,0:T(8,128)(2,1)S(1)} %add_convert_fusion.4.refs_1_), channel_id=1, source_target_pairs={{0,16},{8,24},{16,0},{24,8},{1,17},{9,25},{17,1},{25,9},{2,18},{10... | collective-permute-start | bytes 1572872 | tf_op jit(solution)/shard_map/ppermute | solution.py:19
  219.2 13.3 %collective-permute-start.35 = (bf16[256,1024]{1,0:T(8,128)(2,1)S(1)}, bf16[256,1024]{1,0:T(8,128)(2,1)S(1)}, u32[]{:S(2)}, u32[]{:S(2)}) collective-permute-start(bf16[256,1024]{1,0:T(8,128)(2,1)S(1)} %add_convert_fusion.4.refs_1_), channel_id=1, source_target_pairs={{0,8},{8,0},{16,24},{24,16},{1,9},{9,1},{17,25},{25,17},{2,10},{10... | collective-permute-start | bytes 1572872 | tf_op jit(solution)/shard_map/ppermute | solution.py:19
  220.7 22.3 %collective-permute-start.43 = (bf16[256,1024]{1,0:T(8,128)(2,1)S(1)}, bf16[256,1024]{1,0:T(8,128)(2,1)S(1)}, u32[]{:S(2)}, u32[]{:S(2)}) collective-permute-start(bf16[256,1024]{1,0:T(8,128)(2,1)S(1)} %add_convert_fusion.2), channel_id=1, source_target_pairs={{0,4},{1,5},{2,0},{3,1},{4,6},{5,7},{6,2},{7,3},{8,12},{9,13},{10,... | collective-permute-start | bytes 1572872 | tf_op jit(solution)/shard_map/ppermute | solution.py:361
  222.7 22.5 %collective-permute-start.45 = (bf16[256,1024]{1,0:T(8,128)(2,1)S(1)}, bf16[256,1024]{1,0:T(8,128)(2,1)S(1)}, u32[]{:S(2)}, u32[]{:S(2)}) collective-permute-start(bf16[256,1024]{1,0:T(8,128)(2,1)S(1)} %add_convert_fusion.1), channel_id=1, source_target_pairs={{0,2},{1,3},{2,6},{3,7},{4,0},{5,1},{6,4},{7,5},{8,10},{9,11},{10,... | collective-permute-start | bytes 1572872 | tf_op jit(solution)/shard_map/ppermute | solution.py:361
  (52 other events, 568.5 us)

commit v5 on v4

--- a/solution.py
+++ b/solution.py
@@ -340,7 +340,7 @@
         + [pl.BlockSpec(grad.shape, lambda i: (0, 0)) for grad in grads],
         out_specs=pl.BlockSpec((block, cols), lambda i: (i, 0)),
         out_shape=jax.ShapeDtypeStruct((features.shape[0], cols), jnp.float32),
-        compiler_params=pltpu.CompilerParams(vmem_limit_bytes=VMEM_LIMIT),
+        compiler_params=pltpu.CompilerParams(vmem_limit_bytes=20 * 2**20),
     )(features, *grads)
 
 
@@ -479,7 +479,7 @@
             pltpu.SemaphoreType.DMA((4,)),
             pltpu.SemaphoreType.DMA,
         ],
-        compiler_params=pltpu.CompilerParams(vmem_limit_bytes=VMEM_LIMIT),
+        compiler_params=pltpu.CompilerParams(vmem_limit_bytes=20 * 2**20),
     )(weight, *blocks)
 
 
@@ -499,7 +499,7 @@
             pltpu.SemaphoreType.DMA((4,)),
             pltpu.SemaphoreType.DMA,
         ],
-        compiler_params=pltpu.CompilerParams(vmem_limit_bytes=VMEM_LIMIT),
+        compiler_params=pltpu.CompilerParams(vmem_limit_bytes=24 * 2**20),
     )(rank.reshape(1), token_row, weight, early, *blocks)
     return results[:packs], results[packs]
 
@@ -875,7 +875,6 @@
     second = scatter_second(grad_parts)
     far, (near, attended_parts) = after(far, (near, attended_parts))
     first = scatter_first(grad_parts, far)
-    attended_parts, second = after(attended_parts, second)
     grad_sum = scatter_total(grad_parts, near, second, first)
     grad_hidden = (out_grad.astype(jnp.float32) + grad_sum).astype(jnp.bfloat16)
     every_pack = [grad_hidden] + [

time: 247 us -> 242 us (0.980)
  Pallas kernels: 86.5 us -> 74.4 us
  waiting for transfers between devices: 94.1 us -> 99.7 us
  local copies, waits for them, and re-layouts: 11.7 us -> 15.2 us
    pallas_call x1, Pallas kernels: 9.9 us -> 4.86 us  [line_stitched(): pl.pallas_call(functools.partial(line_stitch_kernel, packs), in_specs=[pl...]
    pallas_call x1, Pallas kernels: 7.04 us -> 2.69 us  [line_stitched_early(): pl.pallas_call(line_stitch_early_kernel, in_specs=[whole] + [far] * 4, ou...]
    unnamed x77 -> x59, local copies, waits for them, and re-layouts: 7.19 us -> 11.3 us
    ppermute x15, waiting for transfers between devices: 62.3 us -> 65.5 us  [along(): return lax.ppermute(value, 'tp', both)]
    pallas_call x1, Pallas kernels: 9.02 us -> 6.39 us  [outer_summed(): pl.pallas_call(outer_kernel, grid=(features.shape[0] // block,), in_specs...]
  transfers between devices with their start and end apart: 46 -> 46, of which waited for: 16 -> 21; matrix products, arithmetic and copies ran while one was open for 7% -> 6% of each run, Pallas kernels for 26% -> 22%
where the time goes in v5:
time: 242 us; the launch traced here: 241 us
  waiting for transfers between devices  99.7 us (41%)
  Pallas kernels  74.4 us (31%)
  starting transfers between devices  38 us (16%)
  local copies, waits for them, and re-layouts  15.2 us (6%)
  other arithmetic  12.8 us (5%)
    ppermute x15, waiting for transfers between devices, along(): return lax.ppermute(value, 'tp', both)  65.5 us
    ppermute x26, waiting for transfers between devices, swapped(): return lax.ppermute(value, axis, pairs)  34.1 us
    ppermute x15, starting transfers between devices, along(): return lax.ppermute(value, 'tp', both)  24.6 us
    pallas_call x1, Pallas kernels, line_middle(): pl.pallas_call(functools.partial(line_middle_kernel, repeat), in_specs=[s...  21.6 us
    ppermute x26, starting transfers between devices, swapped(): return lax.ppermute(value, axis, pairs)  13.2 us
    pallas_call x1, Pallas kernels, line_grad_context(): pl.pallas_call(line_grad_kernel, grid_spec=pltpu.PrefetchScalarGridSpec(n...  11.9 us
    pallas_call x1, Pallas kernels, line_attended(): pl.pallas_call(line_attended_kernel, grid_spec=pltpu.PrefetchScalarGridSp...  11.6 us
    unnamed x59, local copies, waits for them, and re-layouts  11.3 us
  transfers between devices with their start and end apart: 46, of which 21 were waited for; matrix products, arithmetic and copies ran while one was open for 6% of the time, Pallas kernels for 22%

profile of v5, /device:TPU:0, one launch (start us, length us, event | category | flops | bytes accessed | tf_op | source)
XLA Modules:
  0.0 241.3 jit_solution(17407799410474275801)
XLA Ops:
  0.6 4.1 %collective-permute-start = (bf16[128,2048]{1,0:T(8,128)(2,1)}, bf16[128,2048]{1,0:T(8,128)(2,1)S(1)}, u32[]{:S(2)}, u32[]{:S(2)}) collective-permute-start(bf16[128,2048]{1,0:T(8,128)(2,1)} %refs_0_), channel_id=1, source_target_pairs={{2,0},{3,1},{6,2},{7,3},{0,4},{1,5},{4,6},{5,7},{10,8},{11,9},{14,... | collective-permute-start | bytes 1572872 | tf_op jit(solution)/shard_map/ppermute | solution.py:361
  10.5 5.7 %collective-permute-done.refs_2_ = bf16[128,2048]{1,0:T(8,128)(2,1)S(1)} collective-permute-done((bf16[128,2048]{1,0:T(8,128)(2,1)}, bf16[128,2048]{1,0:T(8,128)(2,1)S(1)}, u32[]{:S(2)}, u32[]{:S(2)}) %collective-permute-start) | collective-permute-done | bytes 524320 | tf_op jit(solution)/shard_map/ppermute | solution.py:361
  16.7 2.3 collective-permute-start.4
  19.0 2.3 collective-permute-start.3
  21.3 2.2 copy-done.2
  24.5 2.7 %shard_map.140 = (bf16[512,1024]{1,0:T(8,128)(2,1)S(1)}, bf16[512,2048]{1,0:T(8,128)(2,1)S(1)}) custom-call(bf16[2048,1024]{1,0:T(8,128)(2,1)S(1)} %copy-done.2, bf16[128,2048]{1,0:T(8,128)(2,1)S(1)} %copy-done.7, bf16[128,2048]{1,0:T(8,128)(2,1)S(1)} %collective-permute-done.1.refs_1_, bf16[128,2048]{1,0:T(8,128)(2,1)S(1)} %collective-permute-done.refs_2_, ...), custom_call_target="tpu_custom_call" | custom-call | tf_op jit(solution)/shard_map/pallas_call | solution.py:469
  28.5 2.8 %collective-permute-done.4 = bf16[128,2048]{1,0:T(8,128)(2,1)} collective-permute-done((bf16[128,2048]{1,0:T(8,128)(2,1)S(1)}, bf16[128,2048]{1,0:T(8,128)(2,1)}, u32[]{:S(2)}, u32[]{:S(2)}) %collective-permute-start.4) | collective-permute-done | bytes 524320 | tf_op jit(solution)/shard_map/ppermute | solution.py:361
  31.3 12.6 %collective-permute-done.3.refs_0_ = bf16[128,2048]{1,0:T(8,128)(2,1)S(1)} collective-permute-done((bf16[128,2048]{1,0:T(8,128)(2,1)}, bf16[128,2048]{1,0:T(8,128)(2,1)S(1)}, u32[]{:S(2)}, u32[]{:S(2)}) %collective-permute-start.3) | collective-permute-done | bytes 524320 | tf_op jit(solution)/shard_map/ppermute | solution.py:361
  47.8 2.2 copy-done.3
  50.0 4.9 %shard_map.141 = (bf16[256,1024]{1,0:T(8,128)(2,1)S(1)}, bf16[256,1024]{1,0:T(8,128)(2,1)S(1)}, bf16[256,1024]{1,0:T(8,128)(2,1)S(1)}, bf16[256,1024]{1,0:T(8,128)(2,1)S(1)}, bf16[512,2048]{1,0:T(8,128)(2,1)S(1)}) custom-call(s32[1]{0:T(128)} %bitcast.8.rank_ref, s32[1,1024]{1,0:T(1,128)S(1)} %bitcast.19, bf16[2048,1024]{1,0:T(8,128)(2,1)S(1)} %copy-done.3, ...), custom_call_target="tpu_custom_call" | custom-call | tf_op jit(solution)/shard_map/pallas_call | solution.py:490
  59.9 1.5 collective-permute-start.13
  61.4 9.6 %collective-permute-done.8 = bf16[256,1024]{1,0:T(8,128)(2,1)S(1)} collective-permute-done((bf16[256,1024]{1,0:T(8,128)(2,1)S(1)}, bf16[256,1024]{1,0:T(8,128)(2,1)S(1)}, u32[]{:S(2)}, u32[]{:S(2)}) %collective-permute-start.8) | collective-permute-done | bytes 524320 | tf_op jit(solution)/shard_map/ppermute | solution.py:19
  71.1 11.5 %collective-permute-done.10 = bf16[256,1024]{1,0:T(8,128)(2,1)S(1)} collective-permute-done((bf16[256,1024]{1,0:T(8,128)(2,1)S(1)}, bf16[256,1024]{1,0:T(8,128)(2,1)S(1)}, u32[]{:S(2)}, u32[]{:S(2)}) %collective-permute-start.10) | collective-permute-done | bytes 524320 | tf_op jit(solution)/shard_map/ppermute | solution.py:19
  85.9 8.0 %shard_map.142.refs_0_ = bf16[2048,1024]{1,0:T(8,128)(2,1)} custom-call(s32[1024,1]{1,0:T(8,128)} %copy.26.token_ref, s32[1,1024]{1,0:T(1,128)} %bitcast.23, bf16[512,2048]{1,0:T(8,128)(2,1)} %copy-done.5, bf16[512,2048]{1,0:T(8,128)(2,1)} %copy-done.6), custom_call_target="tpu_custom_call" | custom-call | tf_op jit(solution)/shard_map/pallas_call | solution.py:691
  95.2 10.1 %collective-permute-done.12.refs_2_ = bf16[256,1024]{1,0:T(8,128)(2,1)S(1)} collective-permute-done((bf16[256,1024]{1,0:T(8,128)(2,1)S(1)}, bf16[256,1024]{1,0:T(8,128)(2,1)S(1)}, u32[]{:S(2)}, u32[]{:S(2)}) %collective-permute-start.12) | collective-permute-done | bytes 524320 | tf_op jit(solution)/shard_map/ppermute | solution.py:361
  109.3 7.5 %shard_map.144 = (f32[256,1024]{1,0:T(8,128)}, f32[256,256]{1,0:T(8,128)}, f32[256,1]{1,0:T(8,128)}) custom-call(s32[8]{0:T(128)} %reshape.115.from_ref, f32[1,8192]{1,0:T(1,128)} %bitcast.21, bf16[8192,1024]{1,0:T(8,128)(2,1)} %q_weight_ref.3, bf16[8192,256]{1,0:T(8,128)(2,1)} %kv_weight_ref.3, bf16[256,1024]{1,0:T(8,128)(2,1)} %copy-done.8, ...), custom_call_target="tpu_custom_call" | custom-call | tf_op jit(solution)/shard_map/pallas_call | solution.py:656
  117.8 11.9 %shard_map.143.grad_ref = bf16[256,1024]{1,0:T(8,128)(2,1)} custom-call(s32[4]{0:T(128)} %get-tuple-element.107.chips_ref, s32[1]{0:T(128)} %bitcast.10.core_ref, bf16[1024,8192]{1,0:T(8,128)(2,1)} %weight_ref.7, bf16[256,1024]{1,0:T(8,128)(2,1)} %refs_0_.1, bf16[256,1024]{1,0:T(8,128)(2,1)} %copy-done.19, bf16[256,1024]{1,0:T(8,128)(2,1)} %collective-permute-done.9.refs_2_, ...), custom_call_target="tpu_custom_call" | custom-call | tf_op jit(solution)/shard_map/pallas_call | solution.py:536
  129.7 1.9 collective-permute-done.16
  135.3 21.6 %shard_map.145 = (bf16[256,1024]{1,0:T(8,128)(2,1)}, bf16[256,1024]{1,0:T(8,128)(2,1)}, bf16[256,1024]{1,0:T(8,128)(2,1)}, bf16[256,1024]{1,0:T(8,128)(2,1)}, bf...) custom-call(s32[8]{0:T(128)} %reshape.115.from_ref, ...), custom_call_target="tpu_custom_call" | custom-call | tf_op jit(solution)/shard_map/pallas_call | solution.py:771
  157.4 1.6 collective-permute-done.28
  160.5 3.8 %collective-permute-start.29 = (bf16[256,1024]{1,0:T(8,128)(2,1)S(1)}, bf16[256,1024]{1,0:T(8,128)(2,1)S(1)}, u32[]{:S(2)}, u32[]{:S(2)}) collective-permute-start(bf16[256,1024]{1,0:T(8,128)(2,1)S(1)} %add_convert_fusion.7), channel_id=1, source_target_pairs={{0,2},{1,3},{2,0},{3,1},{4,6},{5,7},{6,4},{7,5},{8,10},{9,11},{10,... | collective-permute-start | bytes 1572872 | tf_op jit(solution)/shard_map/ppermute | solution.py:361
  166.2 11.6 %shard_map.146 = (bf16[256,1024]{1,0:T(8,128)(2,1)}, bf16[256,1024]{1,0:T(8,128)(2,1)}, bf16[256,1024]{1,0:T(8,128)(2,1)}, bf16[256,1024]{1,0:T(8,128)(2,1)}, bf...) custom-call(s32[4]{0:T(128)} %get-tuple-element.125.chips_ref, ...), custom_call_target="tpu_custom_call" | custom-call | tf_op jit(solution)/shard_map/pallas_call | solution.py:574
  178.2 2.1 collective-permute-start.34
  182.3 5.6 %collective-permute-done.32 = bf16[256,1024]{1,0:T(8,128)(2,1)S(1)} collective-permute-done((bf16[256,1024]{1,0:T(8,128)(2,1)S(1)}, bf16[256,1024]{1,0:T(8,128)(2,1)S(1)}, u32[]{:S(2)}, u32[]{:S(2)}) %collective-permute-start.32) | collective-permute-done | bytes 524320 | tf_op jit(solution)/shard_map/ppermute | solution.py:361
  187.9 11.8 %collective-permute-done.34 = bf16[256,1024]{1,0:T(8,128)(2,1)S(1)} collective-permute-done((bf16[256,1024]{1,0:T(8,128)(2,1)S(1)}, bf16[256,1024]{1,0:T(8,128)(2,1)S(1)}, u32[]{:S(2)}, u32[]{:S(2)}) %collective-permute-start.34) | collective-permute-done | bytes 524320 | tf_op jit(solution)/shard_map/ppermute | solution.py:361
  200.5 1.7 add_convert_fusion.4.refs_1_
  202.2 2.5 %collective-permute-start.37 = (bf16[256,1024]{1,0:T(8,128)(2,1)S(1)}, bf16[256,1024]{1,0:T(8,128)(2,1)S(1)}, u32[]{:S(2)}, u32[]{:S(2)}) collective-permute-start(bf16[256,1024]{1,0:T(8,128)(2,1)S(1)} %add_convert_fusion.4.refs_1_), channel_id=1, source_target_pairs={{0,24},{8,16},{16,8},{24,0},{1,25},{9,17},{17,9},{25,1},{2,26},{10... | collective-permute-start | bytes 1572872 | tf_op jit(solution)/shard_map/ppermute | solution.py:19
  205.5 8.1 %collective-permute-done.40 = bf16[256,1024]{1,0:T(8,128)(2,1)S(1)} collective-permute-done((bf16[256,1024]{1,0:T(8,128)(2,1)S(1)}, bf16[256,1024]{1,0:T(8,128)(2,1)S(1)}, u32[]{:S(2)}, u32[]{:S(2)}) %collective-permute-start.40) | collective-permute-done | bytes 524320 | tf_op jit(solution)/shard_map/ppermute | solution.py:361
  216.8 2.5 %collective-permute-start.45 = (bf16[256,1024]{1,0:T(8,128)(2,1)S(1)}, bf16[256,1024]{1,0:T(8,128)(2,1)S(1)}, u32[]{:S(2)}, u32[]{:S(2)}) collective-permute-start(bf16[256,1024]{1,0:T(8,128)(2,1)S(1)} %add_convert_fusion.1), channel_id=1, source_target_pairs={{0,2},{1,3},{2,6},{3,7},{4,0},{5,1},{6,4},{7,5},{8,10},{9,11},{10,... | collective-permute-start | bytes 1572872 | tf_op jit(solution)/shard_map/ppermute | solution.py:361
  219.3 8.2 %collective-permute-done.36.refs_3_ = bf16[256,1024]{1,0:T(8,128)(2,1)S(1)} collective-permute-done((bf16[256,1024]{1,0:T(8,128)(2,1)S(1)}, bf16[256,1024]{1,0:T(8,128)(2,1)S(1)}, u32[]{:S(2)}, u32[]{:S(2)}) %collective-permute-start.36) | collective-permute-done | bytes 524320 | tf_op jit(solution)/shard_map/ppermute | solution.py:19
  227.6 6.4 %shard_map.147 = f32[2048,1024]{1,0:T(8,128)} custom-call(bf16[2048,1024]{1,0:T(8,128)(2,1)S(1)} %copy-done.4, bf16[256,1024]{1,0:T(8,128)(2,1)S(1)} %add_convert_fusion.4.refs_1_, bf16[256,1024]{1,0:T(8,128)(2,1)S(1)} %collective-permute-done.35.refs_2_, bf16[256,1024]{1,0:T(8,128)(2,1)S(1)} %collective-permute-done.36.refs_3_, ...), custom_call_target="tpu_custom_call" | custom-call | tf_op jit(solution)/shard_map/pallas_call | solution.py:336
  234.0 5.8 %collective-permute-done.45 = bf16[256,1024]{1,0:T(8,128)(2,1)S(1)} collective-permute-done((bf16[256,1024]{1,0:T(8,128)(2,1)S(1)}, bf16[256,1024]{1,0:T(8,128)(2,1)S(1)}, u32[]{:S(2)}, u32[]{:S(2)}) %collective-permute-start.45) | collective-permute-done | bytes 524320 | tf_op jit(solution)/shard_map/ppermute | solution.py:361
  (159 shorter events, 43.1 us)
Async XLA Ops:
  0.6 15.6 %collective-permute-start = (bf16[128,2048]{1,0:T(8,128)(2,1)}, bf16[128,2048]{1,0:T(8,128)(2,1)S(1)}, u32[]{:S(2)}, u32[]{:S(2)}) collective-permute-start(bf16[128,2048]{1,0:T(8,128)(2,1)} %refs_0_), channel_id=1, source_target_pairs={{2,0},{3,1},{6,2},{7,3},{0,4},{1,5},{4,6},{5,7},{10,8},{11,9},{14,... | collective-permute-start | bytes 1572872 | tf_op jit(solution)/shard_map/ppermute | solution.py:361
  16.7 14.6 %collective-permute-start.4 = (bf16[128,2048]{1,0:T(8,128)(2,1)S(1)}, bf16[128,2048]{1,0:T(8,128)(2,1)}, u32[]{:S(2)}, u32[]{:S(2)}) collective-permute-start(bf16[128,2048]{1,0:T(8,128)(2,1)S(1)} %collective-permute-done.refs_2_), channel_id=1, source_target_pairs={{0,2},{1,3},{2,0},{3,1},{4,6},{5,7},{6,4},{7,5},{8,10},{9,11},{10,... | collective-permute-start | bytes 1572872 | tf_op jit(solution)/shard_map/ppermute | solution.py:361
  19.0 24.9 %collective-permute-start.3 = (bf16[128,2048]{1,0:T(8,128)(2,1)}, bf16[128,2048]{1,0:T(8,128)(2,1)S(1)}, u32[]{:S(2)}, u32[]{:S(2)}) collective-permute-start(bf16[128,2048]{1,0:T(8,128)(2,1)} %refs_0_), channel_id=1, source_target_pairs={{4,0},{5,1},{0,2},{1,3},{6,4},{7,5},{2,6},{3,7},{12,8},{13,9},{8,1... | collective-permute-start | bytes 1572872 | tf_op jit(solution)/shard_map/ppermute | solution.py:361
  45.6 14.2 %collective-permute-start.9 = (bf16[256,1024]{1,0:T(8,128)(2,1)}, bf16[256,1024]{1,0:T(8,128)(2,1)}, u32[]{:S(2)}, u32[]{:S(2)}) collective-permute-start(bf16[256,1024]{1,0:T(8,128)(2,1)} %refs_0_.1), channel_id=1, source_target_pairs={{2,0},{3,1},{6,2},{7,3},{0,4},{1,5},{4,6},{5,7},{10,8},{11,9},{14,... | collective-permute-start | bytes 1572872 | tf_op jit(solution)/shard_map/ppermute | solution.py:361
  56.2 14.8 %collective-permute-start.8 = (bf16[256,1024]{1,0:T(8,128)(2,1)S(1)}, bf16[256,1024]{1,0:T(8,128)(2,1)S(1)}, u32[]{:S(2)}, u32[]{:S(2)}) collective-permute-start(bf16[256,1024]{1,0:T(8,128)(2,1)S(1)} %get-tuple-element.90), channel_id=1, source_target_pairs={{0,8},{8,0},{16,24},{24,16},{1,9},{9,1},{17,25},{25,17},{2,10},{10... | collective-permute-start | bytes 1572872 | tf_op jit(solution)/shard_map/ppermute | solution.py:19
  57.7 24.9 %collective-permute-start.10 = (bf16[256,1024]{1,0:T(8,128)(2,1)S(1)}, bf16[256,1024]{1,0:T(8,128)(2,1)S(1)}, u32[]{:S(2)}, u32[]{:S(2)}) collective-permute-start(bf16[256,1024]{1,0:T(8,128)(2,1)S(1)} %get-tuple-element.93), channel_id=1, source_target_pairs={{0,16},{8,24},{16,0},{24,8},{1,17},{9,25},{17,1},{25,9},{2,18},{10... | collective-permute-start | bytes 1572872 | tf_op jit(solution)/shard_map/ppermute | solution.py:19
  59.2 23.4 %collective-permute-start.11 = (bf16[256,1024]{1,0:T(8,128)(2,1)S(1)}, bf16[256,1024]{1,0:T(8,128)(2,1)S(1)}, u32[]{:S(2)}, u32[]{:S(2)}) collective-permute-start(bf16[256,1024]{1,0:T(8,128)(2,1)S(1)} %get-tuple-element.94), channel_id=1, source_target_pairs={{0,24},{8,16},{16,8},{24,0},{1,25},{9,17},{17,9},{25,1},{2,26},{10... | collective-permute-start | bytes 1572872 | tf_op jit(solution)/shard_map/ppermute | solution.py:19
  59.7 34.2 %collective-permute-start.15 = (bf16[256,1024]{1,0:T(8,128)(2,1)}, bf16[256,1024]{1,0:T(8,128)(2,1)S(1)}, u32[]{:S(2)}, u32[]{:S(2)}) collective-permute-start(bf16[256,1024]{1,0:T(8,128)(2,1)} %refs_0_.1), channel_id=1, source_target_pairs={{0,1},{1,0},{2,4},{3,5},{4,2},{5,3},{6,7},{7,6},{8,9},{9,8},{10,12... | collective-permute-start | bytes 1572872 | tf_op jit(solution)/shard_map/ppermute | solution.py:386
  59.9 34.5 %collective-permute-start.13 = (bf16[256,1024]{1,0:T(8,128)(2,1)}, bf16[256,1024]{1,0:T(8,128)(2,1)S(1)}, u32[]{:S(2)}, u32[]{:S(2)}) collective-permute-start(bf16[256,1024]{1,0:T(8,128)(2,1)} %refs_0_.1), channel_id=1, source_target_pairs={{4,0},{5,1},{0,2},{1,3},{6,4},{7,5},{2,6},{3,7},{12,8},{13,9},{8,1... | collective-permute-start | bytes 1572872 | tf_op jit(solution)/shard_map/ppermute | solution.py:361
  71.0 24.2 %collective-permute-start.14 = (bf16[256,1024]{1,0:T(8,128)(2,1)}, bf16[256,1024]{1,0:T(8,128)(2,1)S(1)}, u32[]{:S(2)}, u32[]{:S(2)}) collective-permute-start(bf16[256,1024]{1,0:T(8,128)(2,1)} %collective-permute-done.9.refs_2_), channel_id=1, source_target_pairs={{0,2},{1,3},{2,0},{3,1},{4,6},{5,7},{6,4},{7,5},{8,10},{9,11},{10,... | collective-permute-start | bytes 1572872 | tf_op jit(solution)/shard_map/ppermute | solution.py:361
  83.0 22.3 %collective-permute-start.12 = (bf16[256,1024]{1,0:T(8,128)(2,1)S(1)}, bf16[256,1024]{1,0:T(8,128)(2,1)S(1)}, u32[]{:S(2)}, u32[]{:S(2)}) collective-permute-start(bf16[256,1024]{1,0:T(8,128)(2,1)S(1)} %add_convert_fusion.8.refs_0_), channel_id=1, source_target_pairs={{2,0},{3,1},{6,2},{7,3},{0,4},{1,5},{4,6},{5,7},{10,8},{11,9},{14,... | collective-permute-start | bytes 1572872 | tf_op jit(solution)/shard_map/ppermute | solution.py:361
  85.9 20.0 %collective-permute-start.19 = (bf16[256,1024]{1,0:T(8,128)(2,1)}, bf16[256,1024]{1,0:T(8,128)(2,1)S(1)}, u32[]{:S(2)}, u32[]{:S(2)}) collective-permute-start(bf16[256,1024]{1,0:T(8,128)(2,1)} %refs_0_.1), channel_id=1, source_target_pairs={{0,1},{1,0},{2,3},{3,2},{4,5},{5,4},{6,7},{7,6},{8,9},{9,8},{10,11... | collective-permute-start | bytes 1572872 | tf_op jit(solution)/shard_map/ppermute | solution.py:19
  93.9 12.6 %collective-permute-start.20 = (bf16[256,1024]{1,0:T(8,128)(2,1)}, bf16[256,1024]{1,0:T(8,128)(2,1)S(1)}, u32[]{:S(2)}, u32[]{:S(2)}) collective-permute-start(bf16[256,1024]{1,0:T(8,128)(2,1)} %collective-permute-done.9.refs_2_), channel_id=1, source_target_pairs={{0,1},{1,0},{2,3},{3,2},{4,5},{5,4},{6,7},{7,6},{8,9},{9,8},{10,11... | collective-permute-start | bytes 1572872 | tf_op jit(solution)/shard_map/ppermute | solution.py:19
  106.4 25.2 %collective-permute-start.16 = (bf16[256,1024]{1,0:T(8,128)(2,1)S(1)}, bf16[256,1024]{1,0:T(8,128)(2,1)S(1)}, u32[]{:S(2)}, u32[]{:S(2)}) collective-permute-start(bf16[256,1024]{1,0:T(8,128)(2,1)S(1)} %collective-permute-done.12.refs_2_), channel_id=1, source_target_pairs={{0,2},{1,3},{2,0},{3,1},{4,6},{5,7},{6,4},{7,5},{8,10},{9,11},{10,... | collective-permute-start | bytes 1572872 | tf_op jit(solution)/shard_map/ppermute | solution.py:361
  107.2 24.4 %collective-permute-start.18 = (bf16[256,1024]{1,0:T(8,128)(2,1)S(1)}, bf16[256,1024]{1,0:T(8,128)(2,1)S(1)}, u32[]{:S(2)}, u32[]{:S(2)}) collective-permute-start(bf16[256,1024]{1,0:T(8,128)(2,1)S(1)} %add_convert_fusion.8.refs_0_), channel_id=1, source_target_pairs={{4,0},{5,1},{0,2},{1,3},{6,4},{7,5},{2,6},{3,7},{12,8},{13,9},{8,1... | collective-permute-start | bytes 1572872 | tf_op jit(solution)/shard_map/ppermute | solution.py:361
  108.5 23.1 %collective-permute-start.17 = (bf16[256,1024]{1,0:T(8,128)(2,1)S(1)}, bf16[256,1024]{1,0:T(8,128)(2,1)S(1)}, u32[]{:S(2)}, u32[]{:S(2)}) collective-permute-start(bf16[256,1024]{1,0:T(8,128)(2,1)S(1)} %add_convert_fusion.8.refs_0_), channel_id=1, source_target_pairs={{0,1},{1,0},{2,4},{3,5},{4,2},{5,3},{6,7},{7,6},{8,9},{9,8},{10,12... | collective-permute-start | bytes 1572872 | tf_op jit(solution)/shard_map/ppermute | solution.py:386
  160.3 17.5 %collective-permute-start.30 = (bf16[256,1024]{1,0:T(8,128)(2,1)S(1)}, bf16[256,1024]{1,0:T(8,128)(2,1)S(1)}, u32[]{:S(2)}, u32[]{:S(2)}) collective-permute-start(bf16[256,1024]{1,0:T(8,128)(2,1)S(1)} %add_convert_fusion.7), channel_id=1, source_target_pairs={{0,1},{1,0},{2,4},{3,5},{4,2},{5,3},{6,7},{7,6},{8,9},{9,8},{10,12... | collective-permute-start | bytes 1572872 | tf_op jit(solution)/shard_map/ppermute | solution.py:406
  160.5 17.3 %collective-permute-start.29 = (bf16[256,1024]{1,0:T(8,128)(2,1)S(1)}, bf16[256,1024]{1,0:T(8,128)(2,1)S(1)}, u32[]{:S(2)}, u32[]{:S(2)}) collective-permute-start(bf16[256,1024]{1,0:T(8,128)(2,1)S(1)} %add_convert_fusion.7), channel_id=1, source_target_pairs={{0,2},{1,3},{2,0},{3,1},{4,6},{5,7},{6,4},{7,5},{8,10},{9,11},{10,... | collective-permute-start | bytes 1572872 | tf_op jit(solution)/shard_map/ppermute | solution.py:361
  164.3 13.5 %collective-permute-start.33 = (bf16[256,1024]{1,0:T(8,128)(2,1)}, bf16[256,1024]{1,0:T(8,128)(2,1)S(1)}, u32[]{:S(2)}, u32[]{:S(2)}) collective-permute-start(bf16[256,1024]{1,0:T(8,128)(2,1)} %get-tuple-element.140), channel_id=1, source_target_pairs={{0,1},{1,0},{2,3},{3,2},{4,5},{5,4},{6,7},{7,6},{8,9},{9,8},{10,11... | collective-permute-start | bytes 1572872 | tf_op jit(solution)/shard_map/ppermute | solution.py:19
  164.3 17.7 %collective-permute-start.27 = (bf16[256,1024]{1,0:T(8,128)(2,1)}, bf16[256,1024]{1,0:T(8,128)(2,1)S(1)}, u32[]{:S(2)}, u32[]{:S(2)}) collective-permute-start(bf16[256,1024]{1,0:T(8,128)(2,1)} %get-tuple-element.122), channel_id=1, source_target_pairs={{0,1},{1,0},{2,3},{3,2},{4,5},{5,4},{6,7},{7,6},{8,9},{9,8},{10,11... | collective-permute-start | bytes 1572872 | tf_op jit(solution)/shard_map/ppermute | solution.py:19
  166.1 21.8 %collective-permute-start.32 = (bf16[256,1024]{1,0:T(8,128)(2,1)S(1)}, bf16[256,1024]{1,0:T(8,128)(2,1)S(1)}, u32[]{:S(2)}, u32[]{:S(2)}) collective-permute-start(bf16[256,1024]{1,0:T(8,128)(2,1)S(1)} %add_convert_fusion.6), channel_id=1, source_target_pairs={{0,4},{1,5},{2,0},{3,1},{4,6},{5,7},{6,2},{7,3},{8,12},{9,13},{10,... | collective-permute-start | bytes 1572872 | tf_op jit(solution)/shard_map/ppermute | solution.py:361
  178.2 21.6 %collective-permute-start.34 = (bf16[256,1024]{1,0:T(8,128)(2,1)S(1)}, bf16[256,1024]{1,0:T(8,128)(2,1)S(1)}, u32[]{:S(2)}, u32[]{:S(2)}) collective-permute-start(bf16[256,1024]{1,0:T(8,128)(2,1)S(1)} %add_convert_fusion.5), channel_id=1, source_target_pairs={{0,2},{1,3},{2,6},{3,7},{4,0},{5,1},{6,4},{7,5},{8,10},{9,11},{10,... | collective-permute-start | bytes 1572872 | tf_op jit(solution)/shard_map/ppermute | solution.py:361
  180.3 53.7 %collective-permute-start.38 = (bf16[256,1024]{1,0:T(8,128)(2,1)}, bf16[256,1024]{1,0:T(8,128)(2,1)S(1)}, u32[]{:S(2)}, u32[]{:S(2)}) collective-permute-start(bf16[256,1024]{1,0:T(8,128)(2,1)} %get-tuple-element.144), channel_id=1, source_target_pairs={{0,1},{1,0},{2,3},{3,2},{4,5},{5,4},{6,7},{7,6},{8,9},{9,8},{10,11... | collective-permute-start | bytes 1572872 | tf_op jit(solution)/shard_map/ppermute | solution.py:19
  180.5 21.7 %collective-permute-start.42 = (bf16[256,1024]{1,0:T(8,128)(2,1)}, bf16[256,1024]{1,0:T(8,128)(2,1)S(1)}, u32[]{:S(2)}, u32[]{:S(2)}) collective-permute-start(bf16[256,1024]{1,0:T(8,128)(2,1)} %get-tuple-element.149), channel_id=1, source_target_pairs={{0,1},{1,0},{2,3},{3,2},{4,5},{5,4},{6,7},{7,6},{8,9},{9,8},{10,11... | collective-permute-start | bytes 1572872 | tf_op jit(solution)/shard_map/ppermute | solution.py:19
  182.0 33.0 %collective-permute-start.44 = (bf16[256,1024]{1,0:T(8,128)(2,1)}, bf16[256,1024]{1,0:T(8,128)(2,1)S(1)}, u32[]{:S(2)}, u32[]{:S(2)}) collective-permute-start(bf16[256,1024]{1,0:T(8,128)(2,1)} %get-tuple-element.151), channel_id=1, source_target_pairs={{0,1},{1,0},{2,3},{3,2},{4,5},{5,4},{6,7},{7,6},{8,9},{9,8},{10,11... | collective-permute-start | bytes 1572872 | tf_op jit(solution)/shard_map/ppermute | solution.py:19
  187.9 17.0 %collective-permute-start.41 = (bf16[256,1024]{1,0:T(8,128)(2,1)S(1)}, bf16[256,1024]{1,0:T(8,128)(2,1)S(1)}, u32[]{:S(2)}, u32[]{:S(2)}) collective-permute-start(bf16[256,1024]{1,0:T(8,128)(2,1)S(1)} %add_convert_fusion.3), channel_id=1, source_target_pairs={{0,1},{1,0},{2,4},{3,5},{4,2},{5,3},{6,7},{7,6},{8,9},{9,8},{10,12... | collective-permute-start | bytes 1572872 | tf_op jit(solution)/shard_map/ppermute | solution.py:406
  199.7 13.9 %collective-permute-start.40 = (bf16[256,1024]{1,0:T(8,128)(2,1)S(1)}, bf16[256,1024]{1,0:T(8,128)(2,1)S(1)}, u32[]{:S(2)}, u32[]{:S(2)}) collective-permute-start(bf16[256,1024]{1,0:T(8,128)(2,1)S(1)} %add_convert_fusion.3), channel_id=1, source_target_pairs={{0,2},{1,3},{2,0},{3,1},{4,6},{5,7},{6,4},{7,5},{8,10},{9,11},{10,... | collective-permute-start | bytes 1572872 | tf_op jit(solution)/shard_map/ppermute | solution.py:361
  202.2 14.5 %collective-permute-start.37 = (bf16[256,1024]{1,0:T(8,128)(2,1)S(1)}, bf16[256,1024]{1,0:T(8,128)(2,1)S(1)}, u32[]{:S(2)}, u32[]{:S(2)}) collective-permute-start(bf16[256,1024]{1,0:T(8,128)(2,1)S(1)} %add_convert_fusion.4.refs_1_), channel_id=1, source_target_pairs={{0,24},{8,16},{16,8},{24,0},{1,25},{9,17},{17,9},{25,1},{2,26},{10... | collective-permute-start | bytes 1572872 | tf_op jit(solution)/shard_map/ppermute | solution.py:19
  204.9 22.6 %collective-permute-start.36 = (bf16[256,1024]{1,0:T(8,128)(2,1)S(1)}, bf16[256,1024]{1,0:T(8,128)(2,1)S(1)}, u32[]{:S(2)}, u32[]{:S(2)}) collective-permute-start(bf16[256,1024]{1,0:T(8,128)(2,1)S(1)} %add_convert_fusion.4.refs_1_), channel_id=1, source_target_pairs={{0,16},{8,24},{16,0},{24,8},{1,17},{9,25},{17,1},{25,9},{2,18},{10... | collective-permute-start | bytes 1572872 | tf_op jit(solution)/shard_map/ppermute | solution.py:19
  213.6 14.0 %collective-permute-start.35 = (bf16[256,1024]{1,0:T(8,128)(2,1)S(1)}, bf16[256,1024]{1,0:T(8,128)(2,1)S(1)}, u32[]{:S(2)}, u32[]{:S(2)}) collective-permute-start(bf16[256,1024]{1,0:T(8,128)(2,1)S(1)} %add_convert_fusion.4.refs_1_), channel_id=1, source_target_pairs={{0,8},{8,0},{16,24},{24,16},{1,9},{9,1},{17,25},{25,17},{2,10},{10... | collective-permute-start | bytes 1572872 | tf_op jit(solution)/shard_map/ppermute | solution.py:19
  215.1 18.9 %collective-permute-start.43 = (bf16[256,1024]{1,0:T(8,128)(2,1)S(1)}, bf16[256,1024]{1,0:T(8,128)(2,1)S(1)}, u32[]{:S(2)}, u32[]{:S(2)}) collective-permute-start(bf16[256,1024]{1,0:T(8,128)(2,1)S(1)} %add_convert_fusion.2), channel_id=1, source_target_pairs={{0,4},{1,5},{2,0},{3,1},{4,6},{5,7},{6,2},{7,3},{8,12},{9,13},{10,... | collective-permute-start | bytes 1572872 | tf_op jit(solution)/shard_map/ppermute | solution.py:361
  216.8 23.1 %collective-permute-start.45 = (bf16[256,1024]{1,0:T(8,128)(2,1)S(1)}, bf16[256,1024]{1,0:T(8,128)(2,1)S(1)}, u32[]{:S(2)}, u32[]{:S(2)}) collective-permute-start(bf16[256,1024]{1,0:T(8,128)(2,1)S(1)} %add_convert_fusion.1), channel_id=1, source_target_pairs={{0,2},{1,3},{2,6},{3,7},{4,0},{5,1},{6,4},{7,5},{8,10},{9,11},{10,... | collective-permute-start | bytes 1572872 | tf_op jit(solution)/shard_map/ppermute | solution.py:361
  (43 other events, 417.7 us)

commit v6 on v5

--- a/solution.py
+++ b/solution.py
@@ -882,9 +882,10 @@
     ]
     _, far, near = scatter_begun(attended_parts)
     second = scatter_second(attended_parts)
-    far, near = after(far, near)
     first = scatter_first(attended_parts, far)
-    late_hidden, *every_pack = lax.optimization_barrier((hidden_bf, *every_pack))
+    late_hidden, near, second, *every_pack = lax.optimization_barrier(
+        (hidden_bf, near, second, *every_pack)
+    )
     stitch_grad = outer_summed(tokens_last, every_pack)
     attended = scatter_total(attended_parts, near, second, first)
     layer_out = (late_hidden.astype(jnp.float32) + attended).astype(jnp.bfloat16)

time: 242 us -> 241 us (level)
    ppermute x26, waiting for transfers between devices: 34.1 us -> 31 us  [swapped(): return lax.ppermute(value, axis, pairs)]
    unnamed x59 -> x63, local copies, waits for them, and re-layouts: 11.3 us -> 11.3 us
  transfers between devices with their start and end apart: 46 -> 46, of which waited for: 21 -> 22; matrix products, arithmetic and copies ran while one was open for 6% -> 5% of each run, Pallas kernels for 22% -> 22%
where the time goes in v6:
time: 241 us; the launch traced here: 240 us
  waiting for transfers between devices  98.2 us (41%)
  Pallas kernels  74.5 us (31%)
  starting transfers between devices  39.3 us (16%)
  local copies, waits for them, and re-layouts  15.2 us (6%)
  other arithmetic  11.8 us (5%)
    ppermute x15, waiting for transfers between devices, along(): return lax.ppermute(value, 'tp', both)  67.2 us
    ppermute x26, waiting for transfers between devices, swapped(): return lax.ppermute(value, axis, pairs)  31 us
    ppermute x15, starting transfers between devices, along(): return lax.ppermute(value, 'tp', both)  25.7 us
    pallas_call x1, Pallas kernels, line_middle(): pl.pallas_call(functools.partial(line_middle_kernel, repeat), in_specs=[s...  21.6 us
    ppermute x26, starting transfers between devices, swapped(): return lax.ppermute(value, axis, pairs)  13 us
    pallas_call x1, Pallas kernels, line_grad_context(): pl.pallas_call(line_grad_kernel, grid_spec=pltpu.PrefetchScalarGridSpec(n...  11.9 us
    pallas_call x1, Pallas kernels, line_attended(): pl.pallas_call(line_attended_kernel, grid_spec=pltpu.PrefetchScalarGridSp...  11.6 us
    unnamed x63, local copies, waits for them, and re-layouts  11.3 us
  transfers between devices with their start and end apart: 46, of which 22 were waited for; matrix products, arithmetic and copies ran while one was open for 5% of the time, Pallas kernels for 22%

profile of v6, /device:TPU:0, one launch (start us, length us, event | category | flops | bytes accessed | tf_op | source)
XLA Modules:
  0.0 240.3 jit_solution(2869869907757011907)
XLA Ops:
  0.6 4.1 %collective-permute-start = (bf16[128,2048]{1,0:T(8,128)(2,1)}, bf16[128,2048]{1,0:T(8,128)(2,1)S(1)}, u32[]{:S(2)}, u32[]{:S(2)}) collective-permute-start(bf16[128,2048]{1,0:T(8,128)(2,1)} %refs_0_), channel_id=1, source_target_pairs={{2,0},{3,1},{6,2},{7,3},{0,4},{1,5},{4,6},{5,7},{10,8},{11,9},{14,... | collective-permute-start | bytes 1572872 | tf_op jit(solution)/shard_map/ppermute | solution.py:361
  10.6 5.7 %collective-permute-done.refs_2_ = bf16[128,2048]{1,0:T(8,128)(2,1)S(1)} collective-permute-done((bf16[128,2048]{1,0:T(8,128)(2,1)}, bf16[128,2048]{1,0:T(8,128)(2,1)S(1)}, u32[]{:S(2)}, u32[]{:S(2)}) %collective-permute-start) | collective-permute-done | bytes 524320 | tf_op jit(solution)/shard_map/ppermute | solution.py:361
  16.7 2.3 collective-permute-start.4
  19.0 2.3 collective-permute-start.3
  21.3 2.2 copy-done.2
  24.5 2.7 %shard_map.140 = (bf16[512,1024]{1,0:T(8,128)(2,1)S(1)}, bf16[512,2048]{1,0:T(8,128)(2,1)S(1)}) custom-call(bf16[2048,1024]{1,0:T(8,128)(2,1)S(1)} %copy-done.2, bf16[128,2048]{1,0:T(8,128)(2,1)S(1)} %copy-done.7, bf16[128,2048]{1,0:T(8,128)(2,1)S(1)} %collective-permute-done.1.refs_1_, bf16[128,2048]{1,0:T(8,128)(2,1)S(1)} %collective-permute-done.refs_2_, ...), custom_call_target="tpu_custom_call" | custom-call | tf_op jit(solution)/shard_map/pallas_call | solution.py:469
  28.5 2.8 %collective-permute-done.4 = bf16[128,2048]{1,0:T(8,128)(2,1)} collective-permute-done((bf16[128,2048]{1,0:T(8,128)(2,1)S(1)}, bf16[128,2048]{1,0:T(8,128)(2,1)}, u32[]{:S(2)}, u32[]{:S(2)}) %collective-permute-start.4) | collective-permute-done | bytes 524320 | tf_op jit(solution)/shard_map/ppermute | solution.py:361
  31.3 12.6 %collective-permute-done.3.refs_0_ = bf16[128,2048]{1,0:T(8,128)(2,1)S(1)} collective-permute-done((bf16[128,2048]{1,0:T(8,128)(2,1)}, bf16[128,2048]{1,0:T(8,128)(2,1)S(1)}, u32[]{:S(2)}, u32[]{:S(2)}) %collective-permute-start.3) | collective-permute-done | bytes 524320 | tf_op jit(solution)/shard_map/ppermute | solution.py:361
  47.8 2.2 copy-done.3
  50.0 4.9 %shard_map.141 = (bf16[256,1024]{1,0:T(8,128)(2,1)S(1)}, bf16[256,1024]{1,0:T(8,128)(2,1)S(1)}, bf16[256,1024]{1,0:T(8,128)(2,1)S(1)}, bf16[256,1024]{1,0:T(8,128)(2,1)S(1)}, bf16[512,2048]{1,0:T(8,128)(2,1)S(1)}) custom-call(s32[1]{0:T(128)} %bitcast.8.rank_ref, s32[1,1024]{1,0:T(1,128)S(1)} %bitcast.19, bf16[2048,1024]{1,0:T(8,128)(2,1)S(1)} %copy-done.3, ...), custom_call_target="tpu_custom_call" | custom-call | tf_op jit(solution)/shard_map/pallas_call | solution.py:490
  61.4 9.6 %collective-permute-done.8 = bf16[256,1024]{1,0:T(8,128)(2,1)S(1)} collective-permute-done((bf16[256,1024]{1,0:T(8,128)(2,1)S(1)}, bf16[256,1024]{1,0:T(8,128)(2,1)S(1)}, u32[]{:S(2)}, u32[]{:S(2)}) %collective-permute-start.8) | collective-permute-done | bytes 524320 | tf_op jit(solution)/shard_map/ppermute | solution.py:19
  71.1 11.5 %collective-permute-done.10 = bf16[256,1024]{1,0:T(8,128)(2,1)S(1)} collective-permute-done((bf16[256,1024]{1,0:T(8,128)(2,1)S(1)}, bf16[256,1024]{1,0:T(8,128)(2,1)S(1)}, u32[]{:S(2)}, u32[]{:S(2)}) %collective-permute-start.10) | collective-permute-done | bytes 524320 | tf_op jit(solution)/shard_map/ppermute | solution.py:19
  85.9 8.0 %shard_map.142.refs_0_ = bf16[2048,1024]{1,0:T(8,128)(2,1)} custom-call(s32[1024,1]{1,0:T(8,128)} %copy.26.token_ref, s32[1,1024]{1,0:T(1,128)} %bitcast.23, bf16[512,2048]{1,0:T(8,128)(2,1)} %copy-done.5, bf16[512,2048]{1,0:T(8,128)(2,1)} %copy-done.6), custom_call_target="tpu_custom_call" | custom-call | tf_op jit(solution)/shard_map/pallas_call | solution.py:691
  95.2 10.1 %collective-permute-done.12.refs_2_ = bf16[256,1024]{1,0:T(8,128)(2,1)S(1)} collective-permute-done((bf16[256,1024]{1,0:T(8,128)(2,1)S(1)}, bf16[256,1024]{1,0:T(8,128)(2,1)S(1)}, u32[]{:S(2)}, u32[]{:S(2)}) %collective-permute-start.12) | collective-permute-done | bytes 524320 | tf_op jit(solution)/shard_map/ppermute | solution.py:361
  109.3 7.5 %shard_map.144 = (f32[256,1024]{1,0:T(8,128)}, f32[256,256]{1,0:T(8,128)}, f32[256,1]{1,0:T(8,128)}) custom-call(s32[8]{0:T(128)} %reshape.115.from_ref, f32[1,8192]{1,0:T(1,128)} %bitcast.21, bf16[8192,1024]{1,0:T(8,128)(2,1)} %q_weight_ref.3, bf16[8192,256]{1,0:T(8,128)(2,1)} %kv_weight_ref.3, bf16[256,1024]{1,0:T(8,128)(2,1)} %copy-done.8, ...), custom_call_target="tpu_custom_call" | custom-call | tf_op jit(solution)/shard_map/pallas_call | solution.py:656
  117.8 11.9 %shard_map.143.grad_ref = bf16[256,1024]{1,0:T(8,128)(2,1)} custom-call(s32[4]{0:T(128)} %get-tuple-element.107.chips_ref, s32[1]{0:T(128)} %bitcast.10.core_ref, bf16[1024,8192]{1,0:T(8,128)(2,1)} %weight_ref.7, bf16[256,1024]{1,0:T(8,128)(2,1)} %refs_0_.1, bf16[256,1024]{1,0:T(8,128)(2,1)} %copy-done.19, bf16[256,1024]{1,0:T(8,128)(2,1)} %collective-permute-done.9.refs_2_, ...), custom_call_target="tpu_custom_call" | custom-call | tf_op jit(solution)/shard_map/pallas_call | solution.py:536
  129.8 1.8 collective-permute-done.16
  135.3 21.6 %shard_map.145 = (bf16[256,1024]{1,0:T(8,128)(2,1)}, bf16[256,1024]{1,0:T(8,128)(2,1)}, bf16[256,1024]{1,0:T(8,128)(2,1)}, bf16[256,1024]{1,0:T(8,128)(2,1)}, bf...) custom-call(s32[8]{0:T(128)} %reshape.115.from_ref, ...), custom_call_target="tpu_custom_call" | custom-call | tf_op jit(solution)/shard_map/pallas_call | solution.py:771
  157.1 2.0 collective-permute-done.27
  160.5 3.8 %collective-permute-start.28 = (bf16[256,1024]{1,0:T(8,128)(2,1)S(1)}, bf16[256,1024]{1,0:T(8,128)(2,1)S(1)}, u32[]{:S(2)}, u32[]{:S(2)}) collective-permute-start(bf16[256,1024]{1,0:T(8,128)(2,1)S(1)} %add_convert_fusion.7), channel_id=1, source_target_pairs={{0,2},{1,3},{2,0},{3,1},{4,6},{5,7},{6,4},{7,5},{8,10},{9,11},{10,... | collective-permute-start | bytes 1572872 | tf_op jit(solution)/shard_map/ppermute | solution.py:361
  164.8 11.6 %shard_map.146 = (bf16[256,1024]{1,0:T(8,128)(2,1)}, bf16[256,1024]{1,0:T(8,128)(2,1)}, bf16[256,1024]{1,0:T(8,128)(2,1)}, bf16[256,1024]{1,0:T(8,128)(2,1)}, bf...) custom-call(s32[4]{0:T(128)} %get-tuple-element.123.chips_ref, ...), custom_call_target="tpu_custom_call" | custom-call | tf_op jit(solution)/shard_map/pallas_call | solution.py:574
  181.4 2.0 collective-permute-start.44
  183.8 8.3 %collective-permute-done.36 = bf16[256,1024]{1,0:T(8,128)(2,1)S(1)} collective-permute-done((bf16[256,1024]{1,0:T(8,128)(2,1)S(1)}, bf16[256,1024]{1,0:T(8,128)(2,1)S(1)}, u32[]{:S(2)}, u32[]{:S(2)}) %collective-permute-start.36) | collective-permute-done | bytes 524320 | tf_op jit(solution)/shard_map/ppermute | solution.py:361
  192.2 1.6 collective-permute-start.33
  193.7 10.5 %collective-permute-done.38 = bf16[256,1024]{1,0:T(8,128)(2,1)S(1)} collective-permute-done((bf16[256,1024]{1,0:T(8,128)(2,1)S(1)}, bf16[256,1024]{1,0:T(8,128)(2,1)S(1)}, u32[]{:S(2)}, u32[]{:S(2)}) %collective-permute-start.38) | collective-permute-done | bytes 524320 | tf_op jit(solution)/shard_map/ppermute | solution.py:361
  204.3 1.7 add_convert_fusion.2.refs_1_
  206.0 2.5 %collective-permute-start.41 = (bf16[256,1024]{1,0:T(8,128)(2,1)S(1)}, bf16[256,1024]{1,0:T(8,128)(2,1)S(1)}, u32[]{:S(2)}, u32[]{:S(2)}) collective-permute-start(bf16[256,1024]{1,0:T(8,128)(2,1)S(1)} %add_convert_fusion.2.refs_1_), channel_id=1, source_target_pairs={{0,24},{8,16},{16,8},{24,0},{1,25},{9,17},{17,9},{25,1},{2,26},{10... | collective-permute-start | bytes 1572872 | tf_op jit(solution)/shard_map/ppermute | solution.py:19
  209.0 5.5 %collective-permute-done.44 = bf16[256,1024]{1,0:T(8,128)(2,1)S(1)} collective-permute-done((bf16[256,1024]{1,0:T(8,128)(2,1)S(1)}, bf16[256,1024]{1,0:T(8,128)(2,1)S(1)}, u32[]{:S(2)}, u32[]{:S(2)}) %collective-permute-start.44) | collective-permute-done | bytes 524320 | tf_op jit(solution)/shard_map/ppermute | solution.py:361
  216.4 8.4 %collective-permute-done.33 = bf16[256,1024]{1,0:T(8,128)(2,1)S(1)} collective-permute-done((bf16[256,1024]{1,0:T(8,128)(2,1)S(1)}, bf16[256,1024]{1,0:T(8,128)(2,1)S(1)}, u32[]{:S(2)}, u32[]{:S(2)}) %collective-permute-start.33) | collective-permute-done | bytes 524320 | tf_op jit(solution)/shard_map/ppermute | solution.py:361
  224.9 2.4 %collective-permute-start.45 = (bf16[256,1024]{1,0:T(8,128)(2,1)S(1)}, bf16[256,1024]{1,0:T(8,128)(2,1)S(1)}, u32[]{:S(2)}, u32[]{:S(2)}) collective-permute-start(bf16[256,1024]{1,0:T(8,128)(2,1)S(1)} %add_convert_fusion.1), channel_id=1, source_target_pairs={{0,2},{1,3},{2,6},{3,7},{4,0},{5,1},{6,4},{7,5},{8,10},{9,11},{10,... | collective-permute-start | bytes 1572872 | tf_op jit(solution)/shard_map/ppermute | solution.py:361
  227.3 4.7 %collective-permute-done.40.refs_3_ = bf16[256,1024]{1,0:T(8,128)(2,1)S(1)} collective-permute-done((bf16[256,1024]{1,0:T(8,128)(2,1)S(1)}, bf16[256,1024]{1,0:T(8,128)(2,1)S(1)}, u32[]{:S(2)}, u32[]{:S(2)}) %collective-permute-start.40) | collective-permute-done | bytes 524320 | tf_op jit(solution)/shard_map/ppermute | solution.py:19
  232.1 6.4 %shard_map.147 = f32[2048,1024]{1,0:T(8,128)} custom-call(bf16[2048,1024]{1,0:T(8,128)(2,1)S(1)} %copy-done.4, bf16[256,1024]{1,0:T(8,128)(2,1)S(1)} %add_convert_fusion.2.refs_1_, bf16[256,1024]{1,0:T(8,128)(2,1)S(1)} %collective-permute-done.39.refs_2_, bf16[256,1024]{1,0:T(8,128)(2,1)S(1)} %collective-permute-done.40.refs_3_, ...), custom_call_target="tpu_custom_call" | custom-call | tf_op jit(solution)/shard_map/pallas_call | solution.py:336
  (163 shorter events, 44.1 us)
Async XLA Ops:
  0.6 15.6 %collective-permute-start = (bf16[128,2048]{1,0:T(8,128)(2,1)}, bf16[128,2048]{1,0:T(8,128)(2,1)S(1)}, u32[]{:S(2)}, u32[]{:S(2)}) collective-permute-start(bf16[128,2048]{1,0:T(8,128)(2,1)} %refs_0_), channel_id=1, source_target_pairs={{2,0},{3,1},{6,2},{7,3},{0,4},{1,5},{4,6},{5,7},{10,8},{11,9},{14,... | collective-permute-start | bytes 1572872 | tf_op jit(solution)/shard_map/ppermute | solution.py:361
  16.7 14.6 %collective-permute-start.4 = (bf16[128,2048]{1,0:T(8,128)(2,1)S(1)}, bf16[128,2048]{1,0:T(8,128)(2,1)}, u32[]{:S(2)}, u32[]{:S(2)}) collective-permute-start(bf16[128,2048]{1,0:T(8,128)(2,1)S(1)} %collective-permute-done.refs_2_), channel_id=1, source_target_pairs={{0,2},{1,3},{2,0},{3,1},{4,6},{5,7},{6,4},{7,5},{8,10},{9,11},{10,... | collective-permute-start | bytes 1572872 | tf_op jit(solution)/shard_map/ppermute | solution.py:361
  19.0 24.9 %collective-permute-start.3 = (bf16[128,2048]{1,0:T(8,128)(2,1)}, bf16[128,2048]{1,0:T(8,128)(2,1)S(1)}, u32[]{:S(2)}, u32[]{:S(2)}) collective-permute-start(bf16[128,2048]{1,0:T(8,128)(2,1)} %refs_0_), channel_id=1, source_target_pairs={{4,0},{5,1},{0,2},{1,3},{6,4},{7,5},{2,6},{3,7},{12,8},{13,9},{8,1... | collective-permute-start | bytes 1572872 | tf_op jit(solution)/shard_map/ppermute | solution.py:361
  45.6 14.2 %collective-permute-start.9 = (bf16[256,1024]{1,0:T(8,128)(2,1)}, bf16[256,1024]{1,0:T(8,128)(2,1)}, u32[]{:S(2)}, u32[]{:S(2)}) collective-permute-start(bf16[256,1024]{1,0:T(8,128)(2,1)} %refs_0_.1), channel_id=1, source_target_pairs={{2,0},{3,1},{6,2},{7,3},{0,4},{1,5},{4,6},{5,7},{10,8},{11,9},{14,... | collective-permute-start | bytes 1572872 | tf_op jit(solution)/shard_map/ppermute | solution.py:361
  56.2 14.8 %collective-permute-start.8 = (bf16[256,1024]{1,0:T(8,128)(2,1)S(1)}, bf16[256,1024]{1,0:T(8,128)(2,1)S(1)}, u32[]{:S(2)}, u32[]{:S(2)}) collective-permute-start(bf16[256,1024]{1,0:T(8,128)(2,1)S(1)} %get-tuple-element.90), channel_id=1, source_target_pairs={{0,8},{8,0},{16,24},{24,16},{1,9},{9,1},{17,25},{25,17},{2,10},{10... | collective-permute-start | bytes 1572872 | tf_op jit(solution)/shard_map/ppermute | solution.py:19
  57.7 24.9 %collective-permute-start.10 = (bf16[256,1024]{1,0:T(8,128)(2,1)S(1)}, bf16[256,1024]{1,0:T(8,128)(2,1)S(1)}, u32[]{:S(2)}, u32[]{:S(2)}) collective-permute-start(bf16[256,1024]{1,0:T(8,128)(2,1)S(1)} %get-tuple-element.93), channel_id=1, source_target_pairs={{0,16},{8,24},{16,0},{24,8},{1,17},{9,25},{17,1},{25,9},{2,18},{10... | collective-permute-start | bytes 1572872 | tf_op jit(solution)/shard_map/ppermute | solution.py:19
  59.2 23.4 %collective-permute-start.11 = (bf16[256,1024]{1,0:T(8,128)(2,1)S(1)}, bf16[256,1024]{1,0:T(8,128)(2,1)S(1)}, u32[]{:S(2)}, u32[]{:S(2)}) collective-permute-start(bf16[256,1024]{1,0:T(8,128)(2,1)S(1)} %get-tuple-element.94), channel_id=1, source_target_pairs={{0,24},{8,16},{16,8},{24,0},{1,25},{9,17},{17,9},{25,1},{2,26},{10... | collective-permute-start | bytes 1572872 | tf_op jit(solution)/shard_map/ppermute | solution.py:19
  59.7 34.1 %collective-permute-start.15 = (bf16[256,1024]{1,0:T(8,128)(2,1)}, bf16[256,1024]{1,0:T(8,128)(2,1)S(1)}, u32[]{:S(2)}, u32[]{:S(2)}) collective-permute-start(bf16[256,1024]{1,0:T(8,128)(2,1)} %refs_0_.1), channel_id=1, source_target_pairs={{0,1},{1,0},{2,4},{3,5},{4,2},{5,3},{6,7},{7,6},{8,9},{9,8},{10,12... | collective-permute-start | bytes 1572872 | tf_op jit(solution)/shard_map/ppermute | solution.py:386
  59.9 34.5 %collective-permute-start.13 = (bf16[256,1024]{1,0:T(8,128)(2,1)}, bf16[256,1024]{1,0:T(8,128)(2,1)S(1)}, u32[]{:S(2)}, u32[]{:S(2)}) collective-permute-start(bf16[256,1024]{1,0:T(8,128)(2,1)} %refs_0_.1), channel_id=1, source_target_pairs={{4,0},{5,1},{0,2},{1,3},{6,4},{7,5},{2,6},{3,7},{12,8},{13,9},{8,1... | collective-permute-start | bytes 1572872 | tf_op jit(solution)/shard_map/ppermute | solution.py:361
  71.0 24.2 %collective-permute-start.14 = (bf16[256,1024]{1,0:T(8,128)(2,1)}, bf16[256,1024]{1,0:T(8,128)(2,1)S(1)}, u32[]{:S(2)}, u32[]{:S(2)}) collective-permute-start(bf16[256,1024]{1,0:T(8,128)(2,1)} %collective-permute-done.9.refs_2_), channel_id=1, source_target_pairs={{0,2},{1,3},{2,0},{3,1},{4,6},{5,7},{6,4},{7,5},{8,10},{9,11},{10,... | collective-permute-start | bytes 1572872 | tf_op jit(solution)/shard_map/ppermute | solution.py:361
  83.0 22.3 %collective-permute-start.12 = (bf16[256,1024]{1,0:T(8,128)(2,1)S(1)}, bf16[256,1024]{1,0:T(8,128)(2,1)S(1)}, u32[]{:S(2)}, u32[]{:S(2)}) collective-permute-start(bf16[256,1024]{1,0:T(8,128)(2,1)S(1)} %add_convert_fusion.8.refs_0_), channel_id=1, source_target_pairs={{2,0},{3,1},{6,2},{7,3},{0,4},{1,5},{4,6},{5,7},{10,8},{11,9},{14,... | collective-permute-start | bytes 1572872 | tf_op jit(solution)/shard_map/ppermute | solution.py:361
  85.9 20.1 %collective-permute-start.19 = (bf16[256,1024]{1,0:T(8,128)(2,1)}, bf16[256,1024]{1,0:T(8,128)(2,1)S(1)}, u32[]{:S(2)}, u32[]{:S(2)}) collective-permute-start(bf16[256,1024]{1,0:T(8,128)(2,1)} %refs_0_.1), channel_id=1, source_target_pairs={{0,1},{1,0},{2,3},{3,2},{4,5},{5,4},{6,7},{7,6},{8,9},{9,8},{10,11... | collective-permute-start | bytes 1572872 | tf_op jit(solution)/shard_map/ppermute | solution.py:19
  93.8 12.6 %collective-permute-start.20 = (bf16[256,1024]{1,0:T(8,128)(2,1)}, bf16[256,1024]{1,0:T(8,128)(2,1)S(1)}, u32[]{:S(2)}, u32[]{:S(2)}) collective-permute-start(bf16[256,1024]{1,0:T(8,128)(2,1)} %collective-permute-done.9.refs_2_), channel_id=1, source_target_pairs={{0,1},{1,0},{2,3},{3,2},{4,5},{5,4},{6,7},{7,6},{8,9},{9,8},{10,11... | collective-permute-start | bytes 1572872 | tf_op jit(solution)/shard_map/ppermute | solution.py:19
  106.4 25.2 %collective-permute-start.16 = (bf16[256,1024]{1,0:T(8,128)(2,1)S(1)}, bf16[256,1024]{1,0:T(8,128)(2,1)S(1)}, u32[]{:S(2)}, u32[]{:S(2)}) collective-permute-start(bf16[256,1024]{1,0:T(8,128)(2,1)S(1)} %collective-permute-done.12.refs_2_), channel_id=1, source_target_pairs={{0,2},{1,3},{2,0},{3,1},{4,6},{5,7},{6,4},{7,5},{8,10},{9,11},{10,... | collective-permute-start | bytes 1572872 | tf_op jit(solution)/shard_map/ppermute | solution.py:361
  107.2 24.4 %collective-permute-start.18 = (bf16[256,1024]{1,0:T(8,128)(2,1)S(1)}, bf16[256,1024]{1,0:T(8,128)(2,1)S(1)}, u32[]{:S(2)}, u32[]{:S(2)}) collective-permute-start(bf16[256,1024]{1,0:T(8,128)(2,1)S(1)} %add_convert_fusion.8.refs_0_), channel_id=1, source_target_pairs={{4,0},{5,1},{0,2},{1,3},{6,4},{7,5},{2,6},{3,7},{12,8},{13,9},{8,1... | collective-permute-start | bytes 1572872 | tf_op jit(solution)/shard_map/ppermute | solution.py:361
  108.5 23.1 %collective-permute-start.17 = (bf16[256,1024]{1,0:T(8,128)(2,1)S(1)}, bf16[256,1024]{1,0:T(8,128)(2,1)S(1)}, u32[]{:S(2)}, u32[]{:S(2)}) collective-permute-start(bf16[256,1024]{1,0:T(8,128)(2,1)S(1)} %add_convert_fusion.8.refs_0_), channel_id=1, source_target_pairs={{0,1},{1,0},{2,4},{3,5},{4,2},{5,3},{6,7},{7,6},{8,9},{9,8},{10,12... | collective-permute-start | bytes 1572872 | tf_op jit(solution)/shard_map/ppermute | solution.py:386
  160.3 16.1 %collective-permute-start.29 = (bf16[256,1024]{1,0:T(8,128)(2,1)S(1)}, bf16[256,1024]{1,0:T(8,128)(2,1)S(1)}, u32[]{:S(2)}, u32[]{:S(2)}) collective-permute-start(bf16[256,1024]{1,0:T(8,128)(2,1)S(1)} %add_convert_fusion.7), channel_id=1, source_target_pairs={{0,1},{1,0},{2,4},{3,5},{4,2},{5,3},{6,7},{7,6},{8,9},{9,8},{10,12... | collective-permute-start | bytes 1572872 | tf_op jit(solution)/shard_map/ppermute | solution.py:406
  160.5 15.9 %collective-permute-start.28 = (bf16[256,1024]{1,0:T(8,128)(2,1)S(1)}, bf16[256,1024]{1,0:T(8,128)(2,1)S(1)}, u32[]{:S(2)}, u32[]{:S(2)}) collective-permute-start(bf16[256,1024]{1,0:T(8,128)(2,1)S(1)} %add_convert_fusion.7), channel_id=1, source_target_pairs={{0,2},{1,3},{2,0},{3,1},{4,6},{5,7},{6,4},{7,5},{8,10},{9,11},{10,... | collective-permute-start | bytes 1572872 | tf_op jit(solution)/shard_map/ppermute | solution.py:361
  164.3 12.7 %collective-permute-start.35 = (bf16[256,1024]{1,0:T(8,128)(2,1)}, bf16[256,1024]{1,0:T(8,128)(2,1)S(1)}, u32[]{:S(2)}, u32[]{:S(2)}) collective-permute-start(bf16[256,1024]{1,0:T(8,128)(2,1)} %get-tuple-element.142), channel_id=1, source_target_pairs={{0,1},{1,0},{2,3},{3,2},{4,5},{5,4},{6,7},{7,6},{8,9},{9,8},{10,11... | collective-permute-start | bytes 1572872 | tf_op jit(solution)/shard_map/ppermute | solution.py:19
  164.3 14.0 %collective-permute-start.37 = (bf16[256,1024]{1,0:T(8,128)(2,1)}, bf16[256,1024]{1,0:T(8,128)(2,1)S(1)}, u32[]{:S(2)}, u32[]{:S(2)}) collective-permute-start(bf16[256,1024]{1,0:T(8,128)(2,1)} %get-tuple-element.144), channel_id=1, source_target_pairs={{0,1},{1,0},{2,3},{3,2},{4,5},{5,4},{6,7},{7,6},{8,9},{9,8},{10,11... | collective-permute-start | bytes 1572872 | tf_op jit(solution)/shard_map/ppermute | solution.py:19
  164.8 18.7 %collective-permute-start.34 = (bf16[256,1024]{1,0:T(8,128)(2,1)}, bf16[256,1024]{1,0:T(8,128)(2,1)S(1)}, u32[]{:S(2)}, u32[]{:S(2)}) collective-permute-start(bf16[256,1024]{1,0:T(8,128)(2,1)} %get-tuple-element.139), channel_id=1, source_target_pairs={{0,1},{1,0},{2,3},{3,2},{4,5},{5,4},{6,7},{7,6},{8,9},{9,8},{10,11... | collective-permute-start | bytes 1572872 | tf_op jit(solution)/shard_map/ppermute | solution.py:19
  177.2 14.9 %collective-permute-start.36 = (bf16[256,1024]{1,0:T(8,128)(2,1)S(1)}, bf16[256,1024]{1,0:T(8,128)(2,1)S(1)}, u32[]{:S(2)}, u32[]{:S(2)}) collective-permute-start(bf16[256,1024]{1,0:T(8,128)(2,1)S(1)} %add_convert_fusion.4), channel_id=1, source_target_pairs={{0,4},{1,5},{2,0},{3,1},{4,6},{5,7},{6,2},{7,3},{8,12},{9,13},{10,... | collective-permute-start | bytes 1572872 | tf_op jit(solution)/shard_map/ppermute | solution.py:361
  178.6 25.7 %collective-permute-start.38 = (bf16[256,1024]{1,0:T(8,128)(2,1)S(1)}, bf16[256,1024]{1,0:T(8,128)(2,1)S(1)}, u32[]{:S(2)}, u32[]{:S(2)}) collective-permute-start(bf16[256,1024]{1,0:T(8,128)(2,1)S(1)} %add_convert_fusion.3), channel_id=1, source_target_pairs={{0,2},{1,3},{2,6},{3,7},{4,0},{5,1},{6,4},{7,5},{8,10},{9,11},{10,... | collective-permute-start | bytes 1572872 | tf_op jit(solution)/shard_map/ppermute | solution.py:361
  179.9 28.6 %collective-permute-start.43 = (bf16[256,1024]{1,0:T(8,128)(2,1)}, bf16[256,1024]{1,0:T(8,128)(2,1)S(1)}, u32[]{:S(2)}, u32[]{:S(2)}) collective-permute-start(bf16[256,1024]{1,0:T(8,128)(2,1)} %get-tuple-element.152), channel_id=1, source_target_pairs={{0,1},{1,0},{2,3},{3,2},{4,5},{5,4},{6,7},{7,6},{8,9},{9,8},{10,11... | collective-permute-start | bytes 1572872 | tf_op jit(solution)/shard_map/ppermute | solution.py:19
  181.4 33.2 %collective-permute-start.44 = (bf16[256,1024]{1,0:T(8,128)(2,1)S(1)}, bf16[256,1024]{1,0:T(8,128)(2,1)S(1)}, u32[]{:S(2)}, u32[]{:S(2)}) collective-permute-start(bf16[256,1024]{1,0:T(8,128)(2,1)S(1)} %add_convert_fusion.6), channel_id=1, source_target_pairs={{0,2},{1,3},{2,0},{3,1},{4,6},{5,7},{6,4},{7,5},{8,10},{9,11},{10,... | collective-permute-start | bytes 1572872 | tf_op jit(solution)/shard_map/ppermute | solution.py:361
  183.6 32.8 %collective-permute-start.31 = (bf16[256,1024]{1,0:T(8,128)(2,1)S(1)}, bf16[256,1024]{1,0:T(8,128)(2,1)S(1)}, u32[]{:S(2)}, u32[]{:S(2)}) collective-permute-start(bf16[256,1024]{1,0:T(8,128)(2,1)S(1)} %add_convert_fusion.6), channel_id=1, source_target_pairs={{0,1},{1,0},{2,4},{3,5},{4,2},{5,3},{6,7},{7,6},{8,9},{9,8},{10,12... | collective-permute-start | bytes 1572872 | tf_op jit(solution)/shard_map/ppermute | solution.py:406
  192.2 32.7 %collective-permute-start.33 = (bf16[256,1024]{1,0:T(8,128)(2,1)S(1)}, bf16[256,1024]{1,0:T(8,128)(2,1)S(1)}, u32[]{:S(2)}, u32[]{:S(2)}) collective-permute-start(bf16[256,1024]{1,0:T(8,128)(2,1)S(1)} %add_convert_fusion.5), channel_id=1, source_target_pairs={{0,4},{1,5},{2,0},{3,1},{4,6},{5,7},{6,2},{7,3},{8,12},{9,13},{10,... | collective-permute-start | bytes 1572872 | tf_op jit(solution)/shard_map/ppermute | solution.py:361
  206.0 21.3 %collective-permute-start.41 = (bf16[256,1024]{1,0:T(8,128)(2,1)S(1)}, bf16[256,1024]{1,0:T(8,128)(2,1)S(1)}, u32[]{:S(2)}, u32[]{:S(2)}) collective-permute-start(bf16[256,1024]{1,0:T(8,128)(2,1)S(1)} %add_convert_fusion.2.refs_1_), channel_id=1, source_target_pairs={{0,24},{8,16},{16,8},{24,0},{1,25},{9,17},{17,9},{25,1},{2,26},{10... | collective-permute-start | bytes 1572872 | tf_op jit(solution)/shard_map/ppermute | solution.py:19
  208.5 23.5 %collective-permute-start.40 = (bf16[256,1024]{1,0:T(8,128)(2,1)S(1)}, bf16[256,1024]{1,0:T(8,128)(2,1)S(1)}, u32[]{:S(2)}, u32[]{:S(2)}) collective-permute-start(bf16[256,1024]{1,0:T(8,128)(2,1)S(1)} %add_convert_fusion.2.refs_1_), channel_id=1, source_target_pairs={{0,16},{8,24},{16,0},{24,8},{1,17},{9,25},{17,1},{25,9},{2,18},{10... | collective-permute-start | bytes 1572872 | tf_op jit(solution)/shard_map/ppermute | solution.py:19
  214.5 17.5 %collective-permute-start.39 = (bf16[256,1024]{1,0:T(8,128)(2,1)S(1)}, bf16[256,1024]{1,0:T(8,128)(2,1)S(1)}, u32[]{:S(2)}, u32[]{:S(2)}) collective-permute-start(bf16[256,1024]{1,0:T(8,128)(2,1)S(1)} %add_convert_fusion.2.refs_1_), channel_id=1, source_target_pairs={{0,8},{8,0},{16,24},{24,16},{1,9},{9,1},{17,25},{25,17},{2,10},{10... | collective-permute-start | bytes 1572872 | tf_op jit(solution)/shard_map/ppermute | solution.py:19
  216.4 22.1 %collective-permute-start.42 = (bf16[256,1024]{1,0:T(8,128)(2,1)S(1)}, bf16[256,1024]{1,0:T(8,128)(2,1)S(1)}, u32[]{:S(2)}, u32[]{:S(2)}) collective-permute-start(bf16[256,1024]{1,0:T(8,128)(2,1)S(1)} %copy-done.30), channel_id=1, source_target_pairs={{0,1},{1,0},{2,3},{3,2},{4,5},{5,4},{6,7},{7,6},{8,9},{9,8},{10,11... | collective-permute-start | bytes 1572872 | tf_op jit(solution)/shard_map/ppermute | solution.py:19
  224.9 14.0 %collective-permute-start.45 = (bf16[256,1024]{1,0:T(8,128)(2,1)S(1)}, bf16[256,1024]{1,0:T(8,128)(2,1)S(1)}, u32[]{:S(2)}, u32[]{:S(2)}) collective-permute-start(bf16[256,1024]{1,0:T(8,128)(2,1)S(1)} %add_convert_fusion.1), channel_id=1, source_target_pairs={{0,2},{1,3},{2,6},{3,7},{4,0},{5,1},{6,4},{7,5},{8,10},{9,11},{10,... | collective-permute-start | bytes 1572872 | tf_op jit(solution)/shard_map/ppermute | solution.py:361
  (45 other events, 435.6 us)

commit v7 on v6

--- a/solution.py
+++ b/solution.py
@@ -842,6 +842,8 @@
     received = [swapped(placed[distance], "tok", distance) for distance in range(1, packs)]
     received[0], og_first = after(received[0], og_first)
     og_second, og_last = gather_second(out_grad), gather_last(out_grad, og_first)
+    received[1], (og_second, og_near) = after(received[1], (og_second, og_last[1]))
+    og_last = (og_last[0], og_near)
     hidden = placed[0].astype(jnp.float32)
     for part in received:
         hidden += part.astype(jnp.float32)

time: 241 us -> 241 us (level)
    ppermute x26, waiting for transfers between devices: 31 us -> 18 us  [swapped(): return lax.ppermute(value, axis, pairs)]
    ppermute x15, waiting for transfers between devices: 67.2 us -> 79.5 us  [along(): return lax.ppermute(value, 'tp', both)]
    unnamed x63 -> x67, local copies, waits for them, and re-layouts: 11.3 us -> 11.3 us
  transfers between devices with their start and end apart: 46 -> 46, of which waited for: 22 -> 21; matrix products, arithmetic and copies ran while one was open for 5% -> 5% of each run, Pallas kernels for 22% -> 22%
where the time goes in v7:
time: 241 us
  waiting for transfers between devices  97.5 us (40%)
  Pallas kernels  74.5 us (31%)
  starting transfers between devices  41.1 us (17%)
  local copies, waits for them, and re-layouts  15.2 us (6%)
  other arithmetic  11.2 us (5%)
    ppermute x15, waiting for transfers between devices, along(): return lax.ppermute(value, 'tp', both)  79.5 us
    ppermute x15, starting transfers between devices, along(): return lax.ppermute(value, 'tp', both)  26.6 us
    pallas_call x1, Pallas kernels, line_middle(): pl.pallas_call(functools.partial(line_middle_kernel, repeat), in_specs=[s...  21.6 us
    ppermute x26, waiting for transfers between devices, swapped(): return lax.ppermute(value, axis, pairs)  18 us
    ppermute x26, starting transfers between devices, swapped(): return lax.ppermute(value, axis, pairs)  14 us
    pallas_call x1, Pallas kernels, line_grad_context(): pl.pallas_call(line_grad_kernel, grid_spec=pltpu.PrefetchScalarGridSpec(n...  11.9 us
    pallas_call x1, Pallas kernels, line_attended(): pl.pallas_call(line_attended_kernel, grid_spec=pltpu.PrefetchScalarGridSp...  11.6 us
    unnamed x67, local copies, waits for them, and re-layouts  11.3 us
  transfers between devices with their start and end apart: 46, of which 21 were waited for; matrix products, arithmetic and copies ran while one was open for 5% of the time, Pallas kernels for 22%

profile of v7, /device:TPU:0, one launch (start us, length us, event | category | flops | bytes accessed | tf_op | source)
XLA Modules:
  0.0 240.7 jit_solution(1522188336196824530)
XLA Ops:
  0.6 4.1 %collective-permute-start = (bf16[128,2048]{1,0:T(8,128)(2,1)}, bf16[128,2048]{1,0:T(8,128)(2,1)S(1)}, u32[]{:S(2)}, u32[]{:S(2)}) collective-permute-start(bf16[128,2048]{1,0:T(8,128)(2,1)} %refs_0_), channel_id=1, source_target_pairs={{2,0},{3,1},{6,2},{7,3},{0,4},{1,5},{4,6},{5,7},{10,8},{11,9},{14,... | collective-permute-start | bytes 1572872 | tf_op jit(solution)/shard_map/ppermute | solution.py:361
  10.6 5.7 %collective-permute-done.refs_2_ = bf16[128,2048]{1,0:T(8,128)(2,1)S(1)} collective-permute-done((bf16[128,2048]{1,0:T(8,128)(2,1)}, bf16[128,2048]{1,0:T(8,128)(2,1)S(1)}, u32[]{:S(2)}, u32[]{:S(2)}) %collective-permute-start) | collective-permute-done | bytes 524320 | tf_op jit(solution)/shard_map/ppermute | solution.py:361
  16.7 2.3 collective-permute-start.4
  19.0 2.3 collective-permute-start.3
  21.3 2.2 copy-done.2
  24.5 2.7 %shard_map.140 = (bf16[512,1024]{1,0:T(8,128)(2,1)S(1)}, bf16[512,2048]{1,0:T(8,128)(2,1)S(1)}) custom-call(bf16[2048,1024]{1,0:T(8,128)(2,1)S(1)} %copy-done.2, bf16[128,2048]{1,0:T(8,128)(2,1)S(1)} %copy-done.7, bf16[128,2048]{1,0:T(8,128)(2,1)S(1)} %collective-permute-done.1.refs_1_, bf16[128,2048]{1,0:T(8,128)(2,1)S(1)} %collective-permute-done.refs_2_, ...), custom_call_target="tpu_custom_call" | custom-call | tf_op jit(solution)/shard_map/pallas_call | solution.py:469
  28.5 2.8 %collective-permute-done.4 = bf16[128,2048]{1,0:T(8,128)(2,1)} collective-permute-done((bf16[128,2048]{1,0:T(8,128)(2,1)S(1)}, bf16[128,2048]{1,0:T(8,128)(2,1)}, u32[]{:S(2)}, u32[]{:S(2)}) %collective-permute-start.4) | collective-permute-done | bytes 524320 | tf_op jit(solution)/shard_map/ppermute | solution.py:361
  31.3 12.6 %collective-permute-done.3.refs_0_ = bf16[128,2048]{1,0:T(8,128)(2,1)S(1)} collective-permute-done((bf16[128,2048]{1,0:T(8,128)(2,1)}, bf16[128,2048]{1,0:T(8,128)(2,1)S(1)}, u32[]{:S(2)}, u32[]{:S(2)}) %collective-permute-start.3) | collective-permute-done | bytes 524320 | tf_op jit(solution)/shard_map/ppermute | solution.py:361
  47.8 2.2 copy-done.3
  50.0 4.9 %shard_map.141 = (bf16[256,1024]{1,0:T(8,128)(2,1)S(1)}, bf16[256,1024]{1,0:T(8,128)(2,1)S(1)}, bf16[256,1024]{1,0:T(8,128)(2,1)S(1)}, bf16[256,1024]{1,0:T(8,128)(2,1)S(1)}, bf16[512,2048]{1,0:T(8,128)(2,1)S(1)}) custom-call(s32[1]{0:T(128)} %bitcast.8.rank_ref, s32[1,1024]{1,0:T(1,128)S(1)} %bitcast.19, bf16[2048,1024]{1,0:T(8,128)(2,1)S(1)} %copy-done.3, ...), custom_call_target="tpu_custom_call" | custom-call | tf_op jit(solution)/shard_map/pallas_call | solution.py:490
  62.3 8.7 %collective-permute-done.8 = bf16[256,1024]{1,0:T(8,128)(2,1)S(1)} collective-permute-done((bf16[256,1024]{1,0:T(8,128)(2,1)S(1)}, bf16[256,1024]{1,0:T(8,128)(2,1)S(1)}, u32[]{:S(2)}, u32[]{:S(2)}) %collective-permute-start.8) | collective-permute-done | bytes 524320 | tf_op jit(solution)/shard_map/ppermute | solution.py:19
  71.1 12.1 %collective-permute-done.11.refs_4_ = bf16[256,1024]{1,0:T(8,128)(2,1)S(1)} collective-permute-done((bf16[256,1024]{1,0:T(8,128)(2,1)S(1)}, bf16[256,1024]{1,0:T(8,128)(2,1)S(1)}, u32[]{:S(2)}, u32[]{:S(2)}) %collective-permute-start.11) | collective-permute-done | bytes 524320 | tf_op jit(solution)/shard_map/ppermute | solution.py:361
  84.1 2.2 collective-permute-start.14
  88.6 8.0 %shard_map.142.refs_0_ = bf16[2048,1024]{1,0:T(8,128)(2,1)} custom-call(s32[1024,1]{1,0:T(8,128)} %copy.26.token_ref, s32[1,1024]{1,0:T(1,128)} %bitcast.23, bf16[512,2048]{1,0:T(8,128)(2,1)} %copy-done.5, bf16[512,2048]{1,0:T(8,128)(2,1)} %copy-done.6), custom_call_target="tpu_custom_call" | custom-call | tf_op jit(solution)/shard_map/pallas_call | solution.py:691
  96.5 9.1 %collective-permute-done.14.refs_2_ = bf16[256,1024]{1,0:T(8,128)(2,1)S(1)} collective-permute-done((bf16[256,1024]{1,0:T(8,128)(2,1)S(1)}, bf16[256,1024]{1,0:T(8,128)(2,1)S(1)}, u32[]{:S(2)}, u32[]{:S(2)}) %collective-permute-start.14) | collective-permute-done | bytes 524320 | tf_op jit(solution)/shard_map/ppermute | solution.py:361
  109.7 7.5 %shard_map.144 = (f32[256,1024]{1,0:T(8,128)}, f32[256,256]{1,0:T(8,128)}, f32[256,1]{1,0:T(8,128)}) custom-call(s32[8]{0:T(128)} %reshape.115.from_ref, f32[1,8192]{1,0:T(1,128)} %bitcast.21, bf16[8192,1024]{1,0:T(8,128)(2,1)} %q_weight_ref.3, bf16[8192,256]{1,0:T(8,128)(2,1)} %kv_weight_ref.3, bf16[256,1024]{1,0:T(8,128)(2,1)} %copy-done.8, ...), custom_call_target="tpu_custom_call" | custom-call | tf_op jit(solution)/shard_map/pallas_call | solution.py:656
  118.1 11.9 %shard_map.143.grad_ref = bf16[256,1024]{1,0:T(8,128)(2,1)} custom-call(s32[4]{0:T(128)} %get-tuple-element.113.chips_ref, s32[1]{0:T(128)} %bitcast.10.core_ref, bf16[1024,8192]{1,0:T(8,128)(2,1)} %weight_ref.7, bf16[256,1024]{1,0:T(8,128)(2,1)} %refs_0_.1, bf16[256,1024]{1,0:T(8,128)(2,1)} %copy-done.21, bf16[256,1024]{1,0:T(8,128)(2,1)} %collective-permute-done.9.refs_2_, ...), custom_call_target="tpu_custom_call" | custom-call | tf_op jit(solution)/shard_map/pallas_call | solution.py:536
  130.1 1.9 collective-permute-done.16
  135.7 21.6 %shard_map.145 = (bf16[256,1024]{1,0:T(8,128)(2,1)}, bf16[256,1024]{1,0:T(8,128)(2,1)}, bf16[256,1024]{1,0:T(8,128)(2,1)}, bf16[256,1024]{1,0:T(8,128)(2,1)}, bf...) custom-call(s32[8]{0:T(128)} %reshape.115.from_ref, ...), custom_call_target="tpu_custom_call" | custom-call | tf_op jit(solution)/shard_map/pallas_call | solution.py:771
  157.5 2.0 collective-permute-done.27
  160.9 3.2 %collective-permute-start.28 = (bf16[256,1024]{1,0:T(8,128)(2,1)S(1)}, bf16[256,1024]{1,0:T(8,128)(2,1)S(1)}, u32[]{:S(2)}, u32[]{:S(2)}) collective-permute-start(bf16[256,1024]{1,0:T(8,128)(2,1)S(1)} %add_convert_fusion.7), channel_id=1, source_target_pairs={{0,2},{1,3},{2,0},{3,1},{4,6},{5,7},{6,4},{7,5},{8,10},{9,11},{10,... | collective-permute-start | bytes 1572872 | tf_op jit(solution)/shard_map/ppermute | solution.py:361
  164.6 11.6 %shard_map.146 = (bf16[256,1024]{1,0:T(8,128)(2,1)}, bf16[256,1024]{1,0:T(8,128)(2,1)}, bf16[256,1024]{1,0:T(8,128)(2,1)}, bf16[256,1024]{1,0:T(8,128)(2,1)}, bf...) custom-call(s32[4]{0:T(128)} %get-tuple-element.129.chips_ref, ...), custom_call_target="tpu_custom_call" | custom-call | tf_op jit(solution)/shard_map/pallas_call | solution.py:574
  183.6 8.3 %collective-permute-done.36 = bf16[256,1024]{1,0:T(8,128)(2,1)S(1)} collective-permute-done((bf16[256,1024]{1,0:T(8,128)(2,1)S(1)}, bf16[256,1024]{1,0:T(8,128)(2,1)S(1)}, u32[]{:S(2)}, u32[]{:S(2)}) %collective-permute-start.36) | collective-permute-done | bytes 524320 | tf_op jit(solution)/shard_map/ppermute | solution.py:361
  192.0 2.1 collective-permute-start.33
  194.1 10.0 %collective-permute-done.38 = bf16[256,1024]{1,0:T(8,128)(2,1)S(1)} collective-permute-done((bf16[256,1024]{1,0:T(8,128)(2,1)S(1)}, bf16[256,1024]{1,0:T(8,128)(2,1)S(1)}, u32[]{:S(2)}, u32[]{:S(2)}) %collective-permute-start.38) | collective-permute-done | bytes 524320 | tf_op jit(solution)/shard_map/ppermute | solution.py:361
  204.7 2.5 %collective-permute-start.41 = (bf16[256,1024]{1,0:T(8,128)(2,1)S(1)}, bf16[256,1024]{1,0:T(8,128)(2,1)S(1)}, u32[]{:S(2)}, u32[]{:S(2)}) collective-permute-start(bf16[256,1024]{1,0:T(8,128)(2,1)S(1)} %add_convert_fusion.2.refs_1_), channel_id=1, source_target_pairs={{0,24},{8,16},{16,8},{24,0},{1,25},{9,17},{17,9},{25,1},{2,26},{10... | collective-permute-start | bytes 1572872 | tf_op jit(solution)/shard_map/ppermute | solution.py:19
  207.8 6.6 %collective-permute-done.44 = bf16[256,1024]{1,0:T(8,128)(2,1)S(1)} collective-permute-done((bf16[256,1024]{1,0:T(8,128)(2,1)S(1)}, bf16[256,1024]{1,0:T(8,128)(2,1)S(1)}, u32[]{:S(2)}, u32[]{:S(2)}) %collective-permute-start.44) | collective-permute-done | bytes 524320 | tf_op jit(solution)/shard_map/ppermute | solution.py:361
  216.2 8.4 %collective-permute-done.33 = bf16[256,1024]{1,0:T(8,128)(2,1)S(1)} collective-permute-done((bf16[256,1024]{1,0:T(8,128)(2,1)S(1)}, bf16[256,1024]{1,0:T(8,128)(2,1)S(1)}, u32[]{:S(2)}, u32[]{:S(2)}) %collective-permute-start.33) | collective-permute-done | bytes 524320 | tf_op jit(solution)/shard_map/ppermute | solution.py:361
  224.7 2.4 collective-permute-start.45
  227.1 3.7 %collective-permute-done.40.refs_3_ = bf16[256,1024]{1,0:T(8,128)(2,1)S(1)} collective-permute-done((bf16[256,1024]{1,0:T(8,128)(2,1)S(1)}, bf16[256,1024]{1,0:T(8,128)(2,1)S(1)}, u32[]{:S(2)}, u32[]{:S(2)}) %collective-permute-start.40) | collective-permute-done | bytes 524320 | tf_op jit(solution)/shard_map/ppermute | solution.py:19
  230.8 6.4 %shard_map.147 = f32[2048,1024]{1,0:T(8,128)} custom-call(bf16[2048,1024]{1,0:T(8,128)(2,1)S(1)} %copy-done.4, bf16[256,1024]{1,0:T(8,128)(2,1)S(1)} %add_convert_fusion.2.refs_1_, bf16[256,1024]{1,0:T(8,128)(2,1)S(1)} %collective-permute-done.39.refs_2_, bf16[256,1024]{1,0:T(8,128)(2,1)S(1)} %collective-permute-done.40.refs_3_, ...), custom_call_target="tpu_custom_call" | custom-call | tf_op jit(solution)/shard_map/pallas_call | solution.py:336
  237.2 2.0 collective-permute-done.45
  (167 shorter events, 45.8 us)
Async XLA Ops:
  0.6 15.6 %collective-permute-start = (bf16[128,2048]{1,0:T(8,128)(2,1)}, bf16[128,2048]{1,0:T(8,128)(2,1)S(1)}, u32[]{:S(2)}, u32[]{:S(2)}) collective-permute-start(bf16[128,2048]{1,0:T(8,128)(2,1)} %refs_0_), channel_id=1, source_target_pairs={{2,0},{3,1},{6,2},{7,3},{0,4},{1,5},{4,6},{5,7},{10,8},{11,9},{14,... | collective-permute-start | bytes 1572872 | tf_op jit(solution)/shard_map/ppermute | solution.py:361
  16.7 14.6 %collective-permute-start.4 = (bf16[128,2048]{1,0:T(8,128)(2,1)S(1)}, bf16[128,2048]{1,0:T(8,128)(2,1)}, u32[]{:S(2)}, u32[]{:S(2)}) collective-permute-start(bf16[128,2048]{1,0:T(8,128)(2,1)S(1)} %collective-permute-done.refs_2_), channel_id=1, source_target_pairs={{0,2},{1,3},{2,0},{3,1},{4,6},{5,7},{6,4},{7,5},{8,10},{9,11},{10,... | collective-permute-start | bytes 1572872 | tf_op jit(solution)/shard_map/ppermute | solution.py:361
  19.0 24.9 %collective-permute-start.3 = (bf16[128,2048]{1,0:T(8,128)(2,1)}, bf16[128,2048]{1,0:T(8,128)(2,1)S(1)}, u32[]{:S(2)}, u32[]{:S(2)}) collective-permute-start(bf16[128,2048]{1,0:T(8,128)(2,1)} %refs_0_), channel_id=1, source_target_pairs={{4,0},{5,1},{0,2},{1,3},{6,4},{7,5},{2,6},{3,7},{12,8},{13,9},{8,1... | collective-permute-start | bytes 1572872 | tf_op jit(solution)/shard_map/ppermute | solution.py:361
  45.6 15.3 %collective-permute-start.9 = (bf16[256,1024]{1,0:T(8,128)(2,1)}, bf16[256,1024]{1,0:T(8,128)(2,1)}, u32[]{:S(2)}, u32[]{:S(2)}) collective-permute-start(bf16[256,1024]{1,0:T(8,128)(2,1)} %refs_0_.1), channel_id=1, source_target_pairs={{2,0},{3,1},{6,2},{7,3},{0,4},{1,5},{4,6},{5,7},{10,8},{11,9},{14,... | collective-permute-start | bytes 1572872 | tf_op jit(solution)/shard_map/ppermute | solution.py:361
  56.2 14.8 %collective-permute-start.8 = (bf16[256,1024]{1,0:T(8,128)(2,1)S(1)}, bf16[256,1024]{1,0:T(8,128)(2,1)S(1)}, u32[]{:S(2)}, u32[]{:S(2)}) collective-permute-start(bf16[256,1024]{1,0:T(8,128)(2,1)S(1)} %get-tuple-element.93), channel_id=1, source_target_pairs={{0,8},{8,0},{16,24},{24,16},{1,9},{9,1},{17,25},{25,17},{2,10},{10... | collective-permute-start | bytes 1572872 | tf_op jit(solution)/shard_map/ppermute | solution.py:19
  57.7 13.4 %collective-permute-start.12 = (bf16[256,1024]{1,0:T(8,128)(2,1)S(1)}, bf16[256,1024]{1,0:T(8,128)(2,1)S(1)}, u32[]{:S(2)}, u32[]{:S(2)}) collective-permute-start(bf16[256,1024]{1,0:T(8,128)(2,1)S(1)} %copy-done.15), channel_id=1, source_target_pairs={{0,1},{1,0},{2,4},{3,5},{4,2},{5,3},{6,7},{7,6},{8,9},{9,8},{10,12... | collective-permute-start | bytes 1572872 | tf_op jit(solution)/shard_map/ppermute | solution.py:386
  57.7 25.5 %collective-permute-start.11 = (bf16[256,1024]{1,0:T(8,128)(2,1)S(1)}, bf16[256,1024]{1,0:T(8,128)(2,1)S(1)}, u32[]{:S(2)}, u32[]{:S(2)}) collective-permute-start(bf16[256,1024]{1,0:T(8,128)(2,1)S(1)} %copy-done.15), channel_id=1, source_target_pairs={{4,0},{5,1},{0,2},{1,3},{6,4},{7,5},{2,6},{3,7},{12,8},{13,9},{8,1... | collective-permute-start | bytes 1572872 | tf_op jit(solution)/shard_map/ppermute | solution.py:361
  59.4 24.4 %collective-permute-start.10 = (bf16[256,1024]{1,0:T(8,128)(2,1)S(1)}, bf16[256,1024]{1,0:T(8,128)(2,1)S(1)}, u32[]{:S(2)}, u32[]{:S(2)}) collective-permute-start(bf16[256,1024]{1,0:T(8,128)(2,1)S(1)} %get-tuple-element.96), channel_id=1, source_target_pairs={{0,16},{8,24},{16,0},{24,8},{1,17},{9,25},{17,1},{25,9},{2,18},{10... | collective-permute-start | bytes 1572872 | tf_op jit(solution)/shard_map/ppermute | solution.py:19
  60.9 22.8 %collective-permute-start.13 = (bf16[256,1024]{1,0:T(8,128)(2,1)S(1)}, bf16[256,1024]{1,0:T(8,128)(2,1)S(1)}, u32[]{:S(2)}, u32[]{:S(2)}) collective-permute-start(bf16[256,1024]{1,0:T(8,128)(2,1)S(1)} %get-tuple-element.98), channel_id=1, source_target_pairs={{0,24},{8,16},{16,8},{24,0},{1,25},{9,17},{17,9},{25,1},{2,26},{10... | collective-permute-start | bytes 1572872 | tf_op jit(solution)/shard_map/ppermute | solution.py:19
  71.0 25.6 %collective-permute-start.15 = (bf16[256,1024]{1,0:T(8,128)(2,1)}, bf16[256,1024]{1,0:T(8,128)(2,1)S(1)}, u32[]{:S(2)}, u32[]{:S(2)}) collective-permute-start(bf16[256,1024]{1,0:T(8,128)(2,1)} %collective-permute-done.9.refs_2_), channel_id=1, source_target_pairs={{0,2},{1,3},{2,0},{3,1},{4,6},{5,7},{6,4},{7,5},{8,10},{9,11},{10,... | collective-permute-start | bytes 1572872 | tf_op jit(solution)/shard_map/ppermute | solution.py:361
  84.1 21.5 %collective-permute-start.14 = (bf16[256,1024]{1,0:T(8,128)(2,1)S(1)}, bf16[256,1024]{1,0:T(8,128)(2,1)S(1)}, u32[]{:S(2)}, u32[]{:S(2)}) collective-permute-start(bf16[256,1024]{1,0:T(8,128)(2,1)S(1)} %add_convert_fusion.8.refs_0_), channel_id=1, source_target_pairs={{2,0},{3,1},{6,2},{7,3},{0,4},{1,5},{4,6},{5,7},{10,8},{11,9},{14,... | collective-permute-start | bytes 1572872 | tf_op jit(solution)/shard_map/ppermute | solution.py:361
  88.1 18.2 %collective-permute-start.19 = (bf16[256,1024]{1,0:T(8,128)(2,1)}, bf16[256,1024]{1,0:T(8,128)(2,1)S(1)}, u32[]{:S(2)}, u32[]{:S(2)}) collective-permute-start(bf16[256,1024]{1,0:T(8,128)(2,1)} %refs_0_.1), channel_id=1, source_target_pairs={{0,1},{1,0},{2,3},{3,2},{4,5},{5,4},{6,7},{7,6},{8,9},{9,8},{10,11... | collective-permute-start | bytes 1572872 | tf_op jit(solution)/shard_map/ppermute | solution.py:19
  88.1 18.8 %collective-permute-start.20 = (bf16[256,1024]{1,0:T(8,128)(2,1)}, bf16[256,1024]{1,0:T(8,128)(2,1)S(1)}, u32[]{:S(2)}, u32[]{:S(2)}) collective-permute-start(bf16[256,1024]{1,0:T(8,128)(2,1)} %collective-permute-done.9.refs_2_), channel_id=1, source_target_pairs={{0,1},{1,0},{2,3},{3,2},{4,5},{5,4},{6,7},{7,6},{8,9},{9,8},{10,11... | collective-permute-start | bytes 1572872 | tf_op jit(solution)/shard_map/ppermute | solution.py:19
  106.8 25.2 %collective-permute-start.16 = (bf16[256,1024]{1,0:T(8,128)(2,1)S(1)}, bf16[256,1024]{1,0:T(8,128)(2,1)S(1)}, u32[]{:S(2)}, u32[]{:S(2)}) collective-permute-start(bf16[256,1024]{1,0:T(8,128)(2,1)S(1)} %collective-permute-done.14.refs_2_), channel_id=1, source_target_pairs={{0,2},{1,3},{2,0},{3,1},{4,6},{5,7},{6,4},{7,5},{8,10},{9,11},{10,... | collective-permute-start | bytes 1572872 | tf_op jit(solution)/shard_map/ppermute | solution.py:361
  107.5 24.5 %collective-permute-start.18 = (bf16[256,1024]{1,0:T(8,128)(2,1)S(1)}, bf16[256,1024]{1,0:T(8,128)(2,1)S(1)}, u32[]{:S(2)}, u32[]{:S(2)}) collective-permute-start(bf16[256,1024]{1,0:T(8,128)(2,1)S(1)} %add_convert_fusion.8.refs_0_), channel_id=1, source_target_pairs={{4,0},{5,1},{0,2},{1,3},{6,4},{7,5},{2,6},{3,7},{12,8},{13,9},{8,1... | collective-permute-start | bytes 1572872 | tf_op jit(solution)/shard_map/ppermute | solution.py:361
  108.9 23.1 %collective-permute-start.17 = (bf16[256,1024]{1,0:T(8,128)(2,1)S(1)}, bf16[256,1024]{1,0:T(8,128)(2,1)S(1)}, u32[]{:S(2)}, u32[]{:S(2)}) collective-permute-start(bf16[256,1024]{1,0:T(8,128)(2,1)S(1)} %add_convert_fusion.8.refs_0_), channel_id=1, source_target_pairs={{0,1},{1,0},{2,4},{3,5},{4,2},{5,3},{6,7},{7,6},{8,9},{9,8},{10,12... | collective-permute-start | bytes 1572872 | tf_op jit(solution)/shard_map/ppermute | solution.py:386
  160.7 15.6 %collective-permute-start.29 = (bf16[256,1024]{1,0:T(8,128)(2,1)S(1)}, bf16[256,1024]{1,0:T(8,128)(2,1)S(1)}, u32[]{:S(2)}, u32[]{:S(2)}) collective-permute-start(bf16[256,1024]{1,0:T(8,128)(2,1)S(1)} %add_convert_fusion.7), channel_id=1, source_target_pairs={{0,1},{1,0},{2,4},{3,5},{4,2},{5,3},{6,7},{7,6},{8,9},{9,8},{10,12... | collective-permute-start | bytes 1572872 | tf_op jit(solution)/shard_map/ppermute | solution.py:406
  160.9 15.4 %collective-permute-start.28 = (bf16[256,1024]{1,0:T(8,128)(2,1)S(1)}, bf16[256,1024]{1,0:T(8,128)(2,1)S(1)}, u32[]{:S(2)}, u32[]{:S(2)}) collective-permute-start(bf16[256,1024]{1,0:T(8,128)(2,1)S(1)} %add_convert_fusion.7), channel_id=1, source_target_pairs={{0,2},{1,3},{2,0},{3,1},{4,6},{5,7},{6,4},{7,5},{8,10},{9,11},{10,... | collective-permute-start | bytes 1572872 | tf_op jit(solution)/shard_map/ppermute | solution.py:361
  164.1 12.7 %collective-permute-start.35 = (bf16[256,1024]{1,0:T(8,128)(2,1)}, bf16[256,1024]{1,0:T(8,128)(2,1)S(1)}, u32[]{:S(2)}, u32[]{:S(2)}) collective-permute-start(bf16[256,1024]{1,0:T(8,128)(2,1)} %get-tuple-element.148), channel_id=1, source_target_pairs={{0,1},{1,0},{2,3},{3,2},{4,5},{5,4},{6,7},{7,6},{8,9},{9,8},{10,11... | collective-permute-start | bytes 1572872 | tf_op jit(solution)/shard_map/ppermute | solution.py:19
  164.1 14.5 %collective-permute-start.37 = (bf16[256,1024]{1,0:T(8,128)(2,1)}, bf16[256,1024]{1,0:T(8,128)(2,1)S(1)}, u32[]{:S(2)}, u32[]{:S(2)}) collective-permute-start(bf16[256,1024]{1,0:T(8,128)(2,1)} %get-tuple-element.150), channel_id=1, source_target_pairs={{0,1},{1,0},{2,3},{3,2},{4,5},{5,4},{6,7},{7,6},{8,9},{9,8},{10,11... | collective-permute-start | bytes 1572872 | tf_op jit(solution)/shard_map/ppermute | solution.py:19
  164.6 18.7 %collective-permute-start.34 = (bf16[256,1024]{1,0:T(8,128)(2,1)}, bf16[256,1024]{1,0:T(8,128)(2,1)S(1)}, u32[]{:S(2)}, u32[]{:S(2)}) collective-permute-start(bf16[256,1024]{1,0:T(8,128)(2,1)} %get-tuple-element.145), channel_id=1, source_target_pairs={{0,1},{1,0},{2,3},{3,2},{4,5},{5,4},{6,7},{7,6},{8,9},{9,8},{10,11... | collective-permute-start | bytes 1572872 | tf_op jit(solution)/shard_map/ppermute | solution.py:19
  177.0 14.9 %collective-permute-start.36 = (bf16[256,1024]{1,0:T(8,128)(2,1)S(1)}, bf16[256,1024]{1,0:T(8,128)(2,1)S(1)}, u32[]{:S(2)}, u32[]{:S(2)}) collective-permute-start(bf16[256,1024]{1,0:T(8,128)(2,1)S(1)} %add_convert_fusion.4), channel_id=1, source_target_pairs={{0,4},{1,5},{2,0},{3,1},{4,6},{5,7},{6,2},{7,3},{8,12},{9,13},{10,... | collective-permute-start | bytes 1572872 | tf_op jit(solution)/shard_map/ppermute | solution.py:361
  179.0 25.1 %collective-permute-start.38 = (bf16[256,1024]{1,0:T(8,128)(2,1)S(1)}, bf16[256,1024]{1,0:T(8,128)(2,1)S(1)}, u32[]{:S(2)}, u32[]{:S(2)}) collective-permute-start(bf16[256,1024]{1,0:T(8,128)(2,1)S(1)} %add_convert_fusion.3), channel_id=1, source_target_pairs={{0,2},{1,3},{2,6},{3,7},{4,0},{5,1},{6,4},{7,5},{8,10},{9,11},{10,... | collective-permute-start | bytes 1572872 | tf_op jit(solution)/shard_map/ppermute | solution.py:361
  179.7 27.5 %collective-permute-start.43 = (bf16[256,1024]{1,0:T(8,128)(2,1)}, bf16[256,1024]{1,0:T(8,128)(2,1)S(1)}, u32[]{:S(2)}, u32[]{:S(2)}) collective-permute-start(bf16[256,1024]{1,0:T(8,128)(2,1)} %get-tuple-element.158), channel_id=1, source_target_pairs={{0,1},{1,0},{2,3},{3,2},{4,5},{5,4},{6,7},{7,6},{8,9},{9,8},{10,11... | collective-permute-start | bytes 1572872 | tf_op jit(solution)/shard_map/ppermute | solution.py:19
  181.6 32.7 %collective-permute-start.44 = (bf16[256,1024]{1,0:T(8,128)(2,1)S(1)}, bf16[256,1024]{1,0:T(8,128)(2,1)S(1)}, u32[]{:S(2)}, u32[]{:S(2)}) collective-permute-start(bf16[256,1024]{1,0:T(8,128)(2,1)S(1)} %add_convert_fusion.6), channel_id=1, source_target_pairs={{0,2},{1,3},{2,0},{3,1},{4,6},{5,7},{6,4},{7,5},{8,10},{9,11},{10,... | collective-permute-start | bytes 1572872 | tf_op jit(solution)/shard_map/ppermute | solution.py:361
  183.4 32.8 %collective-permute-start.31 = (bf16[256,1024]{1,0:T(8,128)(2,1)S(1)}, bf16[256,1024]{1,0:T(8,128)(2,1)S(1)}, u32[]{:S(2)}, u32[]{:S(2)}) collective-permute-start(bf16[256,1024]{1,0:T(8,128)(2,1)S(1)} %add_convert_fusion.6), channel_id=1, source_target_pairs={{0,1},{1,0},{2,4},{3,5},{4,2},{5,3},{6,7},{7,6},{8,9},{9,8},{10,12... | collective-permute-start | bytes 1572872 | tf_op jit(solution)/shard_map/ppermute | solution.py:406
  192.0 32.7 %collective-permute-start.33 = (bf16[256,1024]{1,0:T(8,128)(2,1)S(1)}, bf16[256,1024]{1,0:T(8,128)(2,1)S(1)}, u32[]{:S(2)}, u32[]{:S(2)}) collective-permute-start(bf16[256,1024]{1,0:T(8,128)(2,1)S(1)} %add_convert_fusion.5), channel_id=1, source_target_pairs={{0,4},{1,5},{2,0},{3,1},{4,6},{5,7},{6,2},{7,3},{8,12},{9,13},{10,... | collective-permute-start | bytes 1572872 | tf_op jit(solution)/shard_map/ppermute | solution.py:361
  204.7 22.3 %collective-permute-start.41 = (bf16[256,1024]{1,0:T(8,128)(2,1)S(1)}, bf16[256,1024]{1,0:T(8,128)(2,1)S(1)}, u32[]{:S(2)}, u32[]{:S(2)}) collective-permute-start(bf16[256,1024]{1,0:T(8,128)(2,1)S(1)} %add_convert_fusion.2.refs_1_), channel_id=1, source_target_pairs={{0,24},{8,16},{16,8},{24,0},{1,25},{9,17},{17,9},{25,1},{2,26},{10... | collective-permute-start | bytes 1572872 | tf_op jit(solution)/shard_map/ppermute | solution.py:19
  207.2 23.5 %collective-permute-start.40 = (bf16[256,1024]{1,0:T(8,128)(2,1)S(1)}, bf16[256,1024]{1,0:T(8,128)(2,1)S(1)}, u32[]{:S(2)}, u32[]{:S(2)}) collective-permute-start(bf16[256,1024]{1,0:T(8,128)(2,1)S(1)} %add_convert_fusion.2.refs_1_), channel_id=1, source_target_pairs={{0,16},{8,24},{16,0},{24,8},{1,17},{9,25},{17,1},{25,9},{2,18},{10... | collective-permute-start | bytes 1572872 | tf_op jit(solution)/shard_map/ppermute | solution.py:19
  214.3 16.5 %collective-permute-start.39 = (bf16[256,1024]{1,0:T(8,128)(2,1)S(1)}, bf16[256,1024]{1,0:T(8,128)(2,1)S(1)}, u32[]{:S(2)}, u32[]{:S(2)}) collective-permute-start(bf16[256,1024]{1,0:T(8,128)(2,1)S(1)} %add_convert_fusion.2.refs_1_), channel_id=1, source_target_pairs={{0,8},{8,0},{16,24},{24,16},{1,9},{9,1},{17,25},{25,17},{2,10},{10... | collective-permute-start | bytes 1572872 | tf_op jit(solution)/shard_map/ppermute | solution.py:19
  216.2 21.1 %collective-permute-start.42 = (bf16[256,1024]{1,0:T(8,128)(2,1)S(1)}, bf16[256,1024]{1,0:T(8,128)(2,1)S(1)}, u32[]{:S(2)}, u32[]{:S(2)}) collective-permute-start(bf16[256,1024]{1,0:T(8,128)(2,1)S(1)} %copy-done.32), channel_id=1, source_target_pairs={{0,1},{1,0},{2,3},{3,2},{4,5},{5,4},{6,7},{7,6},{8,9},{9,8},{10,11... | collective-permute-start | bytes 1572872 | tf_op jit(solution)/shard_map/ppermute | solution.py:19
  224.7 14.6 %collective-permute-start.45 = (bf16[256,1024]{1,0:T(8,128)(2,1)S(1)}, bf16[256,1024]{1,0:T(8,128)(2,1)S(1)}, u32[]{:S(2)}, u32[]{:S(2)}) collective-permute-start(bf16[256,1024]{1,0:T(8,128)(2,1)S(1)} %add_convert_fusion.1), channel_id=1, source_target_pairs={{0,2},{1,3},{2,6},{3,7},{4,0},{5,1},{6,4},{7,5},{8,10},{9,11},{10,... | collective-permute-start | bytes 1572872 | tf_op jit(solution)/shard_map/ppermute | solution.py:361
  (47 other events, 471.7 us)
